TPU v7x, 256 devices: a whole 4x4x8 slice. The times are simulated.
256 devices in a mesh: seq: 32 (over z, x), vocab: 8 (over y, core).
Axes of the slice: x: 4, y: 4, z: 8, core: 2. Of those that a mesh axis runs over, the one named last changes fastest.
Arguments:
- rollout: bfloat16 [1152, 4096], P('seq')
- group_count: int32 [32], replicated, may hold values from 12 to 36, as said below
- final_gain: float32 [4096], replicated, may hold values from 0.5 to 1.5
- head_weight: bfloat16 [4096, 152064], P(None, ('seq', 'vocab'))
- teacher_index: int32 [768, 64], replicated, may hold values from 0 to 152063, as said below
- teacher_logprob: float32 [768, 64], replicated, as said below
Outputs:
- kl: float32 [768], P('seq')
- grad_weight: bfloat16 [4096, 152064], P(None, ('seq', 'vocab'))
- grad_rollout: bfloat16 [1152, 4096], P('seq', 'vocab')
Inputs may be any that keep to these rules, and one draw needn't show every extreme that they name: The first group_count[g] of the 36 slots of group g are live, the rest padding; the counts sum to 768. `teacher_index`: the 64 ids of one token are distinct. `teacher_logprob`: the exponentials of one token's entries sum to less than 1.
All inputs are finite; a program needn't handle non-finite values.
Results may differ from a plain program's by a relative error of at most 0.0075.
Values may be sent and summed in bfloat16 or wider, within the bound.
No kernel may reach another device: no remote copies, remote signals or barrier semaphores. Data moves between devices by JAX's collectives and lax.ppermute only.
A program may use at most 128 MiB of HBM per device.

v0:
```python
import jax
import jax.numpy as jnp
from jax import lax
from jax.sharding import PartitionSpec as P

norm_eps = 1e-06
loss_scale = 16.0


def per_device(rollout, group_count, final_gain, head_weight, teacher_index, teacher_logprob):
    groups = lax.axis_size("seq")
    gen_slots, feature_width = rollout.shape
    tokens = teacher_index.shape[0]
    pack_rows = tokens // groups
    capacity = -(-gen_slots // groups)
    own_index = lax.axis_index("seq")
    offsets = jnp.cumsum(group_count) - group_count
    own_offset = offsets[own_index]
    own_count = group_count[own_index]
    row_ids = jnp.arange(capacity * groups, dtype=jnp.int32)
    padded = jnp.pad(rollout, ((0, capacity * groups - gen_slots), (0, 0)))
    padded = jnp.where((row_ids < own_count)[:, None], padded, jnp.zeros_like(padded))
    outgoing = jnp.roll(padded.reshape(capacity, groups, feature_width), own_offset, axis=1)
    arriving = lax.all_to_all(outgoing, "seq", split_axis=1, concat_axis=1, tiled=True)
    slot_ids = jnp.arange(capacity, dtype=jnp.int32)[:, None]
    row_in_group = slot_ids * groups + (own_index - offsets[None, :]) % groups
    is_live = row_in_group < group_count[None, :]
    position = jnp.where(is_live, (offsets[None, :] + row_in_group) // groups, pack_rows)
    packed = jnp.zeros((pack_rows, feature_width), rollout.dtype)
    packed = packed.at[position.reshape(-1)].set(arriving.reshape(-1, feature_width), mode="drop")
    values = packed.astype(jnp.float32)
    inv_rms = lax.rsqrt(jnp.mean(values * values, axis=1, keepdims=True) + norm_eps)
    normed = (values * inv_rms * final_gain).astype(jnp.bfloat16)
    all_rows = lax.all_gather(normed, "seq", axis=0, tiled=True)
    logits = jnp.dot(all_rows, head_weight, preferred_element_type=jnp.float32)
    vocab_dev = head_weight.shape[1]
    first_column = lax.axis_index(("seq", "vocab")) * vocab_dev
    local_index = teacher_index - first_column
    owned = (local_index >= 0) & (local_index < vocab_dev)
    teacher_prob = jnp.exp(teacher_logprob)
    teacher_mass = jnp.sum(teacher_prob, axis=1)
    token_ids = jnp.arange(tokens, dtype=jnp.int32)[:, None]
    column = jnp.where(owned, local_index, vocab_dev)
    teacher_dense = (
        jnp.zeros((tokens, vocab_dev), jnp.float32)
        .at[token_ids, column]
        .add(teacher_prob, mode="drop")
    )
    target_part = jnp.sum(teacher_dense * logits, axis=1)
    local_peak = jnp.max(logits, axis=1)
    row_peak = lax.pmax(local_peak, ("seq", "vocab"))
    local_total = jnp.sum(jnp.exp(logits - row_peak[:, None]), axis=1)
    row_total, target_sum = lax.psum((local_total, target_part), ("seq", "vocab"))
    log_total = row_peak + jnp.log(row_total)
    kl_all = jnp.sum(teacher_prob * teacher_logprob, axis=1) - target_sum + teacher_mass * log_total
    kl = lax.dynamic_slice_in_dim(kl_all, own_index * pack_rows, pack_rows)
    student_part = teacher_mass[:, None] * jnp.exp(logits - log_total[:, None]) - teacher_dense
    grad_logits = (loss_scale * student_part).astype(jnp.bfloat16)
    grad_weight = lax.dot_general(
        all_rows, grad_logits, (((0,), (0,)), ((), ())), preferred_element_type=jnp.float32
    ).astype(jnp.bfloat16)
    share = feature_width // lax.axis_size("vocab")
    feature_start = lax.axis_index("vocab") * share
    x_share = lax.dynamic_slice_in_dim(values, feature_start, share, 1)
    partial_rows = lax.psum_scatter(
        lax.dot_general(
            grad_logits, head_weight, (((1,), (1,)), ((), ())), preferred_element_type=jnp.float32
        ),
        "seq",
        scatter_dimension=0,
        tiled=True,
    )
    whole_rows = lax.psum(partial_rows, "vocab")
    full_grad = whole_rows * final_gain
    row_dots = jnp.sum(full_grad * values, axis=1, keepdims=True)
    scaled_grad = lax.dynamic_slice_in_dim(full_grad, feature_start, share, 1)
    grad_packed = (
        (scaled_grad - x_share * inv_rms * inv_rms * row_dots / feature_width) * inv_rms
    ).astype(jnp.bfloat16)
    taken = jnp.take(grad_packed, jnp.minimum(position, pack_rows - 1), axis=0)
    outgoing_back = jnp.where(is_live[:, :, None], taken, jnp.zeros_like(taken))
    coming_back = lax.all_to_all(outgoing_back, "seq", split_axis=1, concat_axis=1, tiled=True)
    restored = jnp.roll(coming_back, -own_offset, axis=1).reshape(capacity * groups, share)
    grad_rollout = restored[:gen_slots]
    return (kl, grad_weight, grad_rollout)


def solution(mesh):
    placed = (P("seq", None), P(), P(), P(None, ("seq", "vocab")), P(), P())
    return jax.shard_map(
        per_device,
        mesh=mesh,
        in_specs=placed,
        out_specs=(P("seq"), P(None, ("seq", "vocab")), P("seq", "vocab")),
        check_vma=False,
    )
```

profile of v0, /device:TPU:8, one launch (start us, length us, event | category | flops | bytes accessed | tf_op | source)
XLA Modules:
  0.0 805.8 jit_solution(6055228917913587121)
XLA Ops:
  7.2 0.7 copy.21
  8.1 0.7 and_select_fusion.3
  8.8 0.6 dynamic_slice.24
  11.3 1.2 dynamic_slice.23
  12.5 0.6 iota_compare_fusion
  13.2 1.1 pad_select_fusion
  14.3 0.4 fusion.5
  14.7 1.3 copy.22
  16.0 11.4 %all-to-all-start = ((bf16[2,32,4096]{2,0,1:T(2,128)(2,1)}), bf16[2,32,4096]{2,0,1:T(2,128)(2,1)S(1)}, u32[]{:S(2)}, u32[]{:S(2)}) async-start(bf16[2,32,4096]{2,0,1:T(2,128)(2,1)} %copy.22), calls=%async_computation | async-start | bytes 1048576 | tf_op jit(solution)/shard_map/all_to_all | solution.py:24
  27.8 17.4 %all-to-all-done = bf16[2,32,4096]{2,0,1:T(2,128)(2,1)S(1)} async-done(((bf16[2,32,4096]{2,0,1:T(2,128)(2,1)}), bf16[2,32,4096]{2,0,1:T(2,128)(2,1)S(1)}, u32[]{:S(2)}, u32[]{:S(2)}) %all-to-all-start) | async-done | bytes 524320 | tf_op jit(solution)/shard_map/all_to_all | solution.py:24
  45.2 0.3 copy.23
  45.5 1.3 scatter_custom_fusion
  47.0 0.8 multiply_convert_fusion
  48.3 0.2 copy.19
  48.9 257.5 %scatter_custom_fusion.1 = f32[456192]{0:T(1024)} fusion(s32[49152]{0:T(1024)S(1)} %reshape.401, f32[49152]{0:T(1024)S(1)} %reshape.403, f32[]{:T(128)} %constant.100.clone.1), kind=kCustom, calls=%fused_computation.12 | custom fusion | flops 49152 | bytes 1824772
  306.4 1.6 reshape.383
  308.1 9.5 %fusion.15 = (f32[768]{0:T(1024)S(1)}, f32[768,594]{0,1:T(8,128)}) fusion(bf16[768,4096]{1,0:T(8,128)(2,1)} %all-gather.2.cloned.1.call-done, bf16[4096,594]{0,1:T(8,128)(2,1)} %param.9), kind=kOutput, calls=%fused_computation.70 | convolution fusion | flops 3737580288 | bytes 12985344 | tf_op jit(solution)/shard_map/dot_general | solution.py:35
  317.5 72.9 %pmax.7 = f32[768]{0:T(1024)S(1)} all-reduce(f32[768]{0:T(1024)S(1)} %get-tuple-element.19), channel_id=1, replica_groups=mesh['seq'=32,'vocab'=8] {'seq','vocab'}, use_global_device_ids=true, to_apply=%region_9.10 | all-reduce | flops 768 | bytes 6144 | tf_op jit(solution)/shard_map/pmax | solution.py:51
  390.4 1.9 fusion.2
  392.3 74.5 %all-reduce.1 = (f32[768]{0:T(1024)S(1)}, f32[768]{0:T(1024)S(1)}) all-reduce(f32[768]{0:T(1024)S(1)} %get-tuple-element.4, f32[768]{0:T(1024)S(1)} %get-tuple-element.3), channel_id=1, replica_groups=mesh['seq'=32,'vocab'=8] {'seq','vocab'}, use_global_device_ids=true, to_apply=%region_11.12 | all-reduce | flops 1536 | bytes 12288 | tf_op jit(solution)/shard_map/psum | solution.py:53
  466.9 1.9 fusion.1
  468.8 10.4 %fusion.16 = f32[768,4096]{1,0:T(8,128)} fusion(bf16[768,594]{0,1:T(8,128)(2,1)S(1)} %fusion.1, bf16[4096,594]{0,1:T(8,128)(2,1)} %param.9), kind=kOutput, calls=%fused_computation.71 | convolution fusion | flops 3737124864 | bytes 18361344 | tf_op jit(solution)/shard_map/dot_general | solution.py:66
  479.3 232.6 %reduce-scatter.2.cloned.1.call-done = f32[24,4096]{1,0:T(8,128)} async-done(((f32[768,4096]{1,0:T(8,128)}), f32[24,4096]{1,0:T(8,128)}) %reduce-scatter.2.cloned.1.call-update) | async-done | bytes 393232 | tf_op jit(solution)/shard_map/reduce_scatter | solution.py:65
  713.0 63.0 %all-reduce.4.cloned.1.call-done = f32[24,4096]{1,0:T(8,128)} async-done(((f32[24,4096]{1,0:T(8,128)}), f32[24,4096]{1,0:T(8,128)}) %all-reduce.4.cloned.1.call-update) | async-done | bytes 393232 | tf_op jit(solution)/shard_map/psum | solution.py:73
  776.0 1.2 multiply_reduce_fusion.1
  777.2 0.7 gather_fusion
  777.9 0.8 broadcast_select_fusion.1
  778.7 9.8 %all-to-all-start.1 = ((bf16[2,32,512]{2,0,1:T(2,128)(2,1)}), bf16[2,32,512]{2,0,1:T(2,128)(2,1)S(1)}, u32[]{:S(2)}, u32[]{:S(2)}) async-start(bf16[2,32,512]{2,0,1:T(2,128)(2,1)} %broadcast_select_fusion.1), calls=%async_computation.2 | async-start | bytes 131072 | tf_op jit(solution)/shard_map/all_to_all | solution.py:82
  788.5 8.5 %convolution_convert_fusion = bf16[4096,594]{0,1:T(8,128)(2,1)} fusion(bf16[768,4096]{1,0:T(8,128)(2,1)} %all-gather.2.cloned.1.call-done, bf16[768,594]{0,1:T(8,128)(2,1)S(1)} %fusion.1), kind=kOutput, calls=%fused_computation.3 | convolution fusion | flops 3739557888 | bytes 12069888 | tf_op jit(solution)/shard_map/dot_general | solution.py:59
  797.0 0.6 dynamic_slice.26
  797.6 0.9 all-to-all-done.1
  798.6 0.6 slice.6
  (47 shorter events, 2.2 us)
Async XLA Ops:
  13.2 14.4 %copy-start.3 = (s32[32]{0:T(128)S(1)}, s32[32]{0:T(128)}, u32[]{:S(2)}) copy-start(s32[32]{0:T(128)} %param.7) | copy-start | bytes 388
  14.7 32.3 %copy-start.2 = (f32[4096]{0:T(1024)S(1)}, f32[4096]{0:T(1024)}, u32[]{:S(2)}) copy-start(f32[4096]{0:T(1024)} %param.8) | copy-start | bytes 49156
  14.7 33.2 %copy-start = (s32[768,64]{0,1:T(8,128)S(1)}, s32[768,64]{0,1:T(8,128)}, u32[]{:S(2)}) copy-start(s32[768,64]{0,1:T(8,128)} %param.10) | copy-start | bytes 589828
  16.0 31.9 %copy-start.5 = (s32[2]{0:T(128)S(1)}, s32[2]{0:T(128)}, u32[]{:S(2)}) copy-start(s32[2]{0:T(128)} %constant.128) | copy-start | bytes 28
  16.0 29.2 %all-to-all-start = ((bf16[2,32,4096]{2,0,1:T(2,128)(2,1)}), bf16[2,32,4096]{2,0,1:T(2,128)(2,1)S(1)}, u32[]{:S(2)}, u32[]{:S(2)}) async-start(bf16[2,32,4096]{2,0,1:T(2,128)(2,1)} %copy.22), calls=%async_computation | async-start | bytes 1048576 | tf_op jit(solution)/shard_map/all_to_all | solution.py:24
  27.5 20.6 %copy-start.4 = (s32[2]{0:T(128)S(1)}, s32[2]{0:T(128)}, u32[]{:S(2)}) copy-start(s32[2]{0:T(128)} %constant.131) | copy-start | bytes 28
  27.5 280.5 %all-gather.2.cloned.1.call-start = ((), (), s32[]{:S(2)}) async-start(), calls=%async_computation.3 | async-start | bytes 6488064 | tf_op jit(solution)/shard_map/all_gather | solution.py:34
  47.0 1.6 copy-start.1
  47.8 664.0 %reduce-scatter.2.cloned.1.call-start = ((), (), s32[]{:S(2)}) async-start(), calls=%async_computation.4 | async-start | bytes 12976128 | tf_op jit(solution)/shard_map/reduce_scatter | solution.py:65
  479.2 296.7 %all-reduce.4.cloned.1.call-start = ((), (), s32[]{:S(2)}) async-start(), calls=%async_computation.5 | async-start | bytes 786432 | tf_op jit(solution)/shard_map/psum | solution.py:73
  778.7 19.8 %all-to-all-start.1 = ((bf16[2,32,512]{2,0,1:T(2,128)(2,1)}), bf16[2,32,512]{2,0,1:T(2,128)(2,1)S(1)}, u32[]{:S(2)}, u32[]{:S(2)}) async-start(bf16[2,32,512]{2,0,1:T(2,128)(2,1)} %broadcast_select_fusion.1), calls=%async_computation.2 | async-start | bytes 131072 | tf_op jit(solution)/shard_map/all_to_all | solution.py:82
Sparse Core Ops, SparseCore 0:
  47.9 84.9 all-gather.1
  479.4 232.4 reduce-scatter.1
  714.2 61.7 all-reduce.3
where the time goes:
time: 808 us; the launch traced here: 806 us
  waiting for transfers between devices  314 us (39%)
  other arithmetic  268 us (33%)
  blocking collectives  147 us (18%)
  matrix products  28.4 us (4%)
  starting transfers between devices  21.4 us (3%)
  between operations  16.6 us (2%)
  local copies, waits for them, and re-layouts  10.1 us (1%)
    unnamed x4, other arithmetic  258 us
    reduce_scatter x1, waiting for transfers between devices, per_device(): lax.psum_scatter(lax.dot_general(grad_logits, head_weight, (((1,), (1,)),...  233 us
    psum x1, blocking collectives, per_device(): lax.psum((local_total, target_part), ('seq', 'vocab'))  74.5 us
    pmax x1, blocking collectives, per_device(): row_peak = lax.pmax(local_peak, ('seq', 'vocab'))  72.9 us
    psum x1, waiting for transfers between devices, per_device(): whole_rows = lax.psum(partial_rows, 'vocab')  63 us
    all_to_all x1, waiting for transfers between devices, per_device(): lax.all_to_all(outgoing, 'seq', split_axis=1, concat_axis=1, tiled=True)  17.4 us
  transfers between devices with their start and end apart: 5, of which 4 were waited for; matrix products, arithmetic and copies ran while one was open for 33% of the time, Pallas kernels for 0%

commit v1 on v0

v1 whole, which is shorter than its diff:
```python
import jax
import jax.numpy as jnp
from jax import lax
from jax.experimental import pallas as pl
from jax.experimental.pallas import tpu as pltpu
from jax.sharding import PartitionSpec as P

norm_eps = 1e-06
loss_scale = 16.0
f32, bf16 = jnp.float32, jnp.bfloat16

NX, NY, NZ = 4, 4, 8
GROUPS = NX * NZ
X_LINES = [[z * NX + x for x in range(NX)] for z in range(NZ)]
Z_LINES = [[z * NX + x for z in range(NZ)] for x in range(NX)]
Y_LINES = [[y * 2 + core for y in range(NY)] for core in range(2)]
OTHER_CORE = [(i, i ^ 1) for i in range(2 * NY)]
VMEM = 48 * 2**20


def params():
    return pltpu.CompilerParams(vmem_limit_bytes=VMEM)


def teacher_kernel(first_ref, index_ref, logprob_ref, dense_ref):
    local = index_ref[...] - first_ref[0]
    prob = jnp.exp(logprob_ref[...])
    rows, entries = local.shape
    lanes = lax.broadcasted_iota(jnp.int32, dense_ref.shape, 1)
    dense = jnp.zeros(dense_ref.shape, f32)
    for j in range(entries):
        dense = jnp.where(local[:, j : j + 1] == lanes, prob[:, j : j + 1], dense)
    dense_ref[...] = dense


def teacher_rows(first_column, index, logprob, width):
    tokens, entries = index.shape
    block = 64
    return pl.pallas_call(
        teacher_kernel,
        grid_spec=pltpu.PrefetchScalarGridSpec(
            num_scalar_prefetch=1,
            grid=(tokens // block,),
            in_specs=[pl.BlockSpec((block, entries), lambda i, s: (i, 0))] * 2,
            out_specs=pl.BlockSpec((block, width), lambda i, s: (i, 0)),
        ),
        out_shape=jax.ShapeDtypeStruct((tokens, width), f32),
        cost_estimate=pl.CostEstimate(flops=3 * tokens * width * entries, bytes_accessed=4 * tokens * width, transcendentals=0),
        compiler_params=params(),
        name="teacher_rows",
    )(first_column.reshape(1), index, logprob)


def logits_own_kernel(block_ref, rows_ref, weight_ref, out_ref):
    part = jnp.dot(rows_ref[0], weight_ref[...], preferred_element_type=f32)

    @pl.when(pl.program_id(0) == 0)
    def _():
        out_ref[...] = part

    @pl.when(pl.program_id(0) > 0)
    def _():
        out_ref[...] += part


def logits_rest_kernel(block_ref, rows_ref, weight_ref, own_ref, dense_ref, out_ref, stats_ref):
    part = jnp.dot(rows_ref[0], weight_ref[...], preferred_element_type=f32)

    @pl.when(pl.program_id(0) == 0)
    def _():
        out_ref[...] = own_ref[...] + part

    @pl.when(pl.program_id(0) > 0)
    def _():
        out_ref[...] += part

    @pl.when(pl.program_id(0) == pl.num_programs(0) - 1)
    def _():
        step = 128
        lanes = lax.broadcasted_iota(jnp.int32, (step, 128), 1)
        for i in range(0, out_ref.shape[0], step):
            logits = out_ref[i : i + step, :]
            peak = jnp.max(logits, axis=1, keepdims=True)
            total = peak + jnp.log(jnp.sum(jnp.exp(logits - peak), axis=1, keepdims=True))
            target = jnp.sum(logits * dense_ref[i : i + step, :], axis=1, keepdims=True)
            both = jnp.where(lanes == 0, total, jnp.where(lanes == 1, target, 0.0))
            stats_ref[:, i : i + step] = both.T[: stats_ref.shape[0], :]


def logits_own(blocks, rows, weight):
    count, tokens, share = rows.shape
    width = weight.shape[1]
    return pl.pallas_call(
        logits_own_kernel,
        grid_spec=pltpu.PrefetchScalarGridSpec(
            num_scalar_prefetch=1,
            grid=(count,),
            in_specs=[
                pl.BlockSpec((1, tokens, share), lambda k, b: (k, 0, 0)),
                pl.BlockSpec((share, width), lambda k, b: (b[k], 0)),
            ],
            out_specs=pl.BlockSpec((tokens, width), lambda k, b: (0, 0)),
        ),
        out_shape=jax.ShapeDtypeStruct((tokens, width), f32),
        cost_estimate=pl.CostEstimate(flops=2 * count * tokens * share * width, bytes_accessed=8 * 2**20, transcendentals=0),
        compiler_params=params(),
        name="logits_own",
    )(blocks, rows, weight)


def logits_rest(blocks, rows, weight, own, dense):
    count, tokens, share = rows.shape
    width = weight.shape[1]
    whole = pl.BlockSpec((tokens, width), lambda k, b: (0, 0))
    return pl.pallas_call(
        logits_rest_kernel,
        grid_spec=pltpu.PrefetchScalarGridSpec(
            num_scalar_prefetch=1,
            grid=(count,),
            in_specs=[
                pl.BlockSpec((1, tokens, share), lambda k, b: (k, 0, 0)),
                pl.BlockSpec((share, width), lambda k, b: (b[k], 0)),
                whole,
                whole,
            ],
            out_specs=[whole, pl.BlockSpec((8, tokens), lambda k, b: (0, 0))],
        ),
        out_shape=[jax.ShapeDtypeStruct((tokens, width), f32), jax.ShapeDtypeStruct((8, tokens), f32)],
        cost_estimate=pl.CostEstimate(flops=2 * count * tokens * share * width, bytes_accessed=12 * 2**20, transcendentals=0),
        compiler_params=params(),
        name="logits_rest",
    )(blocks, rows, weight, own, dense)


def times_weight(grad, weight):
    return lax.dot_general(grad, weight, (((1,), (1,)), ((), ())), preferred_element_type=f32)


def grad_rest_kernel(block_ref, totals_ref, logits_ref, dense_ref, logprob_ref, weight_ref, grad_ref, out_ref):
    @pl.when(pl.program_id(0) == 0)
    def _():
        step = 128
        for i in range(0, logits_ref.shape[0], step):
            totals = totals_ref[:, i : i + step]
            peak = jnp.max(totals, axis=0, keepdims=True)
            total = peak + jnp.log(jnp.sum(jnp.exp(totals - peak), axis=0, keepdims=True))
            column = jnp.broadcast_to(total, (128, step)).T[:, :1]
            mass = jnp.sum(jnp.exp(logprob_ref[i : i + step, :]), axis=1, keepdims=True)
            student = mass * jnp.exp(logits_ref[i : i + step, :] - column)
            grad_ref[i : i + step, :] = (loss_scale * (student - dense_ref[i : i + step, :])).astype(bf16)

    out_ref[0] = times_weight(grad_ref[...], weight_ref[...]).astype(bf16)


def grad_rest(blocks, totals, logits, dense, logprob, weight):
    tokens, width = logits.shape
    count = blocks.shape[0]
    share = weight.shape[0] // (2 * count)
    whole = pl.BlockSpec((tokens, width), lambda k, b: (0, 0))
    return pl.pallas_call(
        grad_rest_kernel,
        grid_spec=pltpu.PrefetchScalarGridSpec(
            num_scalar_prefetch=1,
            grid=(count,),
            in_specs=[
                pl.BlockSpec(totals.shape, lambda k, b: (0, 0)),
                whole,
                whole,
                pl.BlockSpec(logprob.shape, lambda k, b: (0, 0)),
                pl.BlockSpec((share, width), lambda k, b: (b[k], 0)),
            ],
            out_specs=[whole, pl.BlockSpec((1, tokens, share), lambda k, b: (k, 0, 0))],
        ),
        out_shape=[jax.ShapeDtypeStruct((tokens, width), bf16), jax.ShapeDtypeStruct((count, tokens, share), bf16)],
        cost_estimate=pl.CostEstimate(flops=2 * count * tokens * share * width, bytes_accessed=12 * 2**20, transcendentals=0),
        compiler_params=params(),
        name="grad_rest",
    )(blocks, totals, logits, dense, logprob, weight)


def grad_own_kernel(block_ref, grad_ref, weight_ref, other_ref, out_ref):
    out_ref[0] = (times_weight(grad_ref[...], weight_ref[...]) + other_ref[0].astype(f32)).astype(bf16)


def grad_own(blocks, grad, weight, other):
    count, tokens, share = other.shape
    width = weight.shape[1]
    piece = pl.BlockSpec((1, tokens, share), lambda k, b: (k, 0, 0))
    return pl.pallas_call(
        grad_own_kernel,
        grid_spec=pltpu.PrefetchScalarGridSpec(
            num_scalar_prefetch=1,
            grid=(count,),
            in_specs=[
                pl.BlockSpec((tokens, width), lambda k, b: (0, 0)),
                pl.BlockSpec((share, width), lambda k, b: (b[k], 0)),
                piece,
            ],
            out_specs=piece,
        ),
        out_shape=jax.ShapeDtypeStruct(other.shape, bf16),
        cost_estimate=pl.CostEstimate(flops=2 * count * tokens * share * width, bytes_accessed=12 * 2**20, transcendentals=0),
        compiler_params=params(),
        name="grad_own",
    )(blocks, grad, weight, other)


def weight_grad_kernel(block_ref, own_ref, rest_ref, grad_ref, out_ref):
    def write(rows):
        out_ref[...] = lax.dot_general(
            rows, grad_ref[...], (((0,), (0,)), ((), ())), preferred_element_type=f32
        ).astype(bf16)

    half = pl.num_programs(0) // 2

    @pl.when(pl.program_id(0) < half)
    def _():
        write(own_ref[0])

    @pl.when(pl.program_id(0) >= half)
    def _():
        write(rest_ref[0])


def weight_grad(blocks, own, rest, grad):
    count, tokens, share = own.shape
    width = grad.shape[1]
    return pl.pallas_call(
        weight_grad_kernel,
        grid_spec=pltpu.PrefetchScalarGridSpec(
            num_scalar_prefetch=1,
            grid=(2 * count,),
            in_specs=[
                pl.BlockSpec((1, tokens, share), lambda k, b: (jnp.minimum(k, count - 1), 0, 0)),
                pl.BlockSpec((1, tokens, share), lambda k, b: (jnp.maximum(k - count, 0), 0, 0)),
                pl.BlockSpec((tokens, width), lambda k, b: (0, 0)),
            ],
            out_specs=pl.BlockSpec((share, width), lambda k, b: (b[k], 0)),
        ),
        out_shape=jax.ShapeDtypeStruct((2 * count * share, width), bf16),
        cost_estimate=pl.CostEstimate(flops=4 * count * tokens * share * width, bytes_accessed=12 * 2**20, transcendentals=0),
        compiler_params=params(),
        name="weight_grad",
    )(blocks, own, rest, grad)


def exchange(x, axis, lines=None):
    return lax.all_to_all(x, axis, 0, 0, tiled=True, axis_index_groups=lines)


def to_all(x, count):
    return jnp.broadcast_to(x[None], (count, *x.shape))


def per_device(rollout, group_count, final_gain, head_weight, teacher_index, teacher_logprob):
    slots, features = rollout.shape
    tokens, entries = teacher_index.shape
    width = head_weight.shape[1]
    parts = 2 * NY
    share = features // parts
    class_rows = tokens // NX
    turns = slots // NX
    pack_rows = tokens // GROUPS
    seq = lax.axis_index("seq")
    own_z, own_x = seq // NX, seq % NX
    vocab = lax.axis_index("vocab")
    core = vocab % 2
    feature_start = vocab * share

    group_ids = jnp.arange(GROUPS, dtype=jnp.int32)
    before = group_ids[None, :] < group_ids[:, None]
    offsets = jnp.sum(jnp.where(before, group_count[None, :], 0), axis=1)
    own_offset = offsets[seq]
    own_count = group_count[seq]
    turn_ids = jnp.arange(turns, dtype=jnp.int32)

    values = rollout.astype(f32)
    inv_rms = lax.rsqrt(jnp.mean(values * values, axis=1, keepdims=True) + norm_eps)
    x_share = lax.dynamic_slice_in_dim(rollout, feature_start, share, 1).astype(f32)
    gain_share = lax.dynamic_slice_in_dim(final_gain, feature_start, share, 0)
    normed = (x_share * inv_rms * gain_share).astype(bf16)
    class_ids = jnp.arange(NX, dtype=jnp.int32)
    source_row = ((class_ids[:, None] - own_offset) % NX + NX * turn_ids[None, :]).reshape(-1)
    slot_ids = jnp.arange(slots, dtype=jnp.int32)
    sort_rows = ((source_row[:, None] == slot_ids[None, :]) & (source_row < own_count)[:, None]).astype(bf16)
    by_class = jnp.dot(sort_rows, normed, preferred_element_type=f32).astype(bf16)
    of_class = exchange(by_class.reshape(NX, turns, share), "seq", X_LINES)
    of_class = exchange(to_all(of_class.reshape(slots, share), NZ), "seq", Z_LINES)

    row_in_group = (own_x - offsets[:, None]) % NX + NX * turn_ids[None, :]
    place = jnp.where(row_in_group < group_count[:, None], (offsets[:, None] + row_in_group) // NX, class_rows)
    place = place.reshape(-1)
    place_ids = jnp.arange(class_rows, dtype=jnp.int32)
    spread = (place[:, None] == place_ids[None, :]).astype(bf16)
    dense_rows = lax.dot_general(
        spread, of_class.reshape(-1, share), (((0,), (0,)), ((), ())), preferred_element_type=f32
    ).astype(bf16)
    all_x = exchange(to_all(dense_rows, NX), "seq", X_LINES).reshape(tokens, share)
    own_rows = exchange(to_all(all_x, NY), "vocab", Y_LINES)
    rest_rows = lax.ppermute(own_rows, "vocab", OTHER_CORE)

    def class_order(a):
        return a.reshape(NZ, NX, pack_rows, entries).transpose(1, 2, 0, 3).reshape(tokens, entries)

    index = class_order(teacher_index)
    logprob = class_order(teacher_logprob)
    first_column = (seq * parts + vocab) * width
    dense = teacher_rows(first_column, index, logprob, width)

    y_ids = jnp.arange(NY, dtype=jnp.int32)
    own_blocks = 2 * y_ids + core
    rest_blocks = 2 * y_ids + 1 - core
    logits_part = logits_own(own_blocks, own_rows, head_weight)
    logits, stats = logits_rest(rest_blocks, rest_rows, head_weight, logits_part, dense)
    stats = exchange(to_all(stats[:2], parts), "vocab")
    peak = jnp.max(stats[:, 0], axis=0)
    part_total = peak + jnp.log(jnp.sum(jnp.exp(stats[:, 0] - peak), axis=0))
    part_target = jnp.sum(stats[:, 1], axis=0)
    stats = exchange(to_all(jnp.stack([part_total, part_target]), GROUPS), "seq")
    totals = stats[:, 0]

    grad, rest_grad = grad_rest(rest_blocks, totals, logits, dense, logprob, head_weight)
    other_grad = lax.ppermute(rest_grad, "vocab", OTHER_CORE)
    chip_grad = grad_own(own_blocks, grad, head_weight, other_grad)
    grad_weight = weight_grad(jnp.concatenate([own_blocks, rest_blocks]), own_rows, rest_rows, grad)

    y_grad = jnp.sum(exchange(chip_grad, "vocab", Y_LINES).astype(f32), axis=0).astype(bf16)
    x_grad = jnp.sum(
        exchange(y_grad.reshape(NX, class_rows, share), "seq", X_LINES).astype(f32), axis=0
    ).astype(bf16)
    spread_grad = jnp.dot(spread, x_grad, preferred_element_type=f32).astype(bf16)
    z_grad = jnp.sum(exchange(spread_grad.reshape(NZ, slots, share), "seq", Z_LINES).astype(f32), axis=0)
    sorted_grad = exchange(z_grad.reshape(NX, turns, share), "seq", X_LINES).reshape(slots, share)
    from_row = (own_offset + slot_ids) % NX * turns + slot_ids // NX
    grad_normed = jnp.take(sorted_grad, from_row, axis=0)

    u = grad_normed * gain_share
    row_dots = jnp.sum(exchange(to_all(jnp.sum(u * x_share, axis=1), parts), "vocab"), axis=0)[:, None]
    grad_rows = (u - x_share * inv_rms * inv_rms * row_dots / features) * inv_rms
    grad_rollout = jnp.where((slot_ids < own_count)[:, None], grad_rows, 0.0).astype(bf16)

    peak = jnp.max(totals, axis=0)
    log_total = peak + jnp.log(jnp.sum(jnp.exp(totals - peak), axis=0))
    target = jnp.sum(stats[:, 1], axis=0)
    prob = jnp.exp(logprob)
    kl_all = jnp.sum(prob * logprob, axis=1) - target + jnp.sum(prob, axis=1) * log_total
    kl_x = lax.dynamic_slice_in_dim(kl_all, own_x * class_rows, class_rows).reshape(pack_rows, NZ)
    kl = jnp.sum(jnp.where(jnp.arange(NZ)[None, :] == own_z, kl_x, 0.0), axis=1)
    return (kl, grad_weight, grad_rollout)


def solution(mesh):
    placed = (P("seq", None), P(), P(), P(None, ("seq", "vocab")), P(), P())
    return jax.shard_map(
        per_device,
        mesh=mesh,
        in_specs=placed,
        out_specs=(P("seq"), P(None, ("seq", "vocab")), P("seq", "vocab")),
        check_vma=False,
    )
```

time: 808 us -> 302 us (0.37)
  waiting for transfers between devices: 314 us -> 34.3 us
  other arithmetic: 268 us -> 21 us
  Pallas kernels: 0 us -> 60.4 us
  blocking collectives: 147 us -> 115 us
  local copies, waits for them, and re-layouts: 10.1 us -> 36.1 us
  matrix products: 28.4 us -> 2.56 us
  between operations: 16.6 us -> 0.99 us
    unnamed x4 -> x0, other arithmetic: 258 us -> none
    reduce_scatter x1 -> x0, waiting for transfers between devices: 233 us -> none  [per_device(): lax.psum_scatter(lax.dot_general(grad_logits, head_weight, (((1,), (1,)),...]
    all_to_all x0 -> x5, blocking collectives: none -> 115 us  [exchange(): return lax.all_to_all(x, axis, 0, 0, tiled=True, axis_index_groups=lines)]
    psum x1 -> x0, blocking collectives: 74.5 us -> none  [per_device(): lax.psum((local_total, target_part), ('seq', 'vocab'))]
    pmax x1 -> x0, blocking collectives: 72.9 us -> none  [per_device(): row_peak = lax.pmax(local_peak, ('seq', 'vocab'))]
    psum x1 -> x0, waiting for transfers between devices: 63 us -> none  [per_device(): whole_rows = lax.psum(partial_rows, 'vocab')]
    pallas_call x0 -> x6, Pallas kernels: none -> 60.4 us  [the longest x1 24.3 us: teacher_rows(): pl.pallas_call(teacher_kernel, grid_spec=pltpu.PrefetchScalarGridSpec(num...]
    dot_general x3, matrix products: 28.4 us -> 2.56 us  [the longest x1 1.21 us: per_device(): jnp.dot(spread, x_grad, preferred_element_type=f32).astype(bf16)]
  transfers between devices with their start and end apart: 5 -> 8, of which waited for: 4 -> 5; matrix products, arithmetic and copies ran while one was open for 33% -> 11% of each run, Pallas kernels for 0% -> 13%
where the time goes in v1:
time: 302 us; the launch traced here: 299 us
  blocking collectives  115 us (38%)
  Pallas kernels  60.4 us (20%)
  local copies, waits for them, and re-layouts  36.1 us (12%)
  waiting for transfers between devices  34.3 us (11%)
  starting transfers between devices  28.4 us (9%)
  other arithmetic  21 us (7%)
    all_to_all x5, blocking collectives, exchange(): return lax.all_to_all(x, axis, 0, 0, tiled=True, axis_index_groups=lines)  115 us
    all_to_all x6, waiting for transfers between devices, exchange(): return lax.all_to_all(x, axis, 0, 0, tiled=True, axis_index_groups=lines)  28.4 us
    all_to_all x6, starting transfers between devices, exchange(): return lax.all_to_all(x, axis, 0, 0, tiled=True, axis_index_groups=lines)  28.4 us
    pallas_call x1, Pallas kernels, teacher_rows(): pl.pallas_call(teacher_kernel, grid_spec=pltpu.PrefetchScalarGridSpec(num...  24.3 us
    unnamed x37, local copies, waits for them, and re-layouts  23.4 us
    pallas_call x1, Pallas kernels, weight_grad(): pl.pallas_call(weight_grad_kernel, grid_spec=pltpu.PrefetchScalarGridSpec...  10.3 us
    pallas_call x1, Pallas kernels, grad_rest(): pl.pallas_call(grad_rest_kernel, grid_spec=pltpu.PrefetchScalarGridSpec(n...  7.14 us
    pallas_call x1, Pallas kernels, logits_rest(): pl.pallas_call(logits_rest_kernel, grid_spec=pltpu.PrefetchScalarGridSpec...  7.12 us
  transfers between devices with their start and end apart: 8, of which 5 were waited for; matrix products, arithmetic and copies ran while one was open for 11% of the time, Pallas kernels for 13%

profile of v1, /device:TPU:8, one launch (start us, length us, event | category | flops | bytes accessed | tf_op | source)
XLA Modules:
  0.0 298.8 jit_solution(4777808946251422534)
XLA Ops:
  1.4 1.2 dynamic_slice.16
  8.9 4.3 %all-to-all-start = ((bf16[4,9,512]{2,1,0:T(8,128)(2,1)}), bf16[4,9,512]{2,1,0:T(8,128)(2,1)S(1)}, u32[]{:S(2)}, u32[]{:S(2)}) async-start(bf16[4,9,512]{2,1,0:T(8,128)(2,1)} %reshape.307), calls=%async_computation | async-start | bytes 131072 | tf_op jit(solution)/shard_map/all_to_all | solution.py:248
  13.2 5.6 %all-to-all-done = bf16[4,9,512]{2,1,0:T(8,128)(2,1)S(1)} async-done(((bf16[4,9,512]{2,1,0:T(8,128)(2,1)}), bf16[4,9,512]{2,1,0:T(8,128)(2,1)S(1)}, u32[]{:S(2)}, u32[]{:S(2)}) %all-to-all-start) | async-done | bytes 36896 | tf_op jit(solution)/shard_map/all_to_all | solution.py:248
  19.6 8.5 %all-to-all-start.1 = ((bf16[8,36,512]{2,1,0:T(8,128)(2,1)}), bf16[8,36,512]{2,1,0:T(8,128)(2,1)S(1)}, u32[]{:S(2)}, u32[]{:S(2)}) async-start(bf16[8,36,512]{2,1,0:T(8,128)(2,1)} %broadcast_in_dim.67), calls=%async_computation.1 | async-start | bytes 655360 | tf_op jit(solution)/shard_map/all_to_all | solution.py:248
  29.1 10.8 %all-to-all-done.1 = bf16[8,36,512]{2,1,0:T(8,128)(2,1)S(1)} async-done(((bf16[8,36,512]{2,1,0:T(8,128)(2,1)}), bf16[8,36,512]{2,1,0:T(8,128)(2,1)S(1)}, u32[]{:S(2)}, u32[]{:S(2)}) %all-to-all-start.1) | async-done | bytes 294944 | tf_op jit(solution)/shard_map/all_to_all | solution.py:248
  40.4 11.9 %all_to_all.56 = bf16[4,192,512]{2,1,0:T(8,128)(2,1)S(1)} all-to-all(bf16[4,192,512]{2,1,0:T(8,128)(2,1)S(1)} %broadcast_in_dim.68), channel_id=1, replica_groups={{0,8,16,24},{32,40,48,56},{64,72,80,88},{96,104,112,120},{128,136,144,1..., dimensions={0} | all-to-all | bytes 1572864 | tf_op jit(solution)/shard_map/all_to_all | solution.py:248
  52.6 36.6 %all_to_all.57.rows_ref.own_ref = bf16[4,768,512]{2,1,0:T(8,128)(2,1)S(1)} all-to-all(bf16[4,768,512]{2,1,0:T(8,128)(2,1)S(1)} %broadcast_in_dim.116), channel_id=1, replica_groups={{0,2,4,6},{1,3,5,7},{8,10,12,14},{9,11,13,15},{16,18,20,22},{17,19,21,2..., dimensions={0} | all-to-all | bytes 6291456 | tf_op jit(solution)/shard_map/all_to_all | solution.py:248
  89.2 7.8 %copy.55.weight_ref = bf16[4096,594]{1,0:T(8,128)(2,1)} copy(bf16[4096,594]{0,1:T(8,128)(2,1)} %param.9) | data formatting | bytes 9732096 | tf_op args[3]
  99.2 1.8 copy.52
  101.0 2.0 copy.53
  104.0 24.3 %teacher_rows.1.dense_ref = f32[768,594]{1,0:T(8,128)S(1)} custom-call(s32[1]{0:T(128)} %bitcast.5.first_ref, s32[768,64]{1,0:T(8,128)S(1)} %bitcast.31, f32[768,64]{1,0:T(8,128)S(1)} %bitcast.29), custom_call_target="tpu_custom_call" | custom-call | flops 87588864 | bytes 1824768 | tf_op jit(solution)/shard_map/teacher_rows/pallas_call | solution.py:39
  128.4 5.6 %logits_own.1.own_ref = f32[768,594]{1,0:T(8,128)S(1)} custom-call(s32[4]{0:T(128)S(1)} %get-tuple-element.35.block_ref, bf16[4,768,512]{2,1,0:T(8,128)(2,1)S(1)} %all_to_all.57.rows_ref.own_ref, bf16[4096,594]{1,0:T(8,128)(2,1)} %copy.55.weight_ref), custom_call_target="tpu_custom_call" | custom-call | flops 1868562432 | bytes 8388608 | tf_op jit(solution)/shard_map/logits_own/pallas_call | solution.py:93
  134.0 7.1 %logits_rest.1 = (f32[768,594]{1,0:T(8,128)S(1)}, f32[8,768]{1,0:T(8,128)S(1)}) custom-call(s32[4]{0:T(128)S(1)} %get-tuple-element.34.block_ref, bf16[4,768,512]{2,1,0:T(8,128)(2,1)} %collective-permute-done.rows_ref.rest_ref, bf16[4096,594]{1,0:T(8,128)(2,1)} %copy.55.weight_ref, f32[768,594]{1,0:T(8,128)S(1)} %logits_own.1.own_ref, ...), custom_call_target="tpu_custom_call" | custom-call | flops 1868562432 | bytes 12582912 | tf_op jit(solution)/shard_map/logits_rest/pallas_call | solution.py:115
  141.2 7.9 %all_to_all.58 = f32[8,2,768]{2,1,0:T(2,128)S(1)} all-to-all(f32[8,2,768]{2,1,0:T(2,128)S(1)} %broadcast_in_dim.117), channel_id=1, replica_groups=mesh['seq'=32,'vocab'=8] {'vocab'}, dimensions={0} | all-to-all | bytes 98304 | tf_op jit(solution)/shard_map/all_to_all | solution.py:248
  149.3 17.1 %all_to_all.59 = f32[32,2,768]{2,1,0:T(2,128)S(1)} all-to-all(f32[32,2,768]{2,1,0:T(2,128)S(1)} %broadcast_in_dim.118), channel_id=1, replica_groups=mesh['seq'=32,'vocab'=8] {'seq'}, dimensions={0} | all-to-all | bytes 393216 | tf_op jit(solution)/shard_map/all_to_all | solution.py:248
  167.9 7.1 %grad_rest.1 = (bf16[768,594]{1,0:T(8,128)(2,1)S(1)}, bf16[4,768,512]{2,1,0:T(8,128)(2,1)}) custom-call(s32[4]{0:T(128)S(1)} %get-tuple-element.34.block_ref, f32[32,768]{1,0:T(8,128)S(1)} %bitcast.32, f32[768,594]{1,0:T(8,128)S(1)} %get-tuple-element.8.logits_ref, f32[768,594]{1,0:T(8,128)S(1)} %teacher_rows.1.dense_ref, f32[768,64]{1,0:T(8,128)S(1)} %bitcast.30, ...), custom_call_target="tpu_custom_call" | custom-call | flops 1868562432 | bytes 12582912 | tf_op jit(solution)/shard_map/grad_rest/pallas_call | solution.py:160
  175.0 5.9 %collective-permute-done.1.other_ref = bf16[4,768,512]{2,1,0:T(8,128)(2,1)S(1)} collective-permute-done((bf16[4,768,512]{2,1,0:T(8,128)(2,1)}, bf16[4,768,512]{2,1,0:T(8,128)(2,1)S(1)}, u32[]{:S(2)}, u32[]{:S(2)}) %collective-permute-start.1) | collective-permute-done | bytes 3145760 | tf_op jit(solution)/shard_map/ppermute | solution.py:323
  180.9 1.7 copy-done.4
  182.6 5.8 %grad_own.1 = bf16[4,768,512]{2,1,0:T(8,128)(2,1)S(1)} custom-call(s32[4]{0:T(128)S(1)} %get-tuple-element.35.block_ref, bf16[768,594]{1,0:T(8,128)(2,1)S(1)} %get-tuple-element.9.grad_ref, bf16[4096,594]{1,0:T(8,128)(2,1)} %copy.55.weight_ref, bf16[4,768,512]{2,1,0:T(8,128)(2,1)} %copy-done.4), custom_call_target="tpu_custom_call" | custom-call | flops 1868562432 | bytes 12582912 | tf_op jit(solution)/shard_map/grad_own/pallas_call | solution.py:189
  188.4 41.5 %all_to_all.60 = bf16[4,768,512]{2,1,0:T(8,128)(2,1)} all-to-all(bf16[4,768,512]{2,1,0:T(8,128)(2,1)S(1)} %grad_own.1), channel_id=1, replica_groups={{0,2,4,6},{1,3,5,7},{8,10,12,14},{9,11,13,15},{16,18,20,22},{17,19,21,2..., dimensions={0} | all-to-all | bytes 6291456 | tf_op jit(solution)/shard_map/all_to_all | solution.py:248
  229.9 3.5 %reduce_sum.147 = bf16[768,512]{1,0:T(8,128)(2,1)} reduce(bf16[4,768,512]{2,1,0:T(8,128)(2,1)} %all_to_all.60, bf16[]{:T(256)} %constant.138.clone.1), dimensions={0}, to_apply=%region_11.12 | reduce | flops 1179648 | bytes 3932162 | tf_op jit(solution)/shard_map/reduce_sum | solution.py:327
  233.4 4.2 %all-to-all-start.7 = ((bf16[4,192,512]{2,1,0:T(8,128)(2,1)}), bf16[4,192,512]{2,1,0:T(8,128)(2,1)}, u32[]{:S(2)}, u32[]{:S(2)}) async-start(bf16[4,192,512]{2,1,0:T(8,128)(2,1)} %bitcast.35), calls=%async_computation.7 | async-start | bytes 1572864 | tf_op jit(solution)/shard_map/all_to_all | solution.py:248
  241.2 1.3 pad_clamp_fusion
  243.4 6.3 %all-to-all-done.7 = bf16[4,192,512]{2,1,0:T(8,128)(2,1)} async-done(((bf16[4,192,512]{2,1,0:T(8,128)(2,1)}), bf16[4,192,512]{2,1,0:T(8,128)(2,1)}, u32[]{:S(2)}, u32[]{:S(2)}) %all-to-all-start.7) | async-done | bytes 786464 | tf_op jit(solution)/shard_map/all_to_all | solution.py:248
  249.7 2.0 reduce_sum.148
  253.7 3.4 %all-to-all-start.8 = ((bf16[8,36,512]{2,1,0:T(8,128)(2,1)}), bf16[8,36,512]{2,1,0:T(8,128)(2,1)S(1)}, u32[]{:S(2)}, u32[]{:S(2)}) async-start(bf16[8,36,512]{2,1,0:T(8,128)(2,1)} %reshape.315), calls=%async_computation.8 | async-start | bytes 655360 | tf_op jit(solution)/shard_map/all_to_all | solution.py:248
  261.5 10.3 %weight_grad.1 = bf16[4096,594]{1,0:T(8,128)(2,1)} custom-call(s32[8]{0:T(128)S(1)} %pad_add_fusion.block_ref, bf16[4,768,512]{2,1,0:T(8,128)(2,1)S(1)} %all_to_all.57.rows_ref.own_ref, bf16[4,768,512]{2,1,0:T(8,128)(2,1)} %collective-permute-done.rows_ref.rest_ref, bf16[768,594]{1,0:T(8,128)(2,1)S(1)} %copy-done.2), custom_call_target="tpu_custom_call" | custom-call | flops 3737124864 | bytes 12582912 | tf_op jit(solution)/shard_map/weight_grad/pallas_call | solution.py:228
  272.6 3.3 %all-to-all-start.9 = ((f32[4,9,512]{2,1,0:T(8,128)}), f32[4,9,512]{2,1,0:T(8,128)S(1)}, u32[]{:S(2)}, u32[]{:S(2)}) async-start(f32[4,9,512]{2,1,0:T(8,128)} %reshape.316), calls=%async_computation.9 | async-start | bytes 262144 | tf_op jit(solution)/shard_map/all_to_all | solution.py:248
  276.1 5.8 %all-to-all-done.9 = f32[4,9,512]{2,1,0:T(8,128)S(1)} async-done(((f32[4,9,512]{2,1,0:T(8,128)}), f32[4,9,512]{2,1,0:T(8,128)S(1)}, u32[]{:S(2)}, u32[]{:S(2)}) %all-to-all-start.9) | async-done | bytes 73760 | tf_op jit(solution)/shard_map/all_to_all | solution.py:248
  284.2 4.7 %all-to-all-start.10 = ((f32[8,1,36]{2,1,0:T(1,128)}), f32[8,1,36]{2,1,0:T(1,128)S(1)}, u32[]{:S(2)}, u32[]{:S(2)}) async-start(f32[8,1,36]{2,1,0:T(1,128)} %broadcast_in_dim.123), calls=%async_computation.10 | async-start | bytes 8192 | tf_op jit(solution)/shard_map/all_to_all | solution.py:248
  289.5 7.7 %copy.63 = bf16[4096,594]{0,1:T(8,128)(2,1)} copy(bf16[4096,594]{1,0:T(8,128)(2,1)} %weight_grad.1) | data formatting | bytes 9732096
  297.3 1.5 fusion.11
  (98 shorter events, 29.1 us)
Async XLA Ops:
  5.2 3.7 %copy-start.12 = (f32[36]{0:T(128)}, f32[36]{0:T(128)S(1)}, u32[]{:S(2)}) copy-start(f32[36]{0:T(128)S(1)} %add_rsqrt_fusion) | copy-start | bytes 436
  6.7 0.6 copy-start.7
  8.9 9.9 %all-to-all-start = ((bf16[4,9,512]{2,1,0:T(8,128)(2,1)}), bf16[4,9,512]{2,1,0:T(8,128)(2,1)S(1)}, u32[]{:S(2)}, u32[]{:S(2)}) async-start(bf16[4,9,512]{2,1,0:T(8,128)(2,1)} %reshape.307), calls=%async_computation | async-start | bytes 131072 | tf_op jit(solution)/shard_map/all_to_all | solution.py:248
  19.6 20.3 %all-to-all-start.1 = ((bf16[8,36,512]{2,1,0:T(8,128)(2,1)}), bf16[8,36,512]{2,1,0:T(8,128)(2,1)S(1)}, u32[]{:S(2)}, u32[]{:S(2)}) async-start(bf16[8,36,512]{2,1,0:T(8,128)(2,1)} %broadcast_in_dim.67), calls=%async_computation.1 | async-start | bytes 655360 | tf_op jit(solution)/shard_map/all_to_all | solution.py:248
  29.1 23.2 %copy-start.9 = (s32[288]{0:T(512)}, s32[288]{0:T(512)S(1)}, u32[]{:S(2)}) copy-start(s32[288]{0:T(512)S(1)} %fusion.24) | copy-start | bytes 3460
  89.2 44.8 %collective-permute-start = (bf16[4,768,512]{2,1,0:T(8,128)(2,1)S(1)}, bf16[4,768,512]{2,1,0:T(8,128)(2,1)}, u32[]{:S(2)}, u32[]{:S(2)}) collective-permute-start(bf16[4,768,512]{2,1,0:T(8,128)(2,1)S(1)} %all_to_all.57.rows_ref.own_ref), channel_id=1, source_target_pairs={{0,1},{1,0},{2,3},{3,2},{4,5},{5,4},{6,7},{7,6},{8,9},{9,8},{10,11... | collective-permute-start | bytes 9437192 | tf_op jit(solution)/shard_map/ppermute | solution.py:300
  89.2 7.8 %copy-start.6 = (f32[768,64]{0,1:T(8,128)S(1)}, f32[768,64]{0,1:T(8,128)}, u32[]{:S(2)}) copy-start(f32[768,64]{0,1:T(8,128)} %param.11) | copy-start | bytes 589828
  103.0 1.0 copy-start
  167.3 0.6 copy-start.5
  175.0 13.4 %copy-start.1 = (bf16[768,594]{1,0:T(8,128)(2,1)}, bf16[768,594]{1,0:T(8,128)(2,1)S(1)}, u32[]{:S(2)}) copy-start(bf16[768,594]{1,0:T(8,128)(2,1)S(1)} %get-tuple-element.9.grad_ref) | copy-start | bytes 2737156
  175.0 5.9 %collective-permute-start.1 = (bf16[4,768,512]{2,1,0:T(8,128)(2,1)}, bf16[4,768,512]{2,1,0:T(8,128)(2,1)S(1)}, u32[]{:S(2)}, u32[]{:S(2)}) collective-permute-start(bf16[4,768,512]{2,1,0:T(8,128)(2,1)} %get-tuple-element.10), channel_id=1, source_target_pairs={{0,1},{1,0},{2,3},{3,2},{4,5},{5,4},{6,7},{7,6},{8,9},{9,8},{10,11... | collective-permute-start | bytes 9437192 | tf_op jit(solution)/shard_map/ppermute | solution.py:323
  180.9 1.7 copy-start.4
  229.9 12.6 %copy-start.3 = (f32[768,64]{1,0:T(8,128)S(1)}, f32[768,64]{1,0:T(8,128)}, u32[]{:S(2)}) copy-start(f32[768,64]{1,0:T(8,128)} %copy.49) | copy-start | bytes 589828
  233.4 16.3 %all-to-all-start.7 = ((bf16[4,192,512]{2,1,0:T(8,128)(2,1)}), bf16[4,192,512]{2,1,0:T(8,128)(2,1)}, u32[]{:S(2)}, u32[]{:S(2)}) async-start(bf16[4,192,512]{2,1,0:T(8,128)(2,1)} %bitcast.35), calls=%async_computation.7 | async-start | bytes 1572864 | tf_op jit(solution)/shard_map/all_to_all | solution.py:248
  253.7 18.2 %all-to-all-start.8 = ((bf16[8,36,512]{2,1,0:T(8,128)(2,1)}), bf16[8,36,512]{2,1,0:T(8,128)(2,1)S(1)}, u32[]{:S(2)}, u32[]{:S(2)}) async-start(bf16[8,36,512]{2,1,0:T(8,128)(2,1)} %reshape.315), calls=%async_computation.8 | async-start | bytes 655360 | tf_op jit(solution)/shard_map/all_to_all | solution.py:248
  260.3 1.2 copy-start.2
  261.5 14.4 %copy-start.10 = (f32[768]{0:T(1024)S(1)}, f32[768]{0:T(1024)}, u32[]{:S(2)}) copy-start(f32[768]{0:T(1024)} %get-tuple-element.28) | copy-start | bytes 9220
  261.5 21.1 %copy-start.8 = (f32[512]{0:T(512)S(1)}, f32[512]{0:T(512)}, u32[]{:S(2)}) copy-start(f32[512]{0:T(512)} %copy-done.7) | copy-start | bytes 6148
  261.5 21.1 %copy-start.11 = (pred[36]{0:T(512)(128)(4,1)S(1)}, pred[36]{0:T(512)(128)(4,1)}, u32[]{:S(2)}) copy-start(pred[36]{0:T(512)(128)(4,1)} %compare_and_fusion) | copy-start | bytes 112
  261.5 27.4 %copy-start.15 = (pred[8]{0:T(512)(128)(4,1)S(1)}, pred[8]{0:T(512)(128)(4,1)}, u32[]{:S(2)}) copy-start(pred[8]{0:T(512)(128)(4,1)} %iota_compare_fusion.6) | copy-start | bytes 28
  272.6 9.3 %all-to-all-start.9 = ((f32[4,9,512]{2,1,0:T(8,128)}), f32[4,9,512]{2,1,0:T(8,128)S(1)}, u32[]{:S(2)}, u32[]{:S(2)}) async-start(f32[4,9,512]{2,1,0:T(8,128)} %reshape.316), calls=%async_computation.9 | async-start | bytes 262144 | tf_op jit(solution)/shard_map/all_to_all | solution.py:248
  284.2 13.0 %all-to-all-start.10 = ((f32[8,1,36]{2,1,0:T(1,128)}), f32[8,1,36]{2,1,0:T(1,128)S(1)}, u32[]{:S(2)}, u32[]{:S(2)}) async-start(f32[8,1,36]{2,1,0:T(1,128)} %broadcast_in_dim.123), calls=%async_computation.10 | async-start | bytes 8192 | tf_op jit(solution)/shard_map/all_to_all | solution.py:248
  289.5 7.7 %copy-start.13 = (f32[36]{0:T(128)S(1)}, f32[36]{0:T(128)}, u32[]{:S(2)}) copy-start(f32[36]{0:T(128)} %copy-done.12) | copy-start | bytes 436
  289.5 7.7 %copy-start.14 = (pred[36]{0:T(512)(128)(4,1)S(1)}, pred[36]{0:T(512)(128)(4,1)}, u32[]{:S(2)}) copy-start(pred[36]{0:T(512)(128)(4,1)} %iota_compare_fusion.5) | copy-start | bytes 112

commit v2 on v0

v2 whole, which is shorter than its diff:
```python
import jax
import jax.numpy as jnp
from jax import lax
from jax.experimental import pallas as pl
from jax.experimental.pallas import tpu as pltpu
from jax.sharding import PartitionSpec as P

norm_eps = 1e-06
loss_scale = 16.0
f32, bf16 = jnp.float32, jnp.bfloat16

NX, NY, NZ = 4, 4, 8
GROUPS = NX * NZ
OTHER_CORE = [(i, i ^ 1) for i in range(2 * NY)]
STEPS = (1, 3, 2)
VMEM = 40 * 2**20


def call(body, name, out, *operands, grid=(), prefetch=(), ins=None, outs=None, scratch=(), flops=0, size=0):
    whole = pl.BlockSpec(memory_space=pltpu.VMEM)
    if ins is None:
        ins, outs = [whole] * len(operands), jax.tree.map(lambda _: whole, out)
    return pl.pallas_call(
        body,
        grid_spec=pltpu.PrefetchScalarGridSpec(
            num_scalar_prefetch=len(prefetch), grid=grid, in_specs=ins, out_specs=outs, scratch_shapes=scratch
        ),
        out_shape=out,
        cost_estimate=pl.CostEstimate(flops=flops, bytes_accessed=size, transcendentals=0),
        compiler_params=pltpu.CompilerParams(vmem_limit_bytes=VMEM),
        name=name,
    )(*prefetch, *operands)


def array(shape, dtype):
    return jax.ShapeDtypeStruct(shape, dtype)


def dot(a, b, over_a=1, over_b=0):
    return lax.dot_general(a, b, (((over_a,), (over_b,)), ((), ())), preferred_element_type=f32)


def own_slots(at_ref, count_ref):
    seq = at_ref[2]
    offset = lax.fori_loop(0, GROUPS, lambda g, o: o + jnp.where(g < seq, count_ref[g], 0), jnp.int32(0))
    return offset, count_ref[seq]


def sort_kernel(at_ref, count_ref, rows_ref, gain_ref, out_ref, inv_ref):
    vocab = at_ref[3]
    slots, features = rows_ref.shape
    turns, share = out_ref.shape[1:]
    offset, count = own_slots(at_ref, count_ref)
    square = jnp.zeros((slots, share), f32)
    for i in range(0, features, share):
        values = rows_ref[:, i : i + share].astype(f32)
        square += values * values
    inv_rms = lax.rsqrt(jnp.sum(square, axis=1, keepdims=True) / features + norm_eps)
    inv_ref[...] = jnp.broadcast_to(inv_rms, inv_ref.shape)
    part = pl.ds(pl.multiple_of(vocab * share, share), share)
    normed = (rows_ref[:, part].astype(f32) * inv_rms * gain_ref[:, part]).astype(bf16)
    to = lax.broadcasted_iota(jnp.int32, (slots, slots), 0)
    source = lax.broadcasted_iota(jnp.int32, (slots, slots), 1)
    kind = sum((to >= i * turns).astype(jnp.int32) for i in range(1, NX))
    row = ((kind - offset) & (NX - 1)) + NX * (to - kind * turns)
    pick = jnp.where((row == source) & (row < count), 1.0, 0.0).astype(bf16)
    by_class = dot(pick, normed).astype(bf16)
    for g in range(out_ref.shape[0]):
        k = g % NX
        out_ref[g] = by_class[k * turns : (k + 1) * turns]


def teacher_kernel(first_ref, index_ref, logprob_ref, dense_ref):
    local = index_ref[...] - first_ref[0]
    prob = jnp.exp(logprob_ref[...])
    width, tokens = dense_ref.shape
    step = 200
    for start in range(0, width, step):
        size = min(step, width - start)
        ids = lax.broadcasted_iota(jnp.int32, (size, tokens), 0) + start
        dense = jnp.zeros((size, tokens), f32)
        for j in range(local.shape[0]):
            dense = jnp.where(local[j : j + 1, :] == ids, prob[j : j + 1, :], dense)
        dense_ref[start : start + size, :] = dense


def teacher_columns(first_column, index, logprob, width):
    entries, tokens = index.shape
    block = 128
    return call(
        teacher_kernel, "teacher_columns", array((width, tokens), f32), index, logprob,
        grid=(tokens // block,), prefetch=(first_column.reshape(1),),
        ins=[pl.BlockSpec((entries, block), lambda i, s: (0, i))] * 2,
        outs=pl.BlockSpec((width, block), lambda i, s: (0, i)),
        flops=4 * tokens * width * entries, size=4 * tokens * width,
    )


def place_kernel(at_ref, *refs):
    x, y = at_ref[0], at_ref[1]
    by_x, by_y, (x_ref, y_ref) = refs[:4], refs[4:8], refs[8:]
    for k in range(4):
        x_ref[(x + k) % 4] = by_x[k][...]
        y_ref[(y + k) % 4] = by_y[k][...]


def gather_kernel(at_ref, *refs):
    x, y = at_ref[0], at_ref[1]
    by_y, by_x, out_ref = refs[:4], refs[4:8], refs[8]
    rows = by_x[0].shape[1]
    for k in range(4):
        out_ref[(y + k) % 4, 0] = by_y[k][...]
        start = pl.multiple_of((x + k) % 4 * rows, 64)
        for j in range(4):
            out_ref[j, 1, pl.ds(start, rows), :] = by_x[k][j]


def logits_part(rows_ref, weight_ref):
    half = rows_ref.shape[3]
    return dot(weight_ref[:, :half], rows_ref[0, 0], 1, 1) + dot(weight_ref[:, half:], rows_ref[0, 1], 1, 1)


def logits_own_kernel(block_ref, rows_ref, weight_ref, out_ref):
    part = logits_part(rows_ref, weight_ref)

    @pl.when(pl.program_id(0) == 0)
    def _():
        out_ref[...] = part

    @pl.when(pl.program_id(0) > 0)
    def _():
        out_ref[...] += part


def logits_rest_kernel(block_ref, rows_ref, weight_ref, own_ref, dense_ref, out_ref, stats_ref):
    part = logits_part(rows_ref, weight_ref)

    @pl.when(pl.program_id(0) == 0)
    def _():
        out_ref[...] = own_ref[...] + part

    @pl.when(pl.program_id(0) > 0)
    def _():
        out_ref[...] += part

    @pl.when(pl.program_id(0) == pl.num_programs(0) - 1)
    def _():
        tokens, step = out_ref.shape[1], 128
        for i in range(0, tokens, step):
            logits = out_ref[:, i : i + step]
            peak = jnp.max(logits, axis=0, keepdims=True)
            total = peak + jnp.log(jnp.sum(jnp.exp(logits - peak), axis=0, keepdims=True))
            stats_ref[:, i : i + step] = total
            stats_ref[:, tokens + i : tokens + i + step] = jnp.sum(
                logits * dense_ref[:, i : i + step], axis=0, keepdims=True
            )


def logits_call(blocks, rows, weight, own=None, dense=None):
    count, _, tokens, half = rows.shape
    width = weight.shape[0]
    whole = pl.BlockSpec((width, tokens), lambda k, b: (0, 0))
    ins = [
        pl.BlockSpec((1, 2, tokens, half), lambda k, b: (k, 0, 0, 0)),
        pl.BlockSpec((width, 2 * half), lambda k, b: (0, b[k])),
    ]
    options = dict(grid=(count,), prefetch=(blocks,), flops=4 * count * tokens * half * width, size=8 * 2**20)
    logits = array((width, tokens), f32)
    if own is None:
        return call(logits_own_kernel, "logits_own", logits, rows, weight, ins=ins, outs=whole, **options)
    return call(
        logits_rest_kernel, "logits_rest", [logits, array((1, 2 * tokens), f32)], rows, weight, own, dense,
        ins=[*ins, whole, whole], outs=[whole, pl.BlockSpec((1, 2 * tokens), lambda k, b: (0, 0))], **options,
    )


def grad_rest_kernel(
    block_ref, totals_ref, logits_ref, dense_ref, logprob_ref, weight_ref, grad_ref, turned_ref, out_ref, pad_ref
):
    width, tokens = logits_ref.shape

    @pl.when(pl.program_id(0) == 0)
    def _():
        step = pad_ref.shape[1]
        pad_ref[...] = jnp.zeros(pad_ref.shape, f32)
        for i in range(0, tokens, step):
            totals = totals_ref[:, i : i + step]
            peak = jnp.max(totals, axis=0, keepdims=True)
            total = peak + jnp.log(jnp.sum(jnp.exp(totals - peak), axis=0, keepdims=True))
            mass = jnp.sum(jnp.exp(logprob_ref[:, i : i + step]), axis=0, keepdims=True)
            student = mass * jnp.exp(logits_ref[:, i : i + step] - total)
            grad = loss_scale * (student - dense_ref[:, i : i + step])
            grad_ref[:, i : i + step] = grad.astype(bf16)
            pad_ref[:width, :] = grad
            turned_ref[i : i + step, :] = pad_ref[...].T[:, :width].astype(bf16)

    out = dot(turned_ref[...], weight_ref[...]).astype(bf16)
    half = out_ref.shape[3]
    out_ref[0, 0] = out[:, :half]
    out_ref[0, 1] = out[:, half:]


def grad_rest(blocks, totals, logits, dense, logprob, weight):
    width, tokens = logits.shape
    count = blocks.shape[0]
    half = weight.shape[1] // (4 * count)
    whole = pl.BlockSpec((width, tokens), lambda k, b: (0, 0))
    return call(
        grad_rest_kernel, "grad_rest",
        [array((width, tokens), bf16), array((tokens, width), bf16), array((count, 2, tokens, half), bf16)],
        totals, logits, dense, logprob, weight,
        grid=(count,), prefetch=(blocks,),
        ins=[
            pl.BlockSpec((totals.shape[0], tokens), lambda k, b: (0, 0)),
            whole,
            whole,
            pl.BlockSpec(logprob.shape, lambda k, b: (0, 0)),
            pl.BlockSpec((width, 2 * half), lambda k, b: (0, b[k])),
        ],
        outs=[
            whole,
            pl.BlockSpec((tokens, width), lambda k, b: (0, 0)),
            pl.BlockSpec((1, 2, tokens, half), lambda k, b: (k, 0, 0, 0)),
        ],
        scratch=[pltpu.VMEM((-(-width // 128) * 128, 128), f32)],
        flops=4 * count * tokens * half * width, size=12 * 2**20,
    )


def grad_own_kernel(block_ref, at_ref, turned_ref, weight_ref, other_ref, *refs):
    by_y, by_x, keep_ref = refs[:4], refs[4:8], refs[8]
    x, y = at_ref[0], at_ref[1]
    step = pl.program_id(0)
    out = dot(turned_ref[...], weight_ref[...])
    half = out.shape[1] // 2
    first = (out[:, :half] + other_ref[0, 0].astype(f32)).astype(bf16)
    for j in range(4):

        @pl.when(step == j)
        def _():
            by_y[j][...] = first

    second = (out[:, half:] + other_ref[0, 1].astype(f32)).astype(bf16)
    rows = keep_ref.shape[1]
    for k in range(4):
        keep_ref[k] = second[k * rows : (k + 1) * rows]
    for k in range(4):
        by_x[k][(y + step) % 4] = keep_ref[(x + k) % 4]


def grad_own(blocks, at, turned, weight, other):
    count, _, tokens, half = other.shape
    width = weight.shape[0]
    rows = tokens // NX
    piece, parts = pl.BlockSpec((tokens, half), lambda k, b, a: (0, 0)), pl.BlockSpec((NY, rows, half), lambda k, b, a: (0, 0, 0))
    return call(
        grad_own_kernel, "grad_own",
        [array((tokens, half), bf16)] * 4 + [array((NY, rows, half), bf16)] * 4,
        turned, weight, other,
        grid=(count,), prefetch=(blocks, at),
        ins=[
            pl.BlockSpec((tokens, width), lambda k, b, a: (0, 0)),
            pl.BlockSpec((width, 2 * half), lambda k, b, a: (0, b[k])),
            pl.BlockSpec((1, 2, tokens, half), lambda k, b, a: ((a[1] + k) % NY, 0, 0, 0)),
        ],
        outs=[piece] * 4 + [parts] * 4,
        scratch=[pltpu.VMEM((NX, rows, half), bf16)],
        flops=4 * count * tokens * half * width, size=12 * 2**20,
    )


def sum_kernel(at_ref, *refs):
    x, y = at_ref[0], at_ref[1]
    by_y, by_x, to_x, to_y, (keep_ref,) = refs[:4], refs[4:8], refs[8:12], refs[12:16], refs[16:]
    count, rows = by_x[0].shape[:2]
    for i in range(count):
        part = pl.ds(i * rows, rows)
        keep_ref[0, i] = sum(r[part, :].astype(f32) for r in by_y).astype(bf16)
        keep_ref[1, i] = sum(r[i].astype(f32) for r in by_x).astype(bf16)
    for k in range(4):
        to_x[k][...] = keep_ref[0, (x + k) % 4]
        to_y[k][...] = keep_ref[1, (y + k) % 4]


def spread_kernel(*refs):
    by_x, by_y, (spread_ref, target_ref, out_ref) = refs[:4], refs[4:8], refs[8:]
    both = jnp.concatenate(
        [sum(r[...].astype(f32) for r in by_x).astype(bf16), sum(r[...].astype(f32) for r in by_y).astype(bf16)], axis=1
    )
    turns, share = out_ref.shape[1] - 1, out_ref.shape[2]
    for z in range(spread_ref.shape[0]):
        rows = dot(spread_ref[z], both).astype(bf16)
        for k in range(NX):
            out_ref[z * NX + k, :turns, :] = rows[k * turns : (k + 1) * turns]
    rest = target_ref[...]
    step = rest.shape[2]
    for i in range(share // step):
        term = rest.astype(bf16)
        out_ref[:, turns:, i * step : (i + 1) * step] = term if i < 3 else jnp.zeros(term.shape, bf16)
        rest = rest - term.astype(f32)


def unsort_kernel(at_ref, count_ref, got_ref, rows_ref, gain_ref, u_ref, dots_ref, target_ref, sum_ref):
    offset, _ = own_slots(at_ref, count_ref)
    turns, share = sum_ref.shape[1:]
    lines = got_ref.shape[0] // NX
    target = jnp.zeros((1, share), f32)
    for k in range(NX):
        total = got_ref[k].astype(f32)
        for z in range(1, lines):
            total += got_ref[z * NX + k].astype(f32)
        sum_ref[k] = total[:turns]
        target += total[turns:]
    step = target_ref.shape[1]
    target_ref[...] = target[:, :step] + (target[:, step : 2 * step] + target[:, 2 * step : 3 * step])
    part = pl.ds(pl.multiple_of(at_ref[3] * share, share), share)
    for i in range(NX):
        for m in range(turns):
            u_ref[NX * m + i : NX * m + i + 1, :] = sum_ref[(offset + i) & (NX - 1), m : m + 1, :] * gain_ref[:, part]
    dots = jnp.sum(u_ref[...] * rows_ref[:, part].astype(f32), axis=1, keepdims=True)
    dots_ref[...] = jnp.broadcast_to(dots, dots_ref.shape)


def finish_kernel(at_ref, count_ref, *refs):
    parts, (u_ref, inv_ref, rows_ref, out_ref) = refs[:4], refs[4:]
    _, count = own_slots(at_ref, count_ref)
    dots = sum(r[:, :1] for r in parts)
    inv_rms = inv_ref[:, :1]
    share = out_ref.shape[1]
    part = pl.ds(pl.multiple_of(at_ref[3] * share, share), share)
    grad = (u_ref[...] - rows_ref[:, part].astype(f32) * (inv_rms * inv_rms * dots / rows_ref.shape[1])) * inv_rms
    live = lax.broadcasted_iota(jnp.int32, grad.shape, 0) < count
    out_ref[...] = jnp.where(live, grad, 0.0).astype(bf16)


def weight_grad_kernel(block_ref, own_ref, rest_ref, grad_ref, out_ref):
    def write(rows_ref):
        half = rows_ref.shape[3]
        for h in range(2):
            out_ref[:, h * half : (h + 1) * half] = dot(grad_ref[...], rows_ref[0, h]).astype(bf16)

    count = pl.num_programs(0) // 2

    @pl.when(pl.program_id(0) < count)
    def _():
        write(own_ref)

    @pl.when(pl.program_id(0) >= count)
    def _():
        write(rest_ref)


def weight_grad(blocks, own, rest, grad):
    count, _, tokens, half = own.shape
    width = grad.shape[0]
    return call(
        weight_grad_kernel, "weight_grad", array((width, 4 * count * half), bf16), own, rest, grad,
        grid=(2 * count,), prefetch=(blocks,),
        ins=[
            pl.BlockSpec((1, 2, tokens, half), lambda k, b: (jnp.minimum(k, count - 1), 0, 0, 0)),
            pl.BlockSpec((1, 2, tokens, half), lambda k, b: (jnp.maximum(k - count, 0), 0, 0, 0)),
            pl.BlockSpec((width, tokens), lambda k, b: (0, 0)),
        ],
        outs=pl.BlockSpec((width, 2 * half), lambda k, b: (0, b[k])),
        flops=8 * count * tokens * half * width, size=16 * 2**20,
    )


def exchange(x, axis):
    return lax.all_to_all(x, axis, 0, 0, tiled=True)


def along_x(x, k):
    return lax.ppermute(x, "seq", [(i, i // NX * NX + (i + k) % NX) for i in range(GROUPS)])


def along_y(x, k):
    return lax.ppermute(x, "vocab", [(i, (i + 2 * k) % (2 * NY)) for i in range(2 * NY)])


def from_ahead(x, move):
    got = {k: move(x, -k) for k in STEPS}
    return [x, got[1], got[2], got[3]]


def to_ahead(pieces, move):
    return [pieces[0], *(move(pieces[k], k) for k in STEPS)]


def merge(stats):
    tokens = stats[0].shape[1] // 2
    totals = [s[:, :tokens] for s in stats]
    peak = totals[0]
    for t in totals[1:]:
        peak = jnp.maximum(peak, t)
    total = peak + jnp.log(sum(jnp.exp(t - peak) for t in totals))
    return jnp.concatenate([total, sum(s[:, tokens:] for s in stats)], axis=1)


def per_device(rollout, group_count, final_gain, head_weight, teacher_index, teacher_logprob):
    slots, features = rollout.shape
    tokens, entries = teacher_index.shape
    width = head_weight.shape[1]
    weight = head_weight.T
    parts = 2 * NY
    share = features // parts
    half = share // 2
    class_rows = tokens // NX
    turns = slots // NX
    pack_rows = tokens // GROUPS
    seq = lax.axis_index("seq")
    own_z, own_x = seq // NX, seq % NX
    vocab = lax.axis_index("vocab")
    own_y, core = vocab // 2, vocab % 2
    at = jnp.stack([own_x, own_y, seq, vocab]).astype(jnp.int32)

    of_class, inv_rms = call(
        sort_kernel, "sort_rows", [array((GROUPS, turns, share), bf16), array((slots, 128), f32)],
        rollout, final_gain[None, :], prefetch=(at, group_count), size=2**19,
    )
    of_class = exchange(of_class, "seq")

    group_ids = jnp.arange(GROUPS, dtype=jnp.int32)
    before = group_ids[None, :] < group_ids[:, None]
    offsets = jnp.sum(jnp.where(before, group_count[None, :], 0), axis=1)
    turn_ids = jnp.arange(turns, dtype=jnp.int32)
    row_in_group = (own_x - offsets[:, None]) % NX + NX * turn_ids[None, :]
    rank = offsets[:, None] + row_in_group
    place = jnp.where(row_in_group < group_count[:, None], rank % GROUPS // NX * pack_rows + rank // GROUPS, class_rows)
    place_ids = jnp.arange(class_rows, dtype=jnp.int32)
    spread = (place.reshape(NZ, slots, 1) == place_ids[None, None, :]).astype(bf16)
    dense_rows = lax.dot_general(
        spread.reshape(-1, class_rows), of_class.reshape(-1, share), (((0,), (0,)), ((), ())), preferred_element_type=f32
    ).astype(bf16)

    by_x = from_ahead(dense_rows[:, :half], along_x)
    by_y = from_ahead(dense_rows[:, half:], along_y)
    all_x, all_y = call(
        place_kernel, "place", [array((4, class_rows, half), bf16)] * 2, *by_x, *by_y, prefetch=(at,), ins=None, size=2**21
    )
    by_y = from_ahead(all_x.reshape(tokens, half), along_y)
    by_x = from_ahead(all_y, along_x)

    def class_order(a):
        return a.reshape(NZ, NX, pack_rows, entries).transpose(1, 0, 2, 3).reshape(tokens, entries).T

    index = class_order(teacher_index)
    logprob = class_order(teacher_logprob)
    first_column = (seq * parts + vocab) * width
    dense = teacher_columns(first_column, index, logprob, width)
    by_y, by_x, dense = lax.optimization_barrier((by_y, by_x, dense))
    own_rows = call(
        gather_kernel, "gather_rows", array((NY, 2, tokens, half), bf16), *by_y, *by_x,
        prefetch=(at,), size=2**23,
    )
    rest_rows = lax.ppermute(own_rows, "vocab", OTHER_CORE)

    y_ids = jnp.arange(NY, dtype=jnp.int32)
    own_blocks = 2 * y_ids + core
    rest_blocks = 2 * y_ids + 1 - core
    logits_own = logits_call(own_blocks, own_rows, weight)
    logits, stats = logits_call(rest_blocks, rest_rows, weight, logits_own, dense)
    stats = merge([stats, lax.ppermute(stats, "vocab", OTHER_CORE)])
    stats = merge(from_ahead(stats, along_y))
    totals = exchange(jnp.broadcast_to(stats[:, :tokens], (GROUPS, tokens)), "seq")

    grad, turned, rest_grad = grad_rest(rest_blocks, totals, logits, dense, logprob, weight)
    other_grad = lax.ppermute(rest_grad, "vocab", OTHER_CORE)
    ahead_blocks = 2 * ((own_y + y_ids) % NY) + core
    pieces = grad_own(ahead_blocks, at, turned, weight, other_grad)
    by_y, by_x = to_ahead(pieces[:4], along_y), to_ahead(pieces[4:], along_x)
    weight_t = weight_grad(jnp.concatenate([own_blocks, rest_blocks]), own_rows, rest_rows, grad)

    own_tokens = own_x * class_rows + own_z * pack_rows
    totals = lax.dynamic_slice_in_dim(totals, own_tokens, pack_rows, 1)
    own_logprob = lax.dynamic_slice_in_dim(logprob, own_tokens, pack_rows, 1)
    peak = jnp.max(totals, axis=0)
    log_total = peak + jnp.log(jnp.sum(jnp.exp(totals - peak), axis=0))
    prob = jnp.exp(own_logprob)
    kl = jnp.sum(prob * own_logprob, axis=0) + jnp.sum(prob, axis=0) * log_total
    target = stats[0, tokens:].reshape(NX, NZ, pack_rows).transpose(1, 0, 2).reshape(GROUPS, 1, pack_rows)
    target = jnp.pad(target, ((0, 0), (0, 0), (0, 128 - pack_rows)))

    by_y, by_x, weight_t, kl, target = lax.optimization_barrier((by_y, by_x, weight_t, kl, target))
    small = array((class_rows, half), bf16)
    pieces = call(
        sum_kernel, "add_pieces", [small] * 8, *by_y, *by_x, prefetch=(at,),
        ins=[pl.BlockSpec(memory_space=pltpu.VMEM)] * 8, outs=[pl.BlockSpec(memory_space=pltpu.VMEM)] * 8,
        scratch=[pltpu.VMEM((2, 4, class_rows, half), bf16)], size=2**22,
    )
    by_x, by_y = to_ahead(pieces[:4], along_x), to_ahead(pieces[4:], along_y)
    spread_grad = call(
        spread_kernel, "spread_rows", array((GROUPS, turns + 1, share), bf16), *by_x, *by_y, spread, target, size=2**20
    )
    got = exchange(spread_grad, "seq")
    u, dots, targets = call(
        unsort_kernel, "unsort_rows",
        [array((slots, share), f32), array((slots, 128), f32), array((1, 128), f32)],
        got, rollout, final_gain[None, :], prefetch=(at, group_count),
        scratch=[pltpu.VMEM((NX, turns, share), f32)], size=2**19,
    )
    kl = kl - targets[0, :pack_rows]
    dots = dots + lax.ppermute(dots, "vocab", OTHER_CORE)
    grad_rollout = call(
        finish_kernel, "finish", array((slots, share), bf16), *from_ahead(dots, along_y), u, inv_rms, rollout,
        prefetch=(at, group_count), size=2**19,
    )
    return (kl, weight_t.T, grad_rollout)


def solution(mesh):
    placed = (P("seq", None), P(), P(), P(None, ("seq", "vocab")), P(), P())
    return jax.shard_map(
        per_device,
        mesh=mesh,
        in_specs=placed,
        out_specs=(P("seq"), P(None, ("seq", "vocab")), P("seq", "vocab")),
        check_vma=False,
    )
```

time: 808 us -> 214 us (0.26)
  waiting for transfers between devices: 314 us -> 40.8 us
  other arithmetic: 268 us -> 2.7 us
  blocking collectives: 147 us -> 34.5 us
  Pallas kernels: 0 us -> 51.4 us
  starting transfers between devices: 21.4 us -> 66.9 us
  matrix products: 28.4 us -> 0.37 us
  between operations: 16.6 us -> 1.09 us
    unnamed x4 -> x1, other arithmetic: 258 us -> 0.01 us
    reduce_scatter x1 -> x0, waiting for transfers between devices: 233 us -> none  [per_device(): lax.psum_scatter(lax.dot_general(grad_logits, head_weight, (((1,), (1,)),...]
    psum x1 -> x0, blocking collectives: 74.5 us -> none  [per_device(): lax.psum((local_total, target_part), ('seq', 'vocab'))]
    pmax x1 -> x0, blocking collectives: 72.9 us -> none  [per_device(): row_peak = lax.pmax(local_peak, ('seq', 'vocab'))]
    psum x1 -> x0, waiting for transfers between devices: 63 us -> none  [per_device(): whole_rows = lax.psum(partial_rows, 'vocab')]
    ppermute x0 -> x34, starting transfers between devices: none -> 55.6 us  [the longest x18 36.1 us: along_y(): lax.ppermute(x, 'vocab', [(i, (i + 2 * k) % (2 * NY)) for i in range(2 *...]
    pallas_call x0 -> x13, Pallas kernels: none -> 51.4 us  [call(): pl.pallas_call(body, grid_spec=pltpu.PrefetchScalarGridSpec(num_scalar_pr...]
    all_to_all x0 -> x2, blocking collectives: none -> 34.5 us  [exchange(): return lax.all_to_all(x, axis, 0, 0, tiled=True)]
  transfers between devices with their start and end apart: 5 -> 35, of which waited for: 4 -> 15; matrix products, arithmetic and copies ran while one was open for 33% -> 2% of each run, Pallas kernels for 0% -> 12%
where the time goes in v2:
time: 214 us; the launch traced here: 212 us
  starting transfers between devices  66.9 us (31%)
  Pallas kernels  51.4 us (24%)
  waiting for transfers between devices  40.8 us (19%)
  blocking collectives  34.5 us (16%)
  local copies, waits for them, and re-layouts  14.4 us (7%)
  other arithmetic  2.7 us (1%)
    pallas_call x13, Pallas kernels, call(): pl.pallas_call(body, grid_spec=pltpu.PrefetchScalarGridSpec(num_scalar_pr...  51.4 us
    ppermute x18, starting transfers between devices, along_y(): lax.ppermute(x, 'vocab', [(i, (i + 2 * k) % (2 * NY)) for i in range(2 *...  36.1 us
    all_to_all x2, blocking collectives, exchange(): return lax.all_to_all(x, axis, 0, 0, tiled=True)  34.5 us
    ppermute x12, starting transfers between devices, along_x(): lax.ppermute(x, 'seq', [(i, i // NX * NX + (i + k) % NX) for i in range(G...  18.8 us
    ppermute x18, waiting for transfers between devices, along_y(): lax.ppermute(x, 'vocab', [(i, (i + 2 * k) % (2 * NY)) for i in range(2 *...  17.3 us
    all_to_all x1, waiting for transfers between devices, exchange(): return lax.all_to_all(x, axis, 0, 0, tiled=True)  15 us
    unnamed x57, local copies, waits for them, and re-layouts  11.9 us
    all_to_all x1, starting transfers between devices, exchange(): return lax.all_to_all(x, axis, 0, 0, tiled=True)  11.3 us
  transfers between devices with their start and end apart: 35, of which 15 were waited for; matrix products, arithmetic and copies ran while one was open for 2% of the time, Pallas kernels for 12%

profile of v2, /device:TPU:8, one launch (start us, length us, event | category | flops | bytes accessed | tf_op | source)
XLA Modules:
  0.0 212.2 jit_solution(15308583399472689556)
XLA Ops:
  3.1 1.8 sort_rows.1
  5.5 11.3 %all-to-all-start = ((bf16[32,9,512]{2,1,0:T(8,128)(2,1)}), bf16[32,9,512]{2,1,0:T(8,128)(2,1)S(1)}, u32[]{:S(2)}, u32[]{:S(2)}) async-start(bf16[32,9,512]{2,1,0:T(8,128)(2,1)} %get-tuple-element.51), calls=%async_computation | async-start | bytes 1048576 | tf_op jit(solution)/shard_map/all_to_all | solution.py:370
  19.5 15.0 %all-to-all-done = bf16[32,9,512]{2,1,0:T(8,128)(2,1)S(1)} async-done(((bf16[32,9,512]{2,1,0:T(8,128)(2,1)}), bf16[32,9,512]{2,1,0:T(8,128)(2,1)S(1)}, u32[]{:S(2)}, u32[]{:S(2)}) %all-to-all-start) | async-done | bytes 294944 | tf_op jit(solution)/shard_map/all_to_all | solution.py:370
  35.1 2.2 %collective-permute-start = (bf16[192,256]{1,0:T(8,128)(2,1)S(1)}, bf16[192,256]{1,0:T(8,128)(2,1)S(1)}, u32[]{:S(2)}, u32[]{:S(2)}) collective-permute-start(bf16[192,256]{1,0:T(8,128)(2,1)S(1)} %get-tuple-element.106.refs_0_), channel_id=1, source_target_pairs={{0,24},{8,0},{16,8},{24,16},{32,56},{40,32},{48,40},{56,48},{64,88... | collective-permute-start | bytes 294920 | tf_op jit(solution)/shard_map/ppermute | solution.py:374
  39.5 2.6 %collective-permute-start.4 = (bf16[192,256]{1,0:T(8,128)(2,1)S(1)}, bf16[192,256]{1,0:T(8,128)(2,1)S(1)}, u32[]{:S(2)}, u32[]{:S(2)}) collective-permute-start(bf16[192,256]{1,0:T(8,128)(2,1)S(1)} %get-tuple-element.105.refs_4_), channel_id=1, source_target_pairs={{0,4},{1,5},{2,6},{3,7},{4,0},{5,1},{6,2},{7,3},{8,12},{9,13},{10,... | collective-permute-start | bytes 294920 | tf_op jit(solution)/shard_map/ppermute | solution.py:378
  42.1 1.9 collective-permute-start.5
  47.4 3.0 %collective-permute-start.6 = (bf16[768,256]{1,0:T(8,128)(2,1)S(1)}, bf16[768,256]{1,0:T(8,128)(2,1)S(1)}, u32[]{:S(2)}, u32[]{:S(2)}) collective-permute-start(bf16[768,256]{1,0:T(8,128)(2,1)S(1)} %bitcast.42), channel_id=1, source_target_pairs={{0,6},{1,7},{2,0},{3,1},{4,2},{5,3},{6,4},{7,5},{8,14},{9,15},{10,... | collective-permute-start | bytes 1179656 | tf_op jit(solution)/shard_map/ppermute | solution.py:378
  52.4 2.4 %collective-permute-start.9 = (bf16[4,192,256]{2,1,0:T(8,128)(2,1)S(1)}, bf16[4,192,256]{2,1,0:T(8,128)(2,1)}, u32[]{:S(2)}, u32[]{:S(2)}) collective-permute-start(bf16[4,192,256]{2,1,0:T(8,128)(2,1)S(1)} %get-tuple-element.58.refs_4_), channel_id=1, source_target_pairs={{0,24},{8,0},{16,8},{24,16},{32,56},{40,32},{48,40},{56,48},{64,88... | collective-permute-start | bytes 1179656 | tf_op jit(solution)/shard_map/ppermute | solution.py:374
  56.2 3.2 %collective-permute-done.6.refs_1_ = bf16[768,256]{1,0:T(8,128)(2,1)S(1)} collective-permute-done((bf16[768,256]{1,0:T(8,128)(2,1)S(1)}, bf16[768,256]{1,0:T(8,128)(2,1)S(1)}, u32[]{:S(2)}, u32[]{:S(2)}) %collective-permute-start.6) | collective-permute-done | bytes 393248 | tf_op jit(solution)/shard_map/ppermute | solution.py:378
  63.3 9.3 %teacher_columns.1.dense_ref = f32[594,768]{1,0:T(8,128)S(1)} custom-call(s32[1]{0:T(128)} %bitcast.6.first_ref, s32[64,768]{1,0:T(8,128)S(1)} %bitcast.40, f32[64,768]{1,0:T(8,128)S(1)} %bitcast.38), custom_call_target="tpu_custom_call" | custom-call | flops 116785152 | bytes 1824768 | tf_op jit(solution)/shard_map/teacher_columns/pallas_call | solution.py:23
  75.3 3.7 %gather_rows.1.rows_ref.own_ref = bf16[4,2,768,256]{3,2,1,0:T(8,128)(2,1)} custom-call(s32[4]{0:T(128)S(1)} %pad_add_fusion.at_ref, bf16[768,256]{1,0:T(8,128)(2,1)S(1)} %bitcast.45, bf16[768,256]{1,0:T(8,128)(2,1)S(1)} %copy-done.4, bf16[768,256]{1,0:T(8,128)(2,1)S(1)} %copy-done.6, bf16[768,256]{1,0:T(8,128)(2,1)} %collective-permute-done.8.refs_3_, ...), custom_call_target="tpu_custom_call" | custom-call | bytes 8388608 | tf_op jit(solution)/shard_map/gather_rows/pallas_call | solution.py:23
  79.1 2.4 %copy-done = bf16[4096,594]{0,1:T(8,128)(2,1)S(1)} copy-done((bf16[4096,594]{0,1:T(8,128)(2,1)S(1)}, bf16[4096,594]{0,1:T(8,128)(2,1)}, u32[]{:S(2)}) %copy-start) | copy-done | bytes 4866072
  81.5 5.8 %logits_own.1.own_ref = f32[594,768]{1,0:T(8,128)S(1)} custom-call(s32[4]{0:T(128)S(1)} %fusion.22.block_ref, bf16[4,2,768,256]{3,2,1,0:T(8,128)(2,1)} %gather_rows.1.rows_ref.own_ref, bf16[594,4096]{1,0:T(8,128)(2,1)S(1)} %bitcast.32), custom_call_target="tpu_custom_call" | custom-call | flops 1868562432 | bytes 8388608 | tf_op jit(solution)/shard_map/logits_own/pallas_call | solution.py:23
  87.3 6.1 %logits_rest.1 = (f32[594,768]{1,0:T(8,128)S(1)}, f32[1,1536]{1,0:T(1,128)S(1)}) custom-call(s32[4]{0:T(128)S(1)} %add_subtract_fusion.block_ref, bf16[4,2,768,256]{3,2,1,0:T(8,128)(2,1)} %collective-permute-done.12.rows_ref.rest_ref, bf16[594,4096]{1,0:T(8,128)(2,1)S(1)} %bitcast.35, f32[594,768]{1,0:T(8,128)S(1)} %logits_own.1.own_ref, ...), custom_call_target="tpu_custom_call" | custom-call | flops 1868562432 | bytes 8388608 | tf_op jit(solution)/shard_map/logits_rest/pallas_call | solution.py:23
  96.1 3.1 %collective-permute-start.15 = (f32[1,1536]{1,0:T(1,128)S(1)}, f32[1,1536]{1,0:T(1,128)S(1)}, u32[]{:S(2)}, u32[]{:S(2)}) collective-permute-start(f32[1,1536]{1,0:T(1,128)S(1)} %pad_maximum_fusion), channel_id=1, source_target_pairs={{0,4},{1,5},{2,6},{3,7},{4,0},{5,1},{6,2},{7,3},{8,12},{9,13},{10,... | collective-permute-start | bytes 18440 | tf_op jit(solution)/shard_map/ppermute | solution.py:378
  99.2 1.9 collective-permute-start.14
  103.0 15.3 %all_to_all.18 = f32[32,1,768]{2,1,0:T(1,128)S(1)} all-to-all(f32[32,1,768]{2,1,0:T(1,128)S(1)} %broadcast_in_dim.40), channel_id=1, replica_groups=mesh['seq'=32,'vocab'=8] {'seq'}, dimensions={0} | all-to-all | bytes 196608 | tf_op jit(solution)/shard_map/all_to_all | solution.py:370
  118.3 4.6 %grad_rest.1 = (bf16[594,768]{1,0:T(8,128)(2,1)S(1)}, bf16[768,594]{1,0:T(8,128)(2,1)S(1)}, bf16[4,2,768,256]{3,2,1,0:T(8,128)(2,1)S(1)}) custom-call(s32[4]{0:T(128)S(1)} %add_subtract_fusion.block_ref, f32[32,768]{1,0:T(8,128)S(1)} %bitcast.41, f32[594,768]{1,0:T(8,128)S(1)} %get-tuple-element.64.logits_ref, f32[594,768]{1,0:T(8,128)S(1)} %teacher_columns.1.dense_ref, ...), custom_call_target="tpu_custom_call" | custom-call | flops 1868562432 | bytes 12582912 | tf_op jit(solution)/shard_map/grad_rest/pallas_call | solution.py:23
  123.1 5.6 %collective-permute-done.17.other_ref = bf16[4,2,768,256]{3,2,1,0:T(8,128)(2,1)S(1)} collective-permute-done((bf16[4,2,768,256]{3,2,1,0:T(8,128)(2,1)S(1)}, bf16[4,2,768,256]{3,2,1,0:T(8,128)(2,1)S(1)}, u32[]{:S(2)}, u32[]{:S(2)}) %collective-permute-start.17) | collective-permute-done | bytes 3145760 | tf_op jit(solution)/shard_map/ppermute | solution.py:468
  128.7 5.3 %grad_own.1 = (bf16[768,256]{1,0:T(8,128)(2,1)S(1)}, bf16[768,256]{1,0:T(8,128)(2,1)}, bf16[768,256]{1,0:T(8,128)(2,1)S(1)}, bf16[768,256]{1,0:T(8,128)(2,1)S(1)...) custom-call(s32[4]{0:T(128)S(1)} %fusion.20.block_ref, ...), custom_call_target="tpu_custom_call" | custom-call | flops 1868562432 | bytes 12582912 | tf_op jit(solution)/shard_map/grad_own/pallas_call | solution.py:23
  140.3 3.0 %collective-permute-start.22 = (bf16[4,192,256]{2,1,0:T(8,128)(2,1)S(1)}, bf16[4,192,256]{2,1,0:T(8,128)(2,1)S(1)}, u32[]{:S(2)}, u32[]{:S(2)}) collective-permute-start(bf16[4,192,256]{2,1,0:T(8,128)(2,1)S(1)} %get-tuple-element.73), channel_id=1, source_target_pairs={{0,24},{8,0},{16,8},{24,16},{32,56},{40,32},{48,40},{56,48},{64,88... | collective-permute-start | bytes 1179656 | tf_op jit(solution)/shard_map/ppermute | solution.py:374
  143.3 3.6 %collective-permute-done.18.refs_1_ = bf16[768,256]{1,0:T(8,128)(2,1)S(1)} collective-permute-done((bf16[768,256]{1,0:T(8,128)(2,1)}, bf16[768,256]{1,0:T(8,128)(2,1)S(1)}, u32[]{:S(2)}, u32[]{:S(2)}) %collective-permute-start.18) | collective-permute-done | bytes 393248 | tf_op jit(solution)/shard_map/ppermute | solution.py:378
  149.5 10.3 %weight_grad.1 = bf16[594,4096]{1,0:T(8,128)(2,1)} custom-call(s32[8]{0:T(128)S(1)} %pad_add_fusion.1.block_ref, bf16[4,2,768,256]{3,2,1,0:T(8,128)(2,1)} %gather_rows.1.rows_ref.own_ref, bf16[4,2,768,256]{3,2,1,0:T(8,128)(2,1)} %collective-permute-done.12.rows_ref.rest_ref, bf16[594,768]{1,0:T(8,128)(2,1)S(1)} %copy-done.14), custom_call_target="tpu_custom_call" | custom-call | flops 3737124864 | bytes 16777216 | tf_op jit(solution)/shard_map/weight_grad/pallas_call | solution.py:23
  162.1 2.5 %collective-permute-start.25 = (bf16[192,256]{1,0:T(8,128)(2,1)S(1)}, bf16[192,256]{1,0:T(8,128)(2,1)S(1)}, u32[]{:S(2)}, u32[]{:S(2)}) collective-permute-start(bf16[192,256]{1,0:T(8,128)(2,1)S(1)} %get-tuple-element.87), channel_id=1, source_target_pairs={{0,24},{8,0},{16,8},{24,16},{32,56},{40,32},{48,40},{56,48},{64,88... | collective-permute-start | bytes 294920 | tf_op jit(solution)/shard_map/ppermute | solution.py:374
  165.8 2.1 collective-permute-start.27
  167.9 6.5 %collective-permute-start.28 = (bf16[192,256]{1,0:T(8,128)(2,1)S(1)}, bf16[192,256]{1,0:T(8,128)(2,1)S(1)}, u32[]{:S(2)}, u32[]{:S(2)}) collective-permute-start(bf16[192,256]{1,0:T(8,128)(2,1)S(1)} %get-tuple-element.91), channel_id=1, source_target_pairs={{0,6},{1,7},{2,0},{3,1},{4,2},{5,3},{6,4},{7,5},{8,14},{9,15},{10,... | collective-permute-start | bytes 294920 | tf_op jit(solution)/shard_map/ppermute | solution.py:378
  174.3 2.1 collective-permute-start.29
  176.9 3.5 %collective-permute-done.29.refs_7_ = bf16[192,256]{1,0:T(8,128)(2,1)S(1)} collective-permute-done((bf16[192,256]{1,0:T(8,128)(2,1)S(1)}, bf16[192,256]{1,0:T(8,128)(2,1)S(1)}, u32[]{:S(2)}, u32[]{:S(2)}) %collective-permute-start.29) | collective-permute-done | bytes 98336 | tf_op jit(solution)/shard_map/ppermute | solution.py:378
  181.0 19.2 %all_to_all.19.got_ref = bf16[32,10,512]{2,1,0:T(8,128)(2,1)S(1)} all-to-all(bf16[32,10,512]{2,1,0:T(8,128)(2,1)S(1)} %spread_rows.1), channel_id=1, replica_groups=mesh['seq'=32,'vocab'=8] {'seq'}, dimensions={0} | all-to-all | bytes 655360 | tf_op jit(solution)/shard_map/all_to_all | solution.py:370
  202.4 3.2 %collective-permute-start.31 = (f32[36,128]{1,0:T(8,128)S(1)}, f32[36,128]{1,0:T(8,128)S(1)}, u32[]{:S(2)}, u32[]{:S(2)}) collective-permute-start(f32[36,128]{1,0:T(8,128)S(1)} %add.233.refs_0_), channel_id=1, source_target_pairs={{0,6},{1,7},{2,0},{3,1},{4,2},{5,3},{6,4},{7,5},{8,14},{9,15},{10,... | collective-permute-start | bytes 55304 | tf_op jit(solution)/shard_map/ppermute | solution.py:378
  205.6 2.2 %collective-permute-start.33 = (f32[36,128]{1,0:T(8,128)S(1)}, f32[36,128]{1,0:T(8,128)S(1)}, u32[]{:S(2)}, u32[]{:S(2)}) collective-permute-start(f32[36,128]{1,0:T(8,128)S(1)} %add.233.refs_0_), channel_id=1, source_target_pairs={{0,2},{1,3},{2,4},{3,5},{4,6},{5,7},{6,0},{7,1},{8,10},{9,11},{10,... | collective-permute-start | bytes 55304 | tf_op jit(solution)/shard_map/ppermute | solution.py:378
  208.4 2.5 %collective-permute-done.32.refs_2_ = f32[36,128]{1,0:T(8,128)S(1)} collective-permute-done((f32[36,128]{1,0:T(8,128)S(1)}, f32[36,128]{1,0:T(8,128)S(1)}, u32[]{:S(2)}, u32[]{:S(2)}) %collective-permute-start.32) | collective-permute-done | bytes 18464 | tf_op jit(solution)/shard_map/ppermute | solution.py:378
  (157 shorter events, 43.7 us)
Async XLA Ops:
  5.5 29.0 %all-to-all-start = ((bf16[32,9,512]{2,1,0:T(8,128)(2,1)}), bf16[32,9,512]{2,1,0:T(8,128)(2,1)S(1)}, u32[]{:S(2)}, u32[]{:S(2)}) async-start(bf16[32,9,512]{2,1,0:T(8,128)(2,1)} %get-tuple-element.51), calls=%async_computation | async-start | bytes 1048576 | tf_op jit(solution)/shard_map/all_to_all | solution.py:370
  35.1 7.0 %collective-permute-start = (bf16[192,256]{1,0:T(8,128)(2,1)S(1)}, bf16[192,256]{1,0:T(8,128)(2,1)S(1)}, u32[]{:S(2)}, u32[]{:S(2)}) collective-permute-start(bf16[192,256]{1,0:T(8,128)(2,1)S(1)} %get-tuple-element.106.refs_0_), channel_id=1, source_target_pairs={{0,24},{8,0},{16,8},{24,16},{32,56},{40,32},{48,40},{56,48},{64,88... | collective-permute-start | bytes 294920 | tf_op jit(solution)/shard_map/ppermute | solution.py:374
  37.3 6.6 %collective-permute-start.1 = (bf16[192,256]{1,0:T(8,128)(2,1)S(1)}, bf16[192,256]{1,0:T(8,128)(2,1)S(1)}, u32[]{:S(2)}, u32[]{:S(2)}) collective-permute-start(bf16[192,256]{1,0:T(8,128)(2,1)S(1)} %get-tuple-element.106.refs_0_), channel_id=1, source_target_pairs={{0,16},{8,24},{16,0},{24,8},{32,48},{40,56},{48,32},{56,40},{64,80... | collective-permute-start | bytes 294920 | tf_op jit(solution)/shard_map/ppermute | solution.py:374
  38.2 6.3 %collective-permute-start.2 = (bf16[192,256]{1,0:T(8,128)(2,1)S(1)}, bf16[192,256]{1,0:T(8,128)(2,1)S(1)}, u32[]{:S(2)}, u32[]{:S(2)}) collective-permute-start(bf16[192,256]{1,0:T(8,128)(2,1)S(1)} %get-tuple-element.106.refs_0_), channel_id=1, source_target_pairs={{0,8},{8,16},{16,24},{24,0},{32,40},{40,48},{48,56},{56,32},{64,72... | collective-permute-start | bytes 294920 | tf_op jit(solution)/shard_map/ppermute | solution.py:374
  39.0 5.5 %collective-permute-start.3 = (bf16[192,256]{1,0:T(8,128)(2,1)S(1)}, bf16[192,256]{1,0:T(8,128)(2,1)S(1)}, u32[]{:S(2)}, u32[]{:S(2)}) collective-permute-start(bf16[192,256]{1,0:T(8,128)(2,1)S(1)} %get-tuple-element.105.refs_4_), channel_id=1, source_target_pairs={{0,6},{1,7},{2,0},{3,1},{4,2},{5,3},{6,4},{7,5},{8,14},{9,15},{10,... | collective-permute-start | bytes 294920 | tf_op jit(solution)/shard_map/ppermute | solution.py:378
  39.5 6.2 %collective-permute-start.4 = (bf16[192,256]{1,0:T(8,128)(2,1)S(1)}, bf16[192,256]{1,0:T(8,128)(2,1)S(1)}, u32[]{:S(2)}, u32[]{:S(2)}) collective-permute-start(bf16[192,256]{1,0:T(8,128)(2,1)S(1)} %get-tuple-element.105.refs_4_), channel_id=1, source_target_pairs={{0,4},{1,5},{2,6},{3,7},{4,0},{5,1},{6,2},{7,3},{8,12},{9,13},{10,... | collective-permute-start | bytes 294920 | tf_op jit(solution)/shard_map/ppermute | solution.py:378
  42.1 4.7 %collective-permute-start.5 = (bf16[192,256]{1,0:T(8,128)(2,1)S(1)}, bf16[192,256]{1,0:T(8,128)(2,1)S(1)}, u32[]{:S(2)}, u32[]{:S(2)}) collective-permute-start(bf16[192,256]{1,0:T(8,128)(2,1)S(1)} %get-tuple-element.105.refs_4_), channel_id=1, source_target_pairs={{0,2},{1,3},{2,4},{3,5},{4,6},{5,7},{6,0},{7,1},{8,10},{9,11},{10,... | collective-permute-start | bytes 294920 | tf_op jit(solution)/shard_map/ppermute | solution.py:378
  47.4 12.1 %collective-permute-start.6 = (bf16[768,256]{1,0:T(8,128)(2,1)S(1)}, bf16[768,256]{1,0:T(8,128)(2,1)S(1)}, u32[]{:S(2)}, u32[]{:S(2)}) collective-permute-start(bf16[768,256]{1,0:T(8,128)(2,1)S(1)} %bitcast.42), channel_id=1, source_target_pairs={{0,6},{1,7},{2,0},{3,1},{4,2},{5,3},{6,4},{7,5},{8,14},{9,15},{10,... | collective-permute-start | bytes 1179656 | tf_op jit(solution)/shard_map/ppermute | solution.py:378
  50.4 22.2 %collective-permute-start.7 = (bf16[768,256]{1,0:T(8,128)(2,1)S(1)}, bf16[768,256]{1,0:T(8,128)(2,1)S(1)}, u32[]{:S(2)}, u32[]{:S(2)}) collective-permute-start(bf16[768,256]{1,0:T(8,128)(2,1)S(1)} %bitcast.43), channel_id=1, source_target_pairs={{0,4},{1,5},{2,6},{3,7},{4,0},{5,1},{6,2},{7,3},{8,12},{9,13},{10,... | collective-permute-start | bytes 1179656 | tf_op jit(solution)/shard_map/ppermute | solution.py:378
  50.7 22.6 %collective-permute-start.8 = (bf16[768,256]{1,0:T(8,128)(2,1)S(1)}, bf16[768,256]{1,0:T(8,128)(2,1)}, u32[]{:S(2)}, u32[]{:S(2)}) collective-permute-start(bf16[768,256]{1,0:T(8,128)(2,1)S(1)} %bitcast.44), channel_id=1, source_target_pairs={{0,2},{1,3},{2,4},{3,5},{4,6},{5,7},{6,0},{7,1},{8,10},{9,11},{10,... | collective-permute-start | bytes 1179656 | tf_op jit(solution)/shard_map/ppermute | solution.py:378
  52.4 20.9 %collective-permute-start.9 = (bf16[4,192,256]{2,1,0:T(8,128)(2,1)S(1)}, bf16[4,192,256]{2,1,0:T(8,128)(2,1)}, u32[]{:S(2)}, u32[]{:S(2)}) collective-permute-start(bf16[4,192,256]{2,1,0:T(8,128)(2,1)S(1)} %get-tuple-element.58.refs_4_), channel_id=1, source_target_pairs={{0,24},{8,0},{16,8},{24,16},{32,56},{40,32},{48,40},{56,48},{64,88... | collective-permute-start | bytes 1179656 | tf_op jit(solution)/shard_map/ppermute | solution.py:374
  54.8 18.6 %collective-permute-start.10 = (bf16[4,192,256]{2,1,0:T(8,128)(2,1)S(1)}, bf16[4,192,256]{2,1,0:T(8,128)(2,1)}, u32[]{:S(2)}, u32[]{:S(2)}) collective-permute-start(bf16[4,192,256]{2,1,0:T(8,128)(2,1)S(1)} %get-tuple-element.58.refs_4_), channel_id=1, source_target_pairs={{0,16},{8,24},{16,0},{24,8},{32,48},{40,56},{48,32},{56,40},{64,80... | collective-permute-start | bytes 1179656 | tf_op jit(solution)/shard_map/ppermute | solution.py:374
  60.2 13.1 %collective-permute-start.11 = (bf16[4,192,256]{2,1,0:T(8,128)(2,1)S(1)}, bf16[4,192,256]{2,1,0:T(8,128)(2,1)}, u32[]{:S(2)}, u32[]{:S(2)}) collective-permute-start(bf16[4,192,256]{2,1,0:T(8,128)(2,1)S(1)} %get-tuple-element.58.refs_4_), channel_id=1, source_target_pairs={{0,8},{8,16},{16,24},{24,0},{32,40},{40,48},{48,56},{56,32},{64,72... | collective-permute-start | bytes 1179656 | tf_op jit(solution)/shard_map/ppermute | solution.py:374
  79.1 8.2 %collective-permute-start.12 = (bf16[4,2,768,256]{3,2,1,0:T(8,128)(2,1)}, bf16[4,2,768,256]{3,2,1,0:T(8,128)(2,1)}, u32[]{:S(2)}, u32[]{:S(2)}) collective-permute-start(bf16[4,2,768,256]{3,2,1,0:T(8,128)(2,1)} %gather_rows.1.rows_ref.own_ref), channel_id=1, source_target_pairs={{0,1},{1,0},{2,3},{3,2},{4,5},{5,4},{6,7},{7,6},{8,9},{9,8},{10,11... | collective-permute-start | bytes 9437192 | tf_op jit(solution)/shard_map/ppermute | solution.py:456
  94.9 6.2 %collective-permute-start.16 = (f32[1,1536]{1,0:T(1,128)S(1)}, f32[1,1536]{1,0:T(1,128)S(1)}, u32[]{:S(2)}, u32[]{:S(2)}) collective-permute-start(f32[1,1536]{1,0:T(1,128)S(1)} %pad_maximum_fusion), channel_id=1, source_target_pairs={{0,2},{1,3},{2,4},{3,5},{4,6},{5,7},{6,0},{7,1},{8,10},{9,11},{10,... | collective-permute-start | bytes 18440 | tf_op jit(solution)/shard_map/ppermute | solution.py:378
  96.1 5.2 %collective-permute-start.15 = (f32[1,1536]{1,0:T(1,128)S(1)}, f32[1,1536]{1,0:T(1,128)S(1)}, u32[]{:S(2)}, u32[]{:S(2)}) collective-permute-start(f32[1,1536]{1,0:T(1,128)S(1)} %pad_maximum_fusion), channel_id=1, source_target_pairs={{0,4},{1,5},{2,6},{3,7},{4,0},{5,1},{6,2},{7,3},{8,12},{9,13},{10,... | collective-permute-start | bytes 18440 | tf_op jit(solution)/shard_map/ppermute | solution.py:378
  123.0 5.7 %collective-permute-start.17 = (bf16[4,2,768,256]{3,2,1,0:T(8,128)(2,1)S(1)}, bf16[4,2,768,256]{3,2,1,0:T(8,128)(2,1)S(1)}, u32[]{:S(2)}, u32[]{:S(2)}) collective-permute-start(bf16[4,2,768,256]{3,2,1,0:T(8,128)(2,1)S(1)} %get-tuple-element.66), channel_id=1, source_target_pairs={{0,1},{1,0},{2,3},{3,2},{4,5},{5,4},{6,7},{7,6},{8,9},{9,8},{10,11... | collective-permute-start | bytes 9437192 | tf_op jit(solution)/shard_map/ppermute | solution.py:468
  134.8 12.2 %collective-permute-start.18 = (bf16[768,256]{1,0:T(8,128)(2,1)}, bf16[768,256]{1,0:T(8,128)(2,1)S(1)}, u32[]{:S(2)}, u32[]{:S(2)}) collective-permute-start(bf16[768,256]{1,0:T(8,128)(2,1)} %get-tuple-element.68), channel_id=1, source_target_pairs={{0,2},{1,3},{2,4},{3,5},{4,6},{5,7},{6,0},{7,1},{8,10},{9,11},{10,... | collective-permute-start | bytes 1179656 | tf_op jit(solution)/shard_map/ppermute | solution.py:378
  136.8 22.9 %collective-permute-start.19 = (bf16[768,256]{1,0:T(8,128)(2,1)}, bf16[768,256]{1,0:T(8,128)(2,1)S(1)}, u32[]{:S(2)}, u32[]{:S(2)}) collective-permute-start(bf16[768,256]{1,0:T(8,128)(2,1)} %copy-done.15), channel_id=1, source_target_pairs={{0,6},{1,7},{2,0},{3,1},{4,2},{5,3},{6,4},{7,5},{8,14},{9,15},{10,... | collective-permute-start | bytes 1179656 | tf_op jit(solution)/shard_map/ppermute | solution.py:378
  138.3 21.5 %collective-permute-start.20 = (bf16[768,256]{1,0:T(8,128)(2,1)S(1)}, bf16[768,256]{1,0:T(8,128)(2,1)S(1)}, u32[]{:S(2)}, u32[]{:S(2)}) collective-permute-start(bf16[768,256]{1,0:T(8,128)(2,1)S(1)} %get-tuple-element.70), channel_id=1, source_target_pairs={{0,4},{1,5},{2,6},{3,7},{4,0},{5,1},{6,2},{7,3},{8,12},{9,13},{10,... | collective-permute-start | bytes 1179656 | tf_op jit(solution)/shard_map/ppermute | solution.py:378
  140.1 20.0 %collective-permute-start.21 = (bf16[4,192,256]{2,1,0:T(8,128)(2,1)S(1)}, bf16[4,192,256]{2,1,0:T(8,128)(2,1)S(1)}, u32[]{:S(2)}, u32[]{:S(2)}) collective-permute-start(bf16[4,192,256]{2,1,0:T(8,128)(2,1)S(1)} %get-tuple-element.72), channel_id=1, source_target_pairs={{0,8},{8,16},{16,24},{24,0},{32,40},{40,48},{48,56},{56,32},{64,72... | collective-permute-start | bytes 1179656 | tf_op jit(solution)/shard_map/ppermute | solution.py:374
  140.3 19.7 %collective-permute-start.22 = (bf16[4,192,256]{2,1,0:T(8,128)(2,1)S(1)}, bf16[4,192,256]{2,1,0:T(8,128)(2,1)S(1)}, u32[]{:S(2)}, u32[]{:S(2)}) collective-permute-start(bf16[4,192,256]{2,1,0:T(8,128)(2,1)S(1)} %get-tuple-element.73), channel_id=1, source_target_pairs={{0,24},{8,0},{16,8},{24,16},{32,56},{40,32},{48,40},{56,48},{64,88... | collective-permute-start | bytes 1179656 | tf_op jit(solution)/shard_map/ppermute | solution.py:374
  146.9 13.1 %collective-permute-start.23 = (bf16[4,192,256]{2,1,0:T(8,128)(2,1)S(1)}, bf16[4,192,256]{2,1,0:T(8,128)(2,1)S(1)}, u32[]{:S(2)}, u32[]{:S(2)}) collective-permute-start(bf16[4,192,256]{2,1,0:T(8,128)(2,1)S(1)} %get-tuple-element.74), channel_id=1, source_target_pairs={{0,16},{8,24},{16,0},{24,8},{32,48},{40,56},{48,32},{56,40},{64,80... | collective-permute-start | bytes 1179656 | tf_op jit(solution)/shard_map/ppermute | solution.py:374
  161.1 13.2 %collective-permute-start.24 = (bf16[192,256]{1,0:T(8,128)(2,1)S(1)}, bf16[192,256]{1,0:T(8,128)(2,1)S(1)}, u32[]{:S(2)}, u32[]{:S(2)}) collective-permute-start(bf16[192,256]{1,0:T(8,128)(2,1)S(1)} %get-tuple-element.86), channel_id=1, source_target_pairs={{0,8},{8,16},{16,24},{24,0},{32,40},{40,48},{48,56},{56,32},{64,72... | collective-permute-start | bytes 294920 | tf_op jit(solution)/shard_map/ppermute | solution.py:374
  162.1 14.5 %collective-permute-start.25 = (bf16[192,256]{1,0:T(8,128)(2,1)S(1)}, bf16[192,256]{1,0:T(8,128)(2,1)S(1)}, u32[]{:S(2)}, u32[]{:S(2)}) collective-permute-start(bf16[192,256]{1,0:T(8,128)(2,1)S(1)} %get-tuple-element.87), channel_id=1, source_target_pairs={{0,24},{8,0},{16,8},{24,16},{32,56},{40,32},{48,40},{56,48},{64,88... | collective-permute-start | bytes 294920 | tf_op jit(solution)/shard_map/ppermute | solution.py:374
  164.5 12.0 %collective-permute-start.26 = (bf16[192,256]{1,0:T(8,128)(2,1)S(1)}, bf16[192,256]{1,0:T(8,128)(2,1)S(1)}, u32[]{:S(2)}, u32[]{:S(2)}) collective-permute-start(bf16[192,256]{1,0:T(8,128)(2,1)S(1)} %get-tuple-element.88), channel_id=1, source_target_pairs={{0,16},{8,24},{16,0},{24,8},{32,48},{40,56},{48,32},{56,40},{64,80... | collective-permute-start | bytes 294920 | tf_op jit(solution)/shard_map/ppermute | solution.py:374
  165.8 11.1 %collective-permute-start.27 = (bf16[192,256]{1,0:T(8,128)(2,1)S(1)}, bf16[192,256]{1,0:T(8,128)(2,1)S(1)}, u32[]{:S(2)}, u32[]{:S(2)}) collective-permute-start(bf16[192,256]{1,0:T(8,128)(2,1)S(1)} %get-tuple-element.90), channel_id=1, source_target_pairs={{0,2},{1,3},{2,4},{3,5},{4,6},{5,7},{6,0},{7,1},{8,10},{9,11},{10,... | collective-permute-start | bytes 294920 | tf_op jit(solution)/shard_map/ppermute | solution.py:378
  167.9 9.1 %collective-permute-start.28 = (bf16[192,256]{1,0:T(8,128)(2,1)S(1)}, bf16[192,256]{1,0:T(8,128)(2,1)S(1)}, u32[]{:S(2)}, u32[]{:S(2)}) collective-permute-start(bf16[192,256]{1,0:T(8,128)(2,1)S(1)} %get-tuple-element.91), channel_id=1, source_target_pairs={{0,6},{1,7},{2,0},{3,1},{4,2},{5,3},{6,4},{7,5},{8,14},{9,15},{10,... | collective-permute-start | bytes 294920 | tf_op jit(solution)/shard_map/ppermute | solution.py:378
  174.3 6.1 %collective-permute-start.29 = (bf16[192,256]{1,0:T(8,128)(2,1)S(1)}, bf16[192,256]{1,0:T(8,128)(2,1)S(1)}, u32[]{:S(2)}, u32[]{:S(2)}) collective-permute-start(bf16[192,256]{1,0:T(8,128)(2,1)S(1)} %get-tuple-element.92), channel_id=1, source_target_pairs={{0,4},{1,5},{2,6},{3,7},{4,0},{5,1},{6,2},{7,3},{8,12},{9,13},{10,... | collective-permute-start | bytes 294920 | tf_op jit(solution)/shard_map/ppermute | solution.py:378
  202.4 6.0 %collective-permute-start.31 = (f32[36,128]{1,0:T(8,128)S(1)}, f32[36,128]{1,0:T(8,128)S(1)}, u32[]{:S(2)}, u32[]{:S(2)}) collective-permute-start(f32[36,128]{1,0:T(8,128)S(1)} %add.233.refs_0_), channel_id=1, source_target_pairs={{0,6},{1,7},{2,0},{3,1},{4,2},{5,3},{6,4},{7,5},{8,14},{9,15},{10,... | collective-permute-start | bytes 55304 | tf_op jit(solution)/shard_map/ppermute | solution.py:378
  205.6 5.3 %collective-permute-start.32 = (f32[36,128]{1,0:T(8,128)S(1)}, f32[36,128]{1,0:T(8,128)S(1)}, u32[]{:S(2)}, u32[]{:S(2)}) collective-permute-start(f32[36,128]{1,0:T(8,128)S(1)} %add.233.refs_0_), channel_id=1, source_target_pairs={{0,4},{1,5},{2,6},{3,7},{4,0},{5,1},{6,2},{7,3},{8,12},{9,13},{10,... | collective-permute-start | bytes 55304 | tf_op jit(solution)/shard_map/ppermute | solution.py:378
  205.6 5.3 %collective-permute-start.33 = (f32[36,128]{1,0:T(8,128)S(1)}, f32[36,128]{1,0:T(8,128)S(1)}, u32[]{:S(2)}, u32[]{:S(2)}) collective-permute-start(f32[36,128]{1,0:T(8,128)S(1)} %add.233.refs_0_), channel_id=1, source_target_pairs={{0,2},{1,3},{2,4},{3,5},{4,6},{5,7},{6,0},{7,1},{8,10},{9,11},{10,... | collective-permute-start | bytes 55304 | tf_op jit(solution)/shard_map/ppermute | solution.py:378
  (30 other events, 359.6 us)

commit v3 on v0

v3 whole, which is shorter than its diff:
```python
import functools

import jax
import jax.numpy as jnp
from jax import lax
from jax.experimental import pallas as pl
from jax.experimental.pallas import tpu as pltpu
from jax.sharding import PartitionSpec as P

norm_eps = 1e-06
loss_scale = 16.0
f32, bf16 = jnp.float32, jnp.bfloat16

NX, NY, NZ = 4, 4, 8
GROUPS = NX * NZ
Y_LINES = [[y * 2 + core for y in range(NY)] for core in range(2)]
OTHER_CORE = [(i, i ^ 1) for i in range(2 * NY)]
STEPS = (1, 3, 2)
VMEM = 24 * 2**20


def call(body, name, out, *operands, grid=(), prefetch=(), ins=None, outs=None, scratch=(), flops=0, size=0):
    whole = pl.BlockSpec(memory_space=pltpu.VMEM)
    if ins is None:
        ins, outs = [whole] * len(operands), jax.tree.map(lambda _: whole, out)
    return pl.pallas_call(
        body,
        grid_spec=pltpu.PrefetchScalarGridSpec(
            num_scalar_prefetch=len(prefetch), grid=grid, in_specs=ins, out_specs=outs, scratch_shapes=scratch
        ),
        out_shape=out,
        cost_estimate=pl.CostEstimate(flops=flops, bytes_accessed=size, transcendentals=0),
        compiler_params=pltpu.CompilerParams(vmem_limit_bytes=VMEM),
        name=name,
    )(*prefetch, *operands)


def array(shape, dtype):
    return jax.ShapeDtypeStruct(shape, dtype)


def dot(a, b, over_a=1, over_b=0):
    return lax.dot_general(a, b, (((over_a,), (over_b,)), ((), ())), preferred_element_type=f32)


def own_slots(at_ref):
    seq = at_ref[2]
    offset = lax.fori_loop(0, GROUPS, lambda g, o: o + jnp.where(g < seq, at_ref[4 + g], 0), jnp.int32(0))
    return offset, at_ref[4 + seq]


def inverse_rms(rows_ref, step):
    slots, features = rows_ref.shape
    square = jnp.zeros((slots, step), f32)
    for i in range(0, features, step):
        values = rows_ref[:, i : i + step].astype(f32)
        square += values * values
    return lax.rsqrt(jnp.sum(square, axis=1, keepdims=True) / features + norm_eps)


def sort_kernel(at_ref, rows_ref, gain_ref, out_ref):
    vocab = at_ref[3]
    slots, features = rows_ref.shape
    turns, share = out_ref.shape[1:]
    offset, count = own_slots(at_ref)
    inv_rms = inverse_rms(rows_ref, share)
    part = pl.ds(pl.multiple_of(vocab * share, share), share)
    normed = (rows_ref[:, part].astype(f32) * inv_rms * gain_ref[:, part]).astype(bf16)
    to = lax.broadcasted_iota(jnp.int32, (slots, slots), 0)
    source = lax.broadcasted_iota(jnp.int32, (slots, slots), 1)
    kind = sum((to >= i * turns).astype(jnp.int32) for i in range(1, NX))
    row = ((kind - offset) & (NX - 1)) + NX * (to - kind * turns)
    pick = jnp.where((row == source) & (row < count), 1.0, 0.0).astype(bf16)
    by_class = dot(pick, normed).astype(bf16)
    for g in range(out_ref.shape[0]):
        k = g % NX
        out_ref[g] = by_class[k * turns : (k + 1) * turns]


def teacher_kernel(first_ref, index_ref, logprob_ref, dense_ref):
    local = index_ref[...] - first_ref[0]
    prob = jnp.exp(logprob_ref[...])
    width, tokens = dense_ref.shape
    step = 200
    for start in range(0, width, step):
        size = min(step, width - start)
        ids = lax.broadcasted_iota(jnp.int32, (size, tokens), 0) + start
        dense = jnp.zeros((size, tokens), f32)
        for j in range(local.shape[0]):
            dense = jnp.where(local[j : j + 1, :] == ids, prob[j : j + 1, :], dense)
        dense_ref[start : start + size, :] = dense


def teacher_columns(first_column, index, logprob, width):
    entries, tokens = index.shape
    block = 128
    return call(
        teacher_kernel, "teacher_columns", array((width, tokens), f32), index, logprob,
        grid=(tokens // block,), prefetch=(first_column.reshape(1),),
        ins=[pl.BlockSpec((entries, block), lambda i, s: (0, i))] * 2,
        outs=pl.BlockSpec((width, block), lambda i, s: (0, i)),
        flops=4 * tokens * width * entries, size=4 * tokens * width,
    )


def place_kernel(at_ref, *refs):
    by_x, out_ref = refs[:4], refs[4]
    for k in range(4):
        piece = by_x[k][...]
        for y in range(4):
            out_ref[y, (at_ref[0] + k) % 4] = piece


def gather_kernel(at_ref, *refs):
    by_x, out_ref = refs[:4], refs[4]
    for k in range(4):
        for y in range(4):
            out_ref[y, (at_ref[0] + k) % 4] = by_x[k][y]


def columns(weight_ref, blocks_ref, start, size):
    width = weight_ref.shape[1] // (2 * NY)
    parts = [pl.ds(pl.multiple_of(blocks_ref[k] * width + start, 256), size) for k in range(NY)]
    return jnp.concatenate([weight_ref[:, p] for p in parts], axis=1)


def side_by_side(rows_ref, part):
    return jnp.concatenate([rows_ref[k, part, :] for k in range(rows_ref.shape[0])], axis=1)


def half_logits_kernel(block_ref, rows_ref, weight_ref, *refs, second, step):
    out_ref = refs[-1]
    half = rows_ref.shape[2]
    left = columns(weight_ref, block_ref, second * half, half)
    for i in range(0, out_ref.shape[1], step):
        part = dot(left, side_by_side(rows_ref, pl.ds(i, step)), 1, 1)
        out_ref[:, i : i + step] = part if len(refs) == 1 else refs[0][:, i : i + step] + part


def half_logits(blocks, second, rows, weight, *before):
    count, tokens, half = rows.shape
    width = weight.shape[0]
    body = functools.partial(half_logits_kernel, second=second, step=256)
    return call(
        body, "logits_half", array((width, tokens), f32), rows, weight, *before,
        prefetch=(blocks,), flops=2 * count * tokens * half * width, size=6 * 2**20,
    )


def logits_rest_kernel(block_ref, first_ref, second_ref, weight_ref, own_ref, dense_ref, out_ref, stats_ref, *, step):
    tokens, half = out_ref.shape[1], first_ref.shape[2]
    left = jnp.concatenate([columns(weight_ref, block_ref, h * half, half) for h in range(2)], axis=1)
    for i in range(0, tokens, step):
        here = pl.ds(i, step)
        right = jnp.concatenate([side_by_side(first_ref, here), side_by_side(second_ref, here)], axis=1)
        logits = own_ref[:, i : i + step] + dot(left, right, 1, 1)
        out_ref[:, i : i + step] = logits
        peak = jnp.max(logits, axis=0, keepdims=True)
        weights = jnp.exp(logits - peak)
        total = jnp.sum(weights, axis=0, keepdims=True)
        stats_ref[:, i : i + step] = peak + jnp.log(total)
        target = jnp.sum(logits * dense_ref[:, i : i + step], axis=0, keepdims=True)
        stats_ref[:, tokens + i : tokens + i + step] = target
        mean = jnp.sum(weights * logits, axis=0, keepdims=True) / total
        stats_ref[:, 2 * tokens + i : 2 * tokens + i + step] = mean


def logits_call(blocks, rows, weight, own, dense):
    count, tokens, half = rows[0].shape
    width = weight.shape[0]
    return call(
        functools.partial(logits_rest_kernel, step=256), "logits_rest",
        [array((width, tokens), f32), array((1, 3 * tokens), f32)], *rows, weight, own, dense,
        prefetch=(blocks,), flops=4 * count * tokens * half * width, size=8 * 2**20,
    )


def grad_kernel(
    block_ref, stats_ref, logits_ref, dense_ref, logprob_ref, weight_ref, grad_ref, turned_ref, out_ref, pad_ref
):
    width, tokens = logits_ref.shape
    step = pad_ref.shape[1]
    pad_ref[...] = jnp.zeros(pad_ref.shape, f32)
    for i in range(0, tokens, step):
        totals = stats_ref[:, i : i + step]
        peak = jnp.max(totals, axis=0, keepdims=True)
        total = peak + jnp.log(jnp.sum(jnp.exp(totals - peak), axis=0, keepdims=True))
        mass = jnp.sum(jnp.exp(logprob_ref[:, i : i + step]), axis=0, keepdims=True)
        student = mass * jnp.exp(logits_ref[:, i : i + step] - total)
        grad = loss_scale * (student - dense_ref[:, i : i + step])
        grad_ref[:, i : i + step] = grad.astype(bf16)
        pad_ref[:width, :] = grad
        turned_ref[i : i + step, :] = pad_ref[...].T[:, :width].astype(bf16)
    rest_kernel(block_ref, turned_ref, weight_ref, out_ref, second=0)


def feature_part(weight_ref, blocks_ref, k, second):
    half = weight_ref.shape[1] // (4 * NY)
    return weight_ref[:, pl.ds(pl.multiple_of(blocks_ref[k] * 2 * half + second * half, 256), half)]


def grad_call(blocks, stats, logits, dense, logprob, weight):
    width, tokens = logits.shape
    count = blocks.shape[0]
    half = weight.shape[1] // (4 * count)
    inside = pl.BlockSpec(memory_space=pltpu.VMEM)
    return call(
        grad_kernel, "grad_logits",
        [array((width, tokens), bf16), array((tokens, width), bf16), array((count, tokens, half), bf16)],
        stats, logits, dense, logprob, weight, prefetch=(blocks,), ins=[inside] * 5, outs=[inside] * 3,
        scratch=[pltpu.VMEM((-(-width // 128) * 128, 128), f32)],
        flops=2 * count * tokens * half * width, size=12 * 2**20,
    )


def rest_kernel(block_ref, turned_ref, weight_ref, out_ref, *, second):
    for k in range(out_ref.shape[0]):
        out_ref[k] = dot(turned_ref[...], feature_part(weight_ref, block_ref, k, second)).astype(bf16)


def add_kernel(block_ref, turned_ref, weight_ref, other_ref, out_ref, *, second):
    for k in range(out_ref.shape[0]):
        out = dot(turned_ref[...], feature_part(weight_ref, block_ref, k, second))
        out_ref[k] = (out + other_ref[k].astype(f32)).astype(bf16)


def split_kernel(block_ref, at_ref, turned_ref, weight_ref, other_ref, *refs, second):
    by_x, keep_ref = refs[:4], refs[4]
    rows = keep_ref.shape[2]
    for y in range(other_ref.shape[0]):
        out = dot(turned_ref[...], feature_part(weight_ref, block_ref, y, second))
        out = (out + other_ref[y].astype(f32)).astype(bf16)
        for k in range(4):
            keep_ref[k, y] = out[k * rows : (k + 1) * rows]
    for k in range(4):
        by_x[k][...] = keep_ref[(at_ref[0] + k) % 4]


def half_call(body, name, blocks, second, turned, weight, *other, at=None):
    tokens, width = turned.shape
    count = blocks.shape[0]
    half = weight.shape[1] // (4 * count)
    rows = tokens // NX
    inside = pl.BlockSpec(memory_space=pltpu.VMEM)
    if at is None:
        out, outs, scratch, prefetch = array((count, tokens, half), bf16), inside, (), (blocks,)
    else:
        out, outs = [array((count, rows, half), bf16)] * 4, [inside] * 4
        scratch, prefetch = [pltpu.VMEM((NX, count, rows, half), bf16)], (blocks, at)
    return call(
        functools.partial(body, second=second), name, out, turned, weight, *other, prefetch=prefetch, scratch=scratch,
        ins=[inside] * (2 + len(other)), outs=outs, flops=2 * count * tokens * half * width, size=6 * 2**20,
    )


def sum_kernel(at_ref, by_y_ref, *refs):
    by_x, to_x, to_y_ref, keep_ref = refs[:4], refs[4:8], refs[8], refs[9]
    count, rows = by_x[0].shape[:2]
    for i in range(count):
        part = pl.ds(i * rows, rows)
        keep_ref[i] = sum(by_y_ref[j, part, :].astype(f32) for j in range(count)).astype(bf16)
        to_y_ref[i] = sum(r[i].astype(f32) for r in by_x).astype(bf16)
    for k in range(4):
        to_x[k][...] = keep_ref[(at_ref[0] + k) % 4]


def tokens_kernel(stats_ref, logprob_ref, kl_ref, dots_ref):
    tokens = kl_ref.shape[1]
    logprob = logprob_ref[...]
    prob = jnp.exp(logprob)
    mass = jnp.sum(prob, axis=0, keepdims=True)
    totals = stats_ref[:, :tokens]
    peak = jnp.max(totals, axis=0, keepdims=True)
    weights = jnp.exp(totals - peak)
    total = jnp.sum(weights, axis=0, keepdims=True)
    target = jnp.sum(stats_ref[:, tokens : 2 * tokens], axis=0, keepdims=True)
    mean = jnp.sum(weights * stats_ref[:, 2 * tokens :], axis=0, keepdims=True) / total
    kl_ref[...] = jnp.sum(prob * logprob, axis=0, keepdims=True) - target + mass * (peak + jnp.log(total))
    dots_ref[...] = loss_scale * (mass * mean - target)


def spread_kernel(*refs):
    by_x, (by_y_ref, spread_ref, out_ref) = refs[:4], refs[4:]
    first = sum(r[...].astype(f32) for r in by_x)
    second = sum(by_y_ref[j].astype(f32) for j in range(by_y_ref.shape[0]))
    both = jnp.concatenate([first.astype(bf16), second.astype(bf16)], axis=1)
    turns = out_ref.shape[1]
    slots = NX * turns
    for z in range(out_ref.shape[0] // NX):
        rows = dot(spread_ref[z * slots : (z + 1) * slots, :].astype(bf16), both).astype(bf16)
        for k in range(NX):
            out_ref[z * NX + k] = rows[k * turns : (k + 1) * turns]


def finish_kernel(at_ref, got_ref, rows_ref, gain_ref, dots_ref, out_ref, sum_ref, grad_ref):
    offset, count = own_slots(at_ref)
    turns, share = sum_ref.shape[1:]
    slots, features = rows_ref.shape
    tokens = dots_ref.shape[1]
    for k in range(NX):
        total = got_ref[k].astype(f32)
        for z in range(1, got_ref.shape[0] // NX):
            total += got_ref[z * NX + k].astype(f32)
        sum_ref[k] = total
    for i in range(NX):
        for m in range(turns):
            grad_ref[NX * m + i : NX * m + i + 1, :] = sum_ref[(offset + i) & (NX - 1), m : m + 1, :]
    rank = offset + lax.broadcasted_iota(jnp.int32, (slots, tokens), 0)
    row = (rank & (NX - 1)) * (tokens // NX) + ((rank & (GROUPS - 1)) >> 2) * (tokens // GROUPS) + (rank >> 5)
    here = row == lax.broadcasted_iota(jnp.int32, (slots, tokens), 1)
    dots = jnp.sum(jnp.where(here, dots_ref[...], 0.0), axis=1, keepdims=True)
    part = pl.ds(pl.multiple_of(at_ref[3] * share, share), share)
    inv_rms = inverse_rms(rows_ref, share)
    grad = (grad_ref[...] * gain_ref[:, part] - rows_ref[:, part].astype(f32) * (inv_rms * dots / features)) * inv_rms
    live = lax.broadcasted_iota(jnp.int32, grad.shape, 0) < count
    out_ref[...] = jnp.where(live, grad, 0.0).astype(bf16)


def weight_grad_kernel(block_ref, *refs):
    own, rest, grad_ref, out_ref = refs[:2], refs[2:4], refs[4], refs[5]

    def write(rows):
        half = rows[0].shape[2]
        for h in range(2):
            out_ref[:, h * half : (h + 1) * half] = dot(grad_ref[...], rows[h][0]).astype(bf16)

    count = pl.num_programs(0) // 2

    @pl.when(pl.program_id(0) < count)
    def _():
        write(own)

    @pl.when(pl.program_id(0) >= count)
    def _():
        write(rest)


def weight_grad(blocks, own, rest, grad):
    count, tokens, half = own[0].shape
    width = grad.shape[0]
    return call(
        weight_grad_kernel, "weight_grad", array((width, 4 * count * half), bf16), *own, *rest, grad,
        grid=(2 * count,), prefetch=(blocks,),
        ins=[
            *[pl.BlockSpec((1, tokens, half), lambda k, b: (jnp.minimum(k, count - 1), 0, 0))] * 2,
            *[pl.BlockSpec((1, tokens, half), lambda k, b: (jnp.maximum(k - count, 0), 0, 0))] * 2,
            pl.BlockSpec((width, tokens), lambda k, b: (0, 0)),
        ],
        outs=pl.BlockSpec((width, 2 * half), lambda k, b: (0, b[k])),
        flops=8 * count * tokens * half * width, size=16 * 2**20,
    )


def after(small, *others):
    return lax.optimization_barrier((small, others))[0]


def exchange(x, axis, lines=None):
    return lax.all_to_all(x, axis, 0, 0, tiled=True, axis_index_groups=lines)


def along_x(x, k):
    return lax.ppermute(x, "seq", [(i, i // NX * NX + (i + k) % NX) for i in range(GROUPS)])


def along_y(x, k):
    return lax.ppermute(x, "vocab", [(i, (i + 2 * k) % (2 * NY)) for i in range(2 * NY)])


def from_ahead(x, move):
    got = {k: move(x, -k) for k in STEPS}
    return [x, got[1], got[2], got[3]]


def to_ahead(pieces, move):
    return [pieces[0], *(move(pieces[k], k) for k in STEPS)]


def merge(stats):
    tokens = stats[0].shape[1] // 3
    totals = [s[:, :tokens] for s in stats]
    peak = totals[0]
    for t in totals[1:]:
        peak = jnp.maximum(peak, t)
    weights = [jnp.exp(t - peak) for t in totals]
    total = sum(weights)
    target = sum(s[:, tokens : 2 * tokens] for s in stats)
    mean = sum(w * s[:, 2 * tokens :] for w, s in zip(weights, stats)) / total
    return jnp.concatenate([peak + jnp.log(total), target, mean], axis=1)


def per_device(rollout, group_count, final_gain, head_weight, teacher_index, teacher_logprob):
    slots, features = rollout.shape
    tokens, entries = teacher_index.shape
    width = head_weight.shape[1]
    weight = head_weight.T
    parts = 2 * NY
    share = features // parts
    half = share // 2
    class_rows = tokens // NX
    turns = slots // NX
    pack_rows = tokens // GROUPS
    seq = lax.axis_index("seq")
    own_z, own_x = seq // NX, seq % NX
    vocab = lax.axis_index("vocab")
    own_y, core = vocab // 2, vocab % 2
    at = jnp.concatenate([jnp.stack([own_x, own_y, seq, vocab]).astype(jnp.int32), group_count])

    of_class = call(
        sort_kernel, "sort_rows", array((GROUPS, turns, share), bf16), rollout, final_gain[None, :], prefetch=(at,), size=2**19
    )
    of_class = exchange(of_class, "seq")

    def class_order(a):
        return a.reshape(NZ, NX, pack_rows, entries).transpose(1, 0, 2, 3).reshape(tokens, entries).T

    index = class_order(teacher_index)
    logprob = class_order(teacher_logprob)
    first_column = (seq * parts + vocab) * width
    dense = teacher_columns(first_column, index, logprob, width)

    group_ids = jnp.arange(GROUPS, dtype=jnp.int32)
    before = group_ids[None, :] < group_ids[:, None]
    offsets = jnp.sum(jnp.where(before, group_count[None, :], 0), axis=1)
    turn_ids = jnp.arange(turns, dtype=jnp.int32)
    row_in_group = (own_x - offsets[:, None]) % NX + NX * turn_ids[None, :]
    rank = offsets[:, None] + row_in_group
    place = jnp.where(row_in_group < group_count[:, None], rank % GROUPS // NX * pack_rows + rank // GROUPS, class_rows)
    place_ids = jnp.arange(class_rows, dtype=jnp.int32)
    place = after(place, dense)
    spread = lax.optimization_barrier((place.reshape(-1, 1) == place_ids[None, :]).astype(f32))
    dense_rows = dot(spread.astype(bf16), of_class.reshape(-1, share), 0, 0).astype(bf16)

    by_x = from_ahead(dense_rows[:, :half], along_x)
    all_y = exchange(jnp.broadcast_to(dense_rows[:, half:], (NY, class_rows, half)), "vocab", Y_LINES)
    all_x = call(place_kernel, "place", array((NY, NX, class_rows, half), bf16), *by_x, prefetch=(at,), size=2**21)
    by_x = from_ahead(all_y, along_x)
    own_first = exchange(all_x.reshape(NY, tokens, half), "vocab", Y_LINES)

    y_ids = jnp.arange(NY, dtype=jnp.int32)
    own_blocks = 2 * y_ids + core
    rest_blocks = 2 * y_ids + 1 - core
    own_second = call(
        gather_kernel, "gather_rows", array((NY, NX, class_rows, half), bf16), *by_x, prefetch=(at,), size=2**22
    ).reshape(NY, tokens, half)
    rest_second = lax.ppermute(own_second, "vocab", OTHER_CORE)
    logits_own = half_logits(own_blocks, 1, own_second, weight)
    rest_first = lax.ppermute(own_first, "vocab", OTHER_CORE)
    logits_own = half_logits(after(own_blocks, logits_own), 0, own_first, weight, logits_own)
    own_rows, rest_rows = [own_first, own_second], [rest_first, rest_second]
    logits, stats = logits_call(rest_blocks, rest_rows, weight, logits_own, dense)
    stats = merge([stats, lax.ppermute(stats, "vocab", OTHER_CORE)])
    stats = merge(from_ahead(stats, along_y))
    stats = exchange(jnp.broadcast_to(stats, (GROUPS, 3 * tokens)), "seq")

    grad, turned, rest_first = grad_call(rest_blocks, stats, logits, dense, logprob, weight)
    other_first = lax.ppermute(rest_first, "vocab", OTHER_CORE)
    other_second = lax.ppermute(half_call(rest_kernel, "grad_rest", rest_blocks, 1, turned, weight), "vocab", OTHER_CORE)
    first = half_call(add_kernel, "grad_first", own_blocks, 0, turned, weight, other_first)
    by_y = exchange(first, "vocab", Y_LINES)
    pieces = half_call(split_kernel, "grad_second", after(own_blocks, first), 1, turned, weight, other_second, at=at)
    by_x = to_ahead(pieces, along_x)
    weight_t = weight_grad(after(jnp.concatenate([own_blocks, rest_blocks]), pieces), own_rows, rest_rows, grad)
    kl, dots = call(tokens_kernel, "tokens", [array((1, tokens), f32)] * 2, stats, logprob, size=2**19)
    kl = lax.dynamic_slice_in_dim(kl[0], own_x * class_rows + own_z * pack_rows, pack_rows)
    at = after(at, weight_t, kl, dots)

    small = array((class_rows, half), bf16)
    inside = pl.BlockSpec(memory_space=pltpu.VMEM)
    *pieces, to_y = call(
        sum_kernel, "add_pieces", [small] * 4 + [array((NY, class_rows, half), bf16)], by_y, *by_x, prefetch=(at,),
        ins=[inside] * 5, outs=[inside] * 5, scratch=[pltpu.VMEM((NX, class_rows, half), bf16)], size=2**22,
    )
    by_x = to_ahead(pieces, along_x)
    by_y = exchange(to_y, "vocab", Y_LINES)
    spread_grad = call(
        spread_kernel, "spread_rows", array((GROUPS, turns, share), bf16), *by_x, by_y, spread, size=2**20
    )
    grad_rollout = call(
        finish_kernel, "finish", array((slots, share), bf16), exchange(spread_grad, "seq"), rollout, final_gain[None, :],
        dots, prefetch=(at,), ins=[inside] * 4, outs=inside,
        scratch=[pltpu.VMEM((NX, turns, share), f32), pltpu.VMEM((slots, share), f32)], size=2**19,
    )
    return (kl, weight_t.T, grad_rollout)


def solution(mesh):
    placed = (P("seq", None), P(), P(), P(None, ("seq", "vocab")), P(), P())
    return jax.shard_map(
        per_device,
        mesh=mesh,
        in_specs=placed,
        out_specs=(P("seq"), P(None, ("seq", "vocab")), P("seq", "vocab")),
        check_vma=False,
    )
```

time: 808 us -> 198 us (0.25)
  waiting for transfers between devices: 314 us -> 37.8 us
  other arithmetic: 268 us -> 0.54 us
  blocking collectives: 147 us -> 37.9 us
  Pallas kernels: 0 us -> 51.4 us
  starting transfers between devices: 21.4 us -> 55.4 us
  matrix products: 28.4 us -> 0.28 us
  between operations: 16.6 us -> 1.11 us
    unnamed x4 -> x1, other arithmetic: 258 us -> 0.01 us
    reduce_scatter x1 -> x0, waiting for transfers between devices: 233 us -> none  [per_device(): lax.psum_scatter(lax.dot_general(grad_logits, head_weight, (((1,), (1,)),...]
    psum x1 -> x0, blocking collectives: 74.5 us -> none  [per_device(): lax.psum((local_total, target_part), ('seq', 'vocab'))]
    pmax x1 -> x0, blocking collectives: 72.9 us -> none  [per_device(): row_peak = lax.pmax(local_peak, ('seq', 'vocab'))]
    psum x1 -> x0, waiting for transfers between devices: 63 us -> none  [per_device(): whole_rows = lax.psum(partial_rows, 'vocab')]
    pallas_call x0 -> x16, Pallas kernels: none -> 51.4 us  [call(): pl.pallas_call(body, grid_spec=pltpu.PrefetchScalarGridSpec(num_scalar_pr...]
    all_to_all x0 -> x2, blocking collectives: none -> 37.9 us  [exchange(): return lax.all_to_all(x, axis, 0, 0, tiled=True, axis_index_groups=lines)]
    ppermute x0 -> x20, waiting for transfers between devices: none -> 30.6 us  [the longest x12 27.6 us: along_x(): lax.ppermute(x, 'seq', [(i, i // NX * NX + (i + k) % NX) for i in range(G...]
  transfers between devices with their start and end apart: 5 -> 25, of which waited for: 4 -> 13; matrix products, arithmetic and copies ran while one was open for 33% -> 1% of each run, Pallas kernels for 0% -> 19%
where the time goes in v3:
time: 198 us; the launch traced here: 197 us
  starting transfers between devices  55.4 us (28%)
  Pallas kernels  51.4 us (26%)
  blocking collectives  37.9 us (19%)
  waiting for transfers between devices  37.8 us (19%)
  local copies, waits for them, and re-layouts  12.8 us (6%)
    pallas_call x16, Pallas kernels, call(): pl.pallas_call(body, grid_spec=pltpu.PrefetchScalarGridSpec(num_scalar_pr...  51.4 us
    all_to_all x2, blocking collectives, exchange(): return lax.all_to_all(x, axis, 0, 0, tiled=True, axis_index_groups=lines)  37.9 us
    all_to_all x5, starting transfers between devices, exchange(): return lax.all_to_all(x, axis, 0, 0, tiled=True, axis_index_groups=lines)  31.6 us
    ppermute x12, waiting for transfers between devices, along_x(): lax.ppermute(x, 'seq', [(i, i // NX * NX + (i + k) % NX) for i in range(G...  27.6 us
    ppermute x12, starting transfers between devices, along_x(): lax.ppermute(x, 'seq', [(i, i // NX * NX + (i + k) % NX) for i in range(G...  17.8 us
    unnamed x59, local copies, waits for them, and re-layouts  9.93 us
    all_to_all x5, waiting for transfers between devices, exchange(): return lax.all_to_all(x, axis, 0, 0, tiled=True, axis_index_groups=lines)  7.18 us
    ppermute x3, starting transfers between devices, along_y(): lax.ppermute(x, 'vocab', [(i, (i + 2 * k) % (2 * NY)) for i in range(2 *...  4.88 us
  transfers between devices with their start and end apart: 25, of which 13 were waited for; matrix products, arithmetic and copies ran while one was open for 1% of the time, Pallas kernels for 19%

profile of v3, /device:TPU:8, one launch (start us, length us, event | category | flops | bytes accessed | tf_op | source)
XLA Modules:
  0.0 197.3 jit_solution(2653556861299798470)
XLA Ops:
  3.1 1.8 sort_rows.1
  5.0 11.4 %all-to-all-start = ((bf16[32,9,512]{2,1,0:T(8,128)(2,1)}), bf16[32,9,512]{2,1,0:T(8,128)(2,1)S(1)}, u32[]{:S(2)}, u32[]{:S(2)}) async-start(bf16[32,9,512]{2,1,0:T(8,128)(2,1)} %sort_rows.1), calls=%async_computation | async-start | bytes 1048576 | tf_op jit(solution)/shard_map/all_to_all | solution.py:359
  17.3 9.3 %teacher_columns.1.dense_ref = f32[594,768]{1,0:T(8,128)S(1)} custom-call(s32[1]{0:T(128)} %bitcast.4.first_ref, s32[64,768]{1,0:T(8,128)S(1)} %bitcast.41, f32[64,768]{1,0:T(8,128)S(1)} %bitcast.36), custom_call_target="tpu_custom_call" | custom-call | flops 116785152 | bytes 1824768 | tf_op jit(solution)/shard_map/teacher_columns/pallas_call | solution.py:26
  27.0 7.2 %all-to-all-done = bf16[32,9,512]{2,1,0:T(8,128)(2,1)S(1)} async-done(((bf16[32,9,512]{2,1,0:T(8,128)(2,1)}), bf16[32,9,512]{2,1,0:T(8,128)(2,1)S(1)}, u32[]{:S(2)}, u32[]{:S(2)}) %all-to-all-start) | async-done | bytes 294944 | tf_op jit(solution)/shard_map/all_to_all | solution.py:359
  35.4 4.9 %all-to-all-start.2 = ((bf16[4,192,256]{2,1,0:T(8,128)(2,1)}), bf16[4,192,256]{2,1,0:T(8,128)(2,1)S(1)}, u32[]{:S(2)}, u32[]{:S(2)}) async-start(bf16[4,192,256]{2,1,0:T(8,128)(2,1)} %broadcast_in_dim.40), calls=%async_computation.2 | async-start | bytes 786432 | tf_op jit(solution)/shard_map/all_to_all | solution.py:359
  41.2 2.7 %collective-permute-start.1 = (bf16[192,256]{1,0:T(8,128)(2,1)S(1)}, bf16[192,256]{1,0:T(8,128)(2,1)S(1)}, u32[]{:S(2)}, u32[]{:S(2)}) collective-permute-start(bf16[192,256]{1,0:T(8,128)(2,1)S(1)} %get-tuple-element.46.refs_0_), channel_id=1, source_target_pairs={{0,16},{8,24},{16,0},{24,8},{32,48},{40,56},{48,32},{56,40},{64,80... | collective-permute-start | bytes 294920 | tf_op jit(solution)/shard_map/ppermute | solution.py:363
  50.3 4.8 %all-to-all-start.1 = ((bf16[4,768,256]{2,1,0:T(8,128)(2,1)}), bf16[4,768,256]{2,1,0:T(8,128)(2,1)}, u32[]{:S(2)}, u32[]{:S(2)}) async-start(bf16[4,768,256]{2,1,0:T(8,128)(2,1)} %bitcast.35), calls=%async_computation.1 | async-start | bytes 3145728 | tf_op jit(solution)/shard_map/all_to_all | solution.py:359
  56.5 2.8 %collective-permute-start.5 = (bf16[4,192,256]{2,1,0:T(8,128)(2,1)S(1)}, bf16[4,192,256]{2,1,0:T(8,128)(2,1)S(1)}, u32[]{:S(2)}, u32[]{:S(2)}) collective-permute-start(bf16[4,192,256]{2,1,0:T(8,128)(2,1)S(1)} %all-to-all-done.2.refs_0_), channel_id=1, source_target_pairs={{0,16},{8,24},{16,0},{24,8},{32,48},{40,56},{48,32},{56,40},{64,80... | collective-permute-start | bytes 1179656 | tf_op jit(solution)/shard_map/ppermute | solution.py:363
  59.7 8.6 %collective-permute-done.6.refs_3_ = bf16[4,192,256]{2,1,0:T(8,128)(2,1)S(1)} collective-permute-done((bf16[4,192,256]{2,1,0:T(8,128)(2,1)S(1)}, bf16[4,192,256]{2,1,0:T(8,128)(2,1)S(1)}, u32[]{:S(2)}, u32[]{:S(2)}) %collective-permute-start.6) | collective-permute-done | bytes 393248 | tf_op jit(solution)/shard_map/ppermute | solution.py:363
  68.3 4.3 %collective-permute-done.5.refs_2_ = bf16[4,192,256]{2,1,0:T(8,128)(2,1)S(1)} collective-permute-done((bf16[4,192,256]{2,1,0:T(8,128)(2,1)S(1)}, bf16[4,192,256]{2,1,0:T(8,128)(2,1)S(1)}, u32[]{:S(2)}, u32[]{:S(2)}) %collective-permute-start.5) | collective-permute-done | bytes 393248 | tf_op jit(solution)/shard_map/ppermute | solution.py:363
  72.6 1.8 gather_rows.1
  74.9 2.4 %copy-done = bf16[4096,594]{0,1:T(8,128)(2,1)S(1)} copy-done((bf16[4096,594]{0,1:T(8,128)(2,1)S(1)}, bf16[4096,594]{0,1:T(8,128)(2,1)}, u32[]{:S(2)}) %copy-start) | copy-done | bytes 4866072
  77.3 3.4 %logits_half.2.refs_0_ = f32[594,768]{1,0:T(8,128)S(1)} custom-call(s32[4]{0:T(128)S(1)} %fusion.21.block_ref, bf16[4,768,256]{2,1,0:T(8,128)(2,1)} %bitcast.15.rows_ref.refs_1_, bf16[594,4096]{1,0:T(8,128)(2,1)S(1)} %bitcast.26), custom_call_target="tpu_custom_call" | custom-call | flops 934281216 | bytes 6291456 | tf_op jit(solution)/shard_map/logits_half/pallas_call | solution.py:26
  80.7 3.1 %logits_half.3.own_ref = f32[594,768]{1,0:T(8,128)S(1)} custom-call(s32[4]{0:T(128)S(1)} %fusion.21.block_ref, bf16[4,768,256]{2,1,0:T(8,128)(2,1)} %all-to-all-done.1.rows_ref.refs_0_, bf16[594,4096]{1,0:T(8,128)(2,1)S(1)} %bitcast.29, f32[594,768]{1,0:T(8,128)S(1)} %logits_half.2.refs_0_), custom_call_target="tpu_custom_call" | custom-call | flops 934281216 | bytes 6291456 | tf_op jit(solution)/shard_map/logits_half/pallas_call | solution.py:26
  83.9 5.1 %logits_rest.1 = (f32[594,768]{1,0:T(8,128)S(1)}, f32[1,2304]{1,0:T(1,128)S(1)}) custom-call(s32[4]{0:T(128)S(1)} %add_subtract_fusion.block_ref, bf16[4,768,256]{2,1,0:T(8,128)(2,1)} %collective-permute-done.3.first_ref.refs_2_, bf16[4,768,256]{2,1,0:T(8,128)(2,1)} %collective-permute-done.7.second_ref.refs_3_, bf16[594,4096]{1,0:T(8,128)(2,1)S(1)} %bitcast.30, ...), custom_call_target="tpu_custom_call" | custom-call | flops 1868562432 | bytes 8388608 | tf_op jit(solution)/shard_map/logits_rest/pallas_call | solution.py:26
  92.9 2.3 %collective-permute-start.9 = (f32[1,2304]{1,0:T(1,128)S(1)}, f32[1,2304]{1,0:T(1,128)S(1)}, u32[]{:S(2)}, u32[]{:S(2)}) collective-permute-start(f32[1,2304]{1,0:T(1,128)S(1)} %pad_maximum_fusion), channel_id=1, source_target_pairs={{0,6},{1,7},{2,0},{3,1},{4,2},{5,3},{6,4},{7,5},{8,14},{9,15},{10,... | collective-permute-start | bytes 27656 | tf_op jit(solution)/shard_map/ppermute | solution.py:367
  95.2 1.8 collective-permute-done.10
  97.3 18.0 %all_to_all.38 = f32[32,1,2304]{2,1,0:T(1,128)S(1)} all-to-all(f32[32,1,2304]{2,1,0:T(1,128)S(1)} %broadcast_in_dim.41), channel_id=1, replica_groups=mesh['seq'=32,'vocab'=8] {'seq'}, dimensions={0} | all-to-all | bytes 589824 | tf_op jit(solution)/shard_map/all_to_all | solution.py:359
  115.3 2.3 %grad_logits.1 = (bf16[594,768]{1,0:T(8,128)(2,1)S(1)}, bf16[768,594]{1,0:T(8,128)(2,1)S(1)}, bf16[4,768,256]{2,1,0:T(8,128)(2,1)S(1)}) custom-call(s32[4]{0:T(128)S(1)} %add_subtract_fusion.block_ref, f32[32,2304]{1,0:T(8,128)S(1)} %bitcast.39, f32[594,768]{1,0:T(8,128)S(1)} %get-tuple-element.28.logits_ref, f32[594,768]{1,0:T(8,128)S(1)} %teacher_columns.1.dense_ref, ...), custom_call_target="tpu_custom_call" | custom-call | flops 934281216 | bytes 12582912 | tf_op jit(solution)/shard_map/grad_logits/pallas_call | solution.py:26
  117.7 3.1 %grad_rest.1 = bf16[4,768,256]{2,1,0:T(8,128)(2,1)} custom-call(s32[4]{0:T(128)S(1)} %add_subtract_fusion.block_ref, bf16[768,594]{1,0:T(8,128)(2,1)S(1)} %get-tuple-element.29.turned_ref, bf16[594,4096]{1,0:T(8,128)(2,1)S(1)} %bitcast.32), custom_call_target="tpu_custom_call" | custom-call | flops 934281216 | bytes 6291456 | tf_op jit(solution)/shard_map/grad_rest/pallas_call | solution.py:26
  121.3 3.2 %grad_first.1 = bf16[4,768,256]{2,1,0:T(8,128)(2,1)} custom-call(s32[4]{0:T(128)S(1)} %fusion.21.block_ref, bf16[768,594]{1,0:T(8,128)(2,1)S(1)} %get-tuple-element.29.turned_ref, bf16[594,4096]{1,0:T(8,128)(2,1)S(1)} %bitcast.33, bf16[4,768,256]{2,1,0:T(8,128)(2,1)S(1)} %collective-permute-done.12.other_ref), custom_call_target="tpu_custom_call" | custom-call | flops 934281216 | bytes 6291456 | tf_op jit(solution)/shard_map/grad_first/pallas_call | solution.py:26
  124.5 5.5 %all-to-all-start.4 = ((bf16[4,768,256]{2,1,0:T(8,128)(2,1)}), bf16[4,768,256]{2,1,0:T(8,128)(2,1)S(1)}, u32[]{:S(2)}, u32[]{:S(2)}) async-start(bf16[4,768,256]{2,1,0:T(8,128)(2,1)} %grad_first.1), calls=%async_computation.4 | async-start | bytes 3145728 | tf_op jit(solution)/shard_map/all_to_all | solution.py:359
  130.3 2.4 %copy-done.1 = bf16[4096,594]{0,1:T(8,128)(2,1)S(1)} copy-done((bf16[4096,594]{0,1:T(8,128)(2,1)S(1)}, bf16[4096,594]{0,1:T(8,128)(2,1)}, u32[]{:S(2)}) %copy-start.1) | copy-done | bytes 4866072
  132.7 3.5 %grad_second.1 = (bf16[4,192,256]{2,1,0:T(8,128)(2,1)S(1)}, bf16[4,192,256]{2,1,0:T(8,128)(2,1)S(1)}, bf16[4,192,256]{2,1,0:T(8,128)(2,1)S(1)}, bf16[4,192,256]{2,1,0:T(8,128)(2,1)S(1)}) custom-call(s32[4]{0:T(128)S(1)} %fusion.21.block_ref, s32[36]{0:T(128)S(1)} %concatenate.14.at_ref, bf16[768,594]{1,0:T(8,128)(2,1)S(1)} %get-tuple-element.29.turned_ref, ...), custom_call_target="tpu_custom_call" | custom-call | flops 934281216 | bytes 6291456 | tf_op jit(solution)/shard_map/grad_second/pallas_call | solution.py:26
  136.2 2.5 %collective-permute-start.16 = (bf16[4,192,256]{2,1,0:T(8,128)(2,1)S(1)}, bf16[4,192,256]{2,1,0:T(8,128)(2,1)S(1)}, u32[]{:S(2)}, u32[]{:S(2)}) collective-permute-start(bf16[4,192,256]{2,1,0:T(8,128)(2,1)S(1)} %get-tuple-element.34), channel_id=1, source_target_pairs={{0,16},{8,24},{16,0},{24,8},{32,48},{40,56},{48,32},{56,40},{64,80... | collective-permute-start | bytes 1179656 | tf_op jit(solution)/shard_map/ppermute | solution.py:363
  140.8 10.2 %weight_grad.1 = bf16[594,4096]{1,0:T(8,128)(2,1)} custom-call(s32[8]{0:T(128)S(1)} %pad_add_fusion.block_ref, bf16[4,768,256]{2,1,0:T(8,128)(2,1)} %all-to-all-done.1.rows_ref.refs_0_, bf16[4,768,256]{2,1,0:T(8,128)(2,1)} %bitcast.15.rows_ref.refs_1_, bf16[4,768,256]{2,1,0:T(8,128)(2,1)} %collective-permute-done.3.first_ref.refs_2_, ...), custom_call_target="tpu_custom_call" | custom-call | flops 3737124864 | bytes 16777216 | tf_op jit(solution)/shard_map/weight_grad/pallas_call | solution.py:26
  151.0 5.5 %collective-permute-done.14.refs_1_ = bf16[4,192,256]{2,1,0:T(8,128)(2,1)S(1)} collective-permute-done((bf16[4,192,256]{2,1,0:T(8,128)(2,1)S(1)}, bf16[4,192,256]{2,1,0:T(8,128)(2,1)S(1)}, u32[]{:S(2)}, u32[]{:S(2)}) %collective-permute-start.14) | collective-permute-done | bytes 393248 | tf_op jit(solution)/shard_map/ppermute | solution.py:363
  160.8 4.9 %all-to-all-start.5 = ((bf16[4,192,256]{2,1,0:T(8,128)(2,1)}), bf16[4,192,256]{2,1,0:T(8,128)(2,1)S(1)}, u32[]{:S(2)}, u32[]{:S(2)}) async-start(bf16[4,192,256]{2,1,0:T(8,128)(2,1)} %get-tuple-element.44), calls=%async_computation.5 | async-start | bytes 786432 | tf_op jit(solution)/shard_map/all_to_all | solution.py:359
  166.5 2.5 %collective-permute-start.18 = (bf16[192,256]{1,0:T(8,128)(2,1)}, bf16[192,256]{1,0:T(8,128)(2,1)S(1)}, u32[]{:S(2)}, u32[]{:S(2)}) collective-permute-start(bf16[192,256]{1,0:T(8,128)(2,1)} %copy-done.21), channel_id=1, source_target_pairs={{0,24},{8,0},{16,8},{24,16},{32,56},{40,32},{48,40},{56,48},{64,88... | collective-permute-start | bytes 294920 | tf_op jit(solution)/shard_map/ppermute | solution.py:363
  169.8 1.9 collective-permute-done.17.refs_1_
  172.4 2.9 %collective-permute-done.19.refs_3_ = bf16[192,256]{1,0:T(8,128)(2,1)S(1)} collective-permute-done((bf16[192,256]{1,0:T(8,128)(2,1)}, bf16[192,256]{1,0:T(8,128)(2,1)S(1)}, u32[]{:S(2)}, u32[]{:S(2)}) %collective-permute-start.19) | collective-permute-done | bytes 98336 | tf_op jit(solution)/shard_map/ppermute | solution.py:363
  175.8 19.9 %all_to_all.39.got_ref = bf16[32,9,512]{2,1,0:T(8,128)(2,1)S(1)} all-to-all(bf16[32,9,512]{2,1,0:T(8,128)(2,1)S(1)} %spread_rows.1), channel_id=1, replica_groups=mesh['seq'=32,'vocab'=8] {'seq'}, dimensions={0} | all-to-all | bytes 589824 | tf_op jit(solution)/shard_map/all_to_all | solution.py:359
  (120 shorter events, 30.0 us)
Async XLA Ops:
  5.0 29.2 %all-to-all-start = ((bf16[32,9,512]{2,1,0:T(8,128)(2,1)}), bf16[32,9,512]{2,1,0:T(8,128)(2,1)S(1)}, u32[]{:S(2)}, u32[]{:S(2)}) async-start(bf16[32,9,512]{2,1,0:T(8,128)(2,1)} %sort_rows.1), calls=%async_computation | async-start | bytes 1048576 | tf_op jit(solution)/shard_map/all_to_all | solution.py:359
  17.3 17.0 %copy-start.3 = (f32[768,64]{0,1:T(8,128)}, f32[768,64]{0,1:T(8,128)S(1)}, u32[]{:S(2)}) copy-start(f32[768,64]{0,1:T(8,128)S(1)} %copy.28) | copy-start | bytes 589828
  35.4 14.9 %all-to-all-start.2 = ((bf16[4,192,256]{2,1,0:T(8,128)(2,1)}), bf16[4,192,256]{2,1,0:T(8,128)(2,1)S(1)}, u32[]{:S(2)}, u32[]{:S(2)}) async-start(bf16[4,192,256]{2,1,0:T(8,128)(2,1)} %broadcast_in_dim.40), calls=%async_computation.2 | async-start | bytes 786432 | tf_op jit(solution)/shard_map/all_to_all | solution.py:359
  40.3 5.8 %collective-permute-start.2 = (bf16[192,256]{1,0:T(8,128)(2,1)S(1)}, bf16[192,256]{1,0:T(8,128)(2,1)S(1)}, u32[]{:S(2)}, u32[]{:S(2)}) collective-permute-start(bf16[192,256]{1,0:T(8,128)(2,1)S(1)} %get-tuple-element.46.refs_0_), channel_id=1, source_target_pairs={{0,8},{8,16},{16,24},{24,0},{32,40},{40,48},{48,56},{56,32},{64,72... | collective-permute-start | bytes 294920 | tf_op jit(solution)/shard_map/ppermute | solution.py:363
  41.2 6.3 %collective-permute-start.1 = (bf16[192,256]{1,0:T(8,128)(2,1)S(1)}, bf16[192,256]{1,0:T(8,128)(2,1)S(1)}, u32[]{:S(2)}, u32[]{:S(2)}) collective-permute-start(bf16[192,256]{1,0:T(8,128)(2,1)S(1)} %get-tuple-element.46.refs_0_), channel_id=1, source_target_pairs={{0,16},{8,24},{16,0},{24,8},{32,48},{40,56},{48,32},{56,40},{64,80... | collective-permute-start | bytes 294920 | tf_op jit(solution)/shard_map/ppermute | solution.py:363
  43.9 4.6 %collective-permute-start = (bf16[192,256]{1,0:T(8,128)(2,1)S(1)}, bf16[192,256]{1,0:T(8,128)(2,1)S(1)}, u32[]{:S(2)}, u32[]{:S(2)}) collective-permute-start(bf16[192,256]{1,0:T(8,128)(2,1)S(1)} %get-tuple-element.46.refs_0_), channel_id=1, source_target_pairs={{0,24},{8,0},{16,8},{24,16},{32,56},{40,32},{48,40},{56,48},{64,88... | collective-permute-start | bytes 294920 | tf_op jit(solution)/shard_map/ppermute | solution.py:363
  50.3 24.1 %all-to-all-start.1 = ((bf16[4,768,256]{2,1,0:T(8,128)(2,1)}), bf16[4,768,256]{2,1,0:T(8,128)(2,1)}, u32[]{:S(2)}, u32[]{:S(2)}) async-start(bf16[4,768,256]{2,1,0:T(8,128)(2,1)} %bitcast.35), calls=%async_computation.1 | async-start | bytes 3145728 | tf_op jit(solution)/shard_map/all_to_all | solution.py:359
  55.1 13.2 %collective-permute-start.6 = (bf16[4,192,256]{2,1,0:T(8,128)(2,1)S(1)}, bf16[4,192,256]{2,1,0:T(8,128)(2,1)S(1)}, u32[]{:S(2)}, u32[]{:S(2)}) collective-permute-start(bf16[4,192,256]{2,1,0:T(8,128)(2,1)S(1)} %all-to-all-done.2.refs_0_), channel_id=1, source_target_pairs={{0,8},{8,16},{16,24},{24,0},{32,40},{40,48},{48,56},{56,32},{64,72... | collective-permute-start | bytes 1179656 | tf_op jit(solution)/shard_map/ppermute | solution.py:363
  56.5 16.1 %collective-permute-start.5 = (bf16[4,192,256]{2,1,0:T(8,128)(2,1)S(1)}, bf16[4,192,256]{2,1,0:T(8,128)(2,1)S(1)}, u32[]{:S(2)}, u32[]{:S(2)}) collective-permute-start(bf16[4,192,256]{2,1,0:T(8,128)(2,1)S(1)} %all-to-all-done.2.refs_0_), channel_id=1, source_target_pairs={{0,16},{8,24},{16,0},{24,8},{32,48},{40,56},{48,32},{56,40},{64,80... | collective-permute-start | bytes 1179656 | tf_op jit(solution)/shard_map/ppermute | solution.py:363
  59.2 13.3 %collective-permute-start.4 = (bf16[4,192,256]{2,1,0:T(8,128)(2,1)S(1)}, bf16[4,192,256]{2,1,0:T(8,128)(2,1)S(1)}, u32[]{:S(2)}, u32[]{:S(2)}) collective-permute-start(bf16[4,192,256]{2,1,0:T(8,128)(2,1)S(1)} %all-to-all-done.2.refs_0_), channel_id=1, source_target_pairs={{0,24},{8,0},{16,8},{24,16},{32,56},{40,32},{48,40},{56,48},{64,88... | collective-permute-start | bytes 1179656 | tf_op jit(solution)/shard_map/ppermute | solution.py:363
  74.4 9.5 %collective-permute-start.7 = (bf16[4,768,256]{2,1,0:T(8,128)(2,1)}, bf16[4,768,256]{2,1,0:T(8,128)(2,1)}, u32[]{:S(2)}, u32[]{:S(2)}) collective-permute-start(bf16[4,768,256]{2,1,0:T(8,128)(2,1)} %bitcast.15.rows_ref.refs_1_), channel_id=1, source_target_pairs={{0,1},{1,0},{2,3},{3,2},{4,5},{5,4},{6,7},{7,6},{8,9},{9,8},{10,11... | collective-permute-start | bytes 4718600 | tf_op jit(solution)/shard_map/ppermute | solution.py:446
  74.4 9.5 %collective-permute-start.3 = (bf16[4,768,256]{2,1,0:T(8,128)(2,1)}, bf16[4,768,256]{2,1,0:T(8,128)(2,1)}, u32[]{:S(2)}, u32[]{:S(2)}) collective-permute-start(bf16[4,768,256]{2,1,0:T(8,128)(2,1)} %all-to-all-done.1.rows_ref.refs_0_), channel_id=1, source_target_pairs={{0,1},{1,0},{2,3},{3,2},{4,5},{5,4},{6,7},{7,6},{8,9},{9,8},{10,11... | collective-permute-start | bytes 4718600 | tf_op jit(solution)/shard_map/ppermute | solution.py:448
  74.9 42.8 %copy-start.14 = (s32[4]{0:T(128)}, s32[4]{0:T(128)S(1)}, u32[]{:S(2)}) copy-start(s32[4]{0:T(128)S(1)} %add_subtract_fusion.block_ref) | copy-start | bytes 52
  89.0 26.3 %copy-start.4 = (f32[768,64]{0,1:T(8,128)S(1)}, f32[768,64]{0,1:T(8,128)}, u32[]{:S(2)}) copy-start(f32[768,64]{0,1:T(8,128)} %copy-done.3) | copy-start | bytes 589828
  89.0 1.3 collective-permute-start.8
  90.3 4.9 %collective-permute-start.11 = (f32[1,2304]{1,0:T(1,128)S(1)}, f32[1,2304]{1,0:T(1,128)S(1)}, u32[]{:S(2)}, u32[]{:S(2)}) collective-permute-start(f32[1,2304]{1,0:T(1,128)S(1)} %pad_maximum_fusion), channel_id=1, source_target_pairs={{0,2},{1,3},{2,4},{3,5},{4,6},{5,7},{6,0},{7,1},{8,10},{9,11},{10,... | collective-permute-start | bytes 27656 | tf_op jit(solution)/shard_map/ppermute | solution.py:367
  91.9 5.2 %collective-permute-start.10 = (f32[1,2304]{1,0:T(1,128)S(1)}, f32[1,2304]{1,0:T(1,128)S(1)}, u32[]{:S(2)}, u32[]{:S(2)}) collective-permute-start(f32[1,2304]{1,0:T(1,128)S(1)} %pad_maximum_fusion), channel_id=1, source_target_pairs={{0,4},{1,5},{2,6},{3,7},{4,0},{5,1},{6,2},{7,3},{8,12},{9,13},{10,... | collective-permute-start | bytes 27656 | tf_op jit(solution)/shard_map/ppermute | solution.py:367
  92.9 4.2 %collective-permute-start.9 = (f32[1,2304]{1,0:T(1,128)S(1)}, f32[1,2304]{1,0:T(1,128)S(1)}, u32[]{:S(2)}, u32[]{:S(2)}) collective-permute-start(f32[1,2304]{1,0:T(1,128)S(1)} %pad_maximum_fusion), channel_id=1, source_target_pairs={{0,6},{1,7},{2,0},{3,1},{4,2},{5,3},{6,4},{7,5},{8,14},{9,15},{10,... | collective-permute-start | bytes 27656 | tf_op jit(solution)/shard_map/ppermute | solution.py:367
  117.6 3.7 %collective-permute-start.12 = (bf16[4,768,256]{2,1,0:T(8,128)(2,1)S(1)}, bf16[4,768,256]{2,1,0:T(8,128)(2,1)S(1)}, u32[]{:S(2)}, u32[]{:S(2)}) collective-permute-start(bf16[4,768,256]{2,1,0:T(8,128)(2,1)S(1)} %get-tuple-element.30), channel_id=1, source_target_pairs={{0,1},{1,0},{2,3},{3,2},{4,5},{5,4},{6,7},{7,6},{8,9},{9,8},{10,11... | collective-permute-start | bytes 4718600 | tf_op jit(solution)/shard_map/ppermute | solution.py:457
  120.8 9.4 %collective-permute-start.13 = (bf16[4,768,256]{2,1,0:T(8,128)(2,1)}, bf16[4,768,256]{2,1,0:T(8,128)(2,1)}, u32[]{:S(2)}, u32[]{:S(2)}) collective-permute-start(bf16[4,768,256]{2,1,0:T(8,128)(2,1)} %grad_rest.1), channel_id=1, source_target_pairs={{0,1},{1,0},{2,3},{3,2},{4,5},{5,4},{6,7},{7,6},{8,9},{9,8},{10,11... | collective-permute-start | bytes 4718600 | tf_op jit(solution)/shard_map/ppermute | solution.py:458
  124.5 32.6 %all-to-all-start.4 = ((bf16[4,768,256]{2,1,0:T(8,128)(2,1)}), bf16[4,768,256]{2,1,0:T(8,128)(2,1)S(1)}, u32[]{:S(2)}, u32[]{:S(2)}) async-start(bf16[4,768,256]{2,1,0:T(8,128)(2,1)} %grad_first.1), calls=%async_computation.4 | async-start | bytes 3145728 | tf_op jit(solution)/shard_map/all_to_all | solution.py:359
  136.1 20.4 %collective-permute-start.14 = (bf16[4,192,256]{2,1,0:T(8,128)(2,1)S(1)}, bf16[4,192,256]{2,1,0:T(8,128)(2,1)S(1)}, u32[]{:S(2)}, u32[]{:S(2)}) collective-permute-start(bf16[4,192,256]{2,1,0:T(8,128)(2,1)S(1)} %get-tuple-element.33), channel_id=1, source_target_pairs={{0,8},{8,16},{16,24},{24,0},{32,40},{40,48},{48,56},{56,32},{64,72... | collective-permute-start | bytes 1179656 | tf_op jit(solution)/shard_map/ppermute | solution.py:363
  136.2 20.3 %collective-permute-start.16 = (bf16[4,192,256]{2,1,0:T(8,128)(2,1)S(1)}, bf16[4,192,256]{2,1,0:T(8,128)(2,1)S(1)}, u32[]{:S(2)}, u32[]{:S(2)}) collective-permute-start(bf16[4,192,256]{2,1,0:T(8,128)(2,1)S(1)} %get-tuple-element.34), channel_id=1, source_target_pairs={{0,16},{8,24},{16,0},{24,8},{32,48},{40,56},{48,32},{56,40},{64,80... | collective-permute-start | bytes 1179656 | tf_op jit(solution)/shard_map/ppermute | solution.py:363
  138.8 18.4 %collective-permute-start.15 = (bf16[4,192,256]{2,1,0:T(8,128)(2,1)S(1)}, bf16[4,192,256]{2,1,0:T(8,128)(2,1)S(1)}, u32[]{:S(2)}, u32[]{:S(2)}) collective-permute-start(bf16[4,192,256]{2,1,0:T(8,128)(2,1)S(1)} %get-tuple-element.35), channel_id=1, source_target_pairs={{0,24},{8,0},{16,8},{24,16},{32,56},{40,32},{48,40},{56,48},{64,88... | collective-permute-start | bytes 1179656 | tf_op jit(solution)/shard_map/ppermute | solution.py:363
  151.0 24.3 %copy-start.9 = (f32[288,192]{1,0:T(8,128)S(1)}, f32[288,192]{1,0:T(8,128)}, u32[]{:S(2)}) copy-start(f32[288,192]{1,0:T(8,128)} %copy-done.8) | copy-start | bytes 663556
  160.8 34.9 %copy-start.11 = (bf16[36,4096]{1,0:T(8,128)(2,1)S(1)}, bf16[36,4096]{1,0:T(8,128)(2,1)}, u32[]{:S(2)}) copy-start(bf16[36,4096]{1,0:T(8,128)(2,1)} %rows_ref.3) | copy-start | bytes 884740
  160.8 34.9 %copy-start.13 = (f32[4096]{0:T(1024)S(1)}, f32[4096]{0:T(1024)}, u32[]{:S(2)}) copy-start(f32[4096]{0:T(1024)} %param.8) | copy-start | bytes 49156
  160.8 34.9 %copy-start.17 = (f32[1,768]{1,0:T(1,128)S(1)}, f32[1,768]{1,0:T(1,128)}, u32[]{:S(2)}) copy-start(f32[1,768]{1,0:T(1,128)} %copy-done.16) | copy-start | bytes 9220
  160.8 14.5 %all-to-all-start.5 = ((bf16[4,192,256]{2,1,0:T(8,128)(2,1)}), bf16[4,192,256]{2,1,0:T(8,128)(2,1)S(1)}, u32[]{:S(2)}, u32[]{:S(2)}) async-start(bf16[4,192,256]{2,1,0:T(8,128)(2,1)} %get-tuple-element.44), calls=%async_computation.5 | async-start | bytes 786432 | tf_op jit(solution)/shard_map/all_to_all | solution.py:359
  165.8 6.0 %collective-permute-start.17 = (bf16[192,256]{1,0:T(8,128)(2,1)}, bf16[192,256]{1,0:T(8,128)(2,1)S(1)}, u32[]{:S(2)}, u32[]{:S(2)}) collective-permute-start(bf16[192,256]{1,0:T(8,128)(2,1)} %copy-done.22), channel_id=1, source_target_pairs={{0,8},{8,16},{16,24},{24,0},{32,40},{40,48},{48,56},{56,32},{64,72... | collective-permute-start | bytes 294920 | tf_op jit(solution)/shard_map/ppermute | solution.py:363
  166.5 6.0 %collective-permute-start.18 = (bf16[192,256]{1,0:T(8,128)(2,1)}, bf16[192,256]{1,0:T(8,128)(2,1)S(1)}, u32[]{:S(2)}, u32[]{:S(2)}) collective-permute-start(bf16[192,256]{1,0:T(8,128)(2,1)} %copy-done.21), channel_id=1, source_target_pairs={{0,24},{8,0},{16,8},{24,16},{32,56},{40,32},{48,40},{56,48},{64,88... | collective-permute-start | bytes 294920 | tf_op jit(solution)/shard_map/ppermute | solution.py:363
  169.0 6.3 %collective-permute-start.19 = (bf16[192,256]{1,0:T(8,128)(2,1)}, bf16[192,256]{1,0:T(8,128)(2,1)S(1)}, u32[]{:S(2)}, u32[]{:S(2)}) collective-permute-start(bf16[192,256]{1,0:T(8,128)(2,1)} %copy-done.20), channel_id=1, source_target_pairs={{0,16},{8,24},{16,0},{24,8},{32,48},{40,56},{48,32},{56,40},{64,80... | collective-permute-start | bytes 294920 | tf_op jit(solution)/shard_map/ppermute | solution.py:363
  (21 other events, 107.0 us)

commit v4 on v3

--- a/solution.py
+++ b/solution.py
@@ -224,32 +224,39 @@
         out_ref[k] = (out + other_ref[k].astype(f32)).astype(bf16)
 
 
-def split_kernel(block_ref, at_ref, turned_ref, weight_ref, other_ref, *refs, second):
+def own_kernel(block_ref, at_ref, turned_ref, weight_ref, first_ref, second_ref, out_ref, *refs):
+    add_kernel(block_ref, turned_ref, weight_ref, first_ref, out_ref, second=0)
     by_x, keep_ref = refs[:4], refs[4]
     rows = keep_ref.shape[2]
-    for y in range(other_ref.shape[0]):
-        out = dot(turned_ref[...], feature_part(weight_ref, block_ref, y, second))
-        out = (out + other_ref[y].astype(f32)).astype(bf16)
+    for y in range(second_ref.shape[0]):
+        out = dot(turned_ref[...], feature_part(weight_ref, block_ref, y, 1))
+        out = (out + second_ref[y].astype(f32)).astype(bf16)
         for k in range(4):
             keep_ref[k, y] = out[k * rows : (k + 1) * rows]
     for k in range(4):
         by_x[k][...] = keep_ref[(at_ref[0] + k) % 4]
 
 
-def half_call(body, name, blocks, second, turned, weight, *other, at=None):
+def rest_call(blocks, turned, weight):
     tokens, width = turned.shape
     count = blocks.shape[0]
     half = weight.shape[1] // (4 * count)
+    return call(
+        functools.partial(rest_kernel, second=1), "grad_rest", array((count, tokens, half), bf16), turned, weight,
+        prefetch=(blocks,), flops=2 * count * tokens * half * width, size=6 * 2**20,
+    )
+
+
+def own_call(blocks, at, turned, weight, first, second):
+    tokens, width = turned.shape
+    count, _, half = first.shape
     rows = tokens // NX
     inside = pl.BlockSpec(memory_space=pltpu.VMEM)
-    if at is None:
-        out, outs, scratch, prefetch = array((count, tokens, half), bf16), inside, (), (blocks,)
-    else:
-        out, outs = [array((count, rows, half), bf16)] * 4, [inside] * 4
-        scratch, prefetch = [pltpu.VMEM((NX, count, rows, half), bf16)], (blocks, at)
-    return call(
-        functools.partial(body, second=second), name, out, turned, weight, *other, prefetch=prefetch, scratch=scratch,
-        ins=[inside] * (2 + len(other)), outs=outs, flops=2 * count * tokens * half * width, size=6 * 2**20,
+    return call(
+        own_kernel, "grad_own", [array(first.shape, bf16)] + [array((count, rows, half), bf16)] * 4,
+        turned, weight, first, second, prefetch=(blocks, at), ins=[inside] * 4, outs=[inside] * 5,
+        scratch=[pltpu.VMEM((NX, count, rows, half), bf16)],
+        flops=4 * count * tokens * half * width, size=12 * 2**20,
     )
 
 
@@ -455,10 +462,9 @@
 
     grad, turned, rest_first = grad_call(rest_blocks, stats, logits, dense, logprob, weight)
     other_first = lax.ppermute(rest_first, "vocab", OTHER_CORE)
-    other_second = lax.ppermute(half_call(rest_kernel, "grad_rest", rest_blocks, 1, turned, weight), "vocab", OTHER_CORE)
-    first = half_call(add_kernel, "grad_first", own_blocks, 0, turned, weight, other_first)
+    other_second = lax.ppermute(rest_call(rest_blocks, turned, weight), "vocab", OTHER_CORE)
+    first, *pieces = own_call(own_blocks, at, turned, weight, other_first, other_second)
     by_y = exchange(first, "vocab", Y_LINES)
-    pieces = half_call(split_kernel, "grad_second", after(own_blocks, first), 1, turned, weight, other_second, at=at)
     by_x = to_ahead(pieces, along_x)
     weight_t = weight_grad(after(jnp.concatenate([own_blocks, rest_blocks]), pieces), own_rows, rest_rows, grad)
     kl, dots = call(tokens_kernel, "tokens", [array((1, tokens), f32)] * 2, stats, logprob, size=2**19)

time: 198 us -> 200 us (1.010)
  waiting for transfers between devices: 37.8 us -> 41.9 us
  Pallas kernels: 51.4 us -> 47.8 us
    pallas_call x16 -> x15, Pallas kernels: 51.4 us -> 47.8 us  [call(): pl.pallas_call(body, grid_spec=pltpu.PrefetchScalarGridSpec(num_scalar_pr...]
    ppermute x1, waiting for transfers between devices: 0.01 us -> 2.9 us  [per_device(): lax.ppermute(rest_call(rest_blocks, turned, weight), 'vocab', OTHER_CORE)]
    ppermute x1, waiting for transfers between devices: 0.01 us -> 2.25 us  [per_device(): other_first = lax.ppermute(rest_first, 'vocab', OTHER_CORE)]
    unnamed x59 -> x43, local copies, waits for them, and re-layouts: 9.93 us -> 11.5 us
  transfers between devices with their start and end apart: 25 -> 25, of which waited for: 13 -> 15; matrix products, arithmetic and copies ran while one was open for 1% -> 1% of each run, Pallas kernels for 19% -> 14%
where the time goes in v4:
time: 200 us; the launch traced here: 199 us
  starting transfers between devices  55.4 us (28%)
  Pallas kernels  47.8 us (24%)
  waiting for transfers between devices  41.9 us (21%)
  blocking collectives  37.9 us (19%)
  local copies, waits for them, and re-layouts  14.4 us (7%)
    pallas_call x15, Pallas kernels, call(): pl.pallas_call(body, grid_spec=pltpu.PrefetchScalarGridSpec(num_scalar_pr...  47.8 us
    all_to_all x2, blocking collectives, exchange(): return lax.all_to_all(x, axis, 0, 0, tiled=True, axis_index_groups=lines)  37.9 us
    all_to_all x5, starting transfers between devices, exchange(): return lax.all_to_all(x, axis, 0, 0, tiled=True, axis_index_groups=lines)  31.5 us
    ppermute x12, waiting for transfers between devices, along_x(): lax.ppermute(x, 'seq', [(i, i // NX * NX + (i + k) % NX) for i in range(G...  26.6 us
    ppermute x12, starting transfers between devices, along_x(): lax.ppermute(x, 'seq', [(i, i // NX * NX + (i + k) % NX) for i in range(G...  17.8 us
    unnamed x43, local copies, waits for them, and re-layouts  11.5 us
    all_to_all x5, waiting for transfers between devices, exchange(): return lax.all_to_all(x, axis, 0, 0, tiled=True, axis_index_groups=lines)  7.2 us
    ppermute x3, starting transfers between devices, along_y(): lax.ppermute(x, 'vocab', [(i, (i + 2 * k) % (2 * NY)) for i in range(2 *...  4.91 us
  transfers between devices with their start and end apart: 25, of which 15 were waited for; matrix products, arithmetic and copies ran while one was open for 1% of the time, Pallas kernels for 14%

profile of v4, /device:TPU:8, one launch (start us, length us, event | category | flops | bytes accessed | tf_op | source)
XLA Modules:
  0.0 199.2 jit_solution(15746772458125883300)
XLA Ops:
  3.1 1.8 sort_rows.1
  5.0 11.4 %all-to-all-start = ((bf16[32,9,512]{2,1,0:T(8,128)(2,1)}), bf16[32,9,512]{2,1,0:T(8,128)(2,1)S(1)}, u32[]{:S(2)}, u32[]{:S(2)}) async-start(bf16[32,9,512]{2,1,0:T(8,128)(2,1)} %sort_rows.1), calls=%async_computation | async-start | bytes 1048576 | tf_op jit(solution)/shard_map/all_to_all | solution.py:366
  17.3 9.3 %teacher_columns.1.dense_ref = f32[594,768]{1,0:T(8,128)S(1)} custom-call(s32[1]{0:T(128)} %bitcast.4.first_ref, s32[64,768]{1,0:T(8,128)S(1)} %bitcast.40, f32[64,768]{1,0:T(8,128)S(1)} %bitcast.35), custom_call_target="tpu_custom_call" | custom-call | flops 116785152 | bytes 1824768 | tf_op jit(solution)/shard_map/teacher_columns/pallas_call | solution.py:26
  26.9 7.2 %all-to-all-done = bf16[32,9,512]{2,1,0:T(8,128)(2,1)S(1)} async-done(((bf16[32,9,512]{2,1,0:T(8,128)(2,1)}), bf16[32,9,512]{2,1,0:T(8,128)(2,1)S(1)}, u32[]{:S(2)}, u32[]{:S(2)}) %all-to-all-start) | async-done | bytes 294944 | tf_op jit(solution)/shard_map/all_to_all | solution.py:366
  35.4 4.9 %all-to-all-start.2 = ((bf16[4,192,256]{2,1,0:T(8,128)(2,1)}), bf16[4,192,256]{2,1,0:T(8,128)(2,1)S(1)}, u32[]{:S(2)}, u32[]{:S(2)}) async-start(bf16[4,192,256]{2,1,0:T(8,128)(2,1)} %broadcast_in_dim.40), calls=%async_computation.2 | async-start | bytes 786432 | tf_op jit(solution)/shard_map/all_to_all | solution.py:366
  41.2 2.7 %collective-permute-start.1 = (bf16[192,256]{1,0:T(8,128)(2,1)S(1)}, bf16[192,256]{1,0:T(8,128)(2,1)S(1)}, u32[]{:S(2)}, u32[]{:S(2)}) collective-permute-start(bf16[192,256]{1,0:T(8,128)(2,1)S(1)} %get-tuple-element.46.refs_0_), channel_id=1, source_target_pairs={{0,16},{8,24},{16,0},{24,8},{32,48},{40,56},{48,32},{56,40},{64,80... | collective-permute-start | bytes 294920 | tf_op jit(solution)/shard_map/ppermute | solution.py:370
  50.3 4.8 %all-to-all-start.1 = ((bf16[4,768,256]{2,1,0:T(8,128)(2,1)}), bf16[4,768,256]{2,1,0:T(8,128)(2,1)}, u32[]{:S(2)}, u32[]{:S(2)}) async-start(bf16[4,768,256]{2,1,0:T(8,128)(2,1)} %bitcast.34), calls=%async_computation.1 | async-start | bytes 3145728 | tf_op jit(solution)/shard_map/all_to_all | solution.py:366
  56.5 2.8 %collective-permute-start.5 = (bf16[4,192,256]{2,1,0:T(8,128)(2,1)S(1)}, bf16[4,192,256]{2,1,0:T(8,128)(2,1)S(1)}, u32[]{:S(2)}, u32[]{:S(2)}) collective-permute-start(bf16[4,192,256]{2,1,0:T(8,128)(2,1)S(1)} %all-to-all-done.2.refs_0_), channel_id=1, source_target_pairs={{0,16},{8,24},{16,0},{24,8},{32,48},{40,56},{48,32},{56,40},{64,80... | collective-permute-start | bytes 1179656 | tf_op jit(solution)/shard_map/ppermute | solution.py:370
  59.7 8.6 %collective-permute-done.6.refs_3_ = bf16[4,192,256]{2,1,0:T(8,128)(2,1)S(1)} collective-permute-done((bf16[4,192,256]{2,1,0:T(8,128)(2,1)S(1)}, bf16[4,192,256]{2,1,0:T(8,128)(2,1)S(1)}, u32[]{:S(2)}, u32[]{:S(2)}) %collective-permute-start.6) | collective-permute-done | bytes 393248 | tf_op jit(solution)/shard_map/ppermute | solution.py:370
  68.3 4.3 %collective-permute-done.5.refs_2_ = bf16[4,192,256]{2,1,0:T(8,128)(2,1)S(1)} collective-permute-done((bf16[4,192,256]{2,1,0:T(8,128)(2,1)S(1)}, bf16[4,192,256]{2,1,0:T(8,128)(2,1)S(1)}, u32[]{:S(2)}, u32[]{:S(2)}) %collective-permute-start.5) | collective-permute-done | bytes 393248 | tf_op jit(solution)/shard_map/ppermute | solution.py:370
  73.6 1.8 gather_rows.1
  75.9 2.4 %copy-done = bf16[4096,594]{0,1:T(8,128)(2,1)S(1)} copy-done((bf16[4096,594]{0,1:T(8,128)(2,1)S(1)}, bf16[4096,594]{0,1:T(8,128)(2,1)}, u32[]{:S(2)}) %copy-start) | copy-done | bytes 4866072
  78.3 3.4 %logits_half.2.refs_0_ = f32[594,768]{1,0:T(8,128)S(1)} custom-call(s32[4]{0:T(128)S(1)} %fusion.21.block_ref, bf16[4,768,256]{2,1,0:T(8,128)(2,1)} %bitcast.15.rows_ref.refs_1_, bf16[594,4096]{1,0:T(8,128)(2,1)S(1)} %bitcast.26), custom_call_target="tpu_custom_call" | custom-call | flops 934281216 | bytes 6291456 | tf_op jit(solution)/shard_map/logits_half/pallas_call | solution.py:26
  81.7 3.1 %logits_half.3.own_ref = f32[594,768]{1,0:T(8,128)S(1)} custom-call(s32[4]{0:T(128)S(1)} %fusion.21.block_ref, bf16[4,768,256]{2,1,0:T(8,128)(2,1)} %all-to-all-done.1.rows_ref.refs_0_, bf16[594,4096]{1,0:T(8,128)(2,1)S(1)} %bitcast.29, f32[594,768]{1,0:T(8,128)S(1)} %logits_half.2.refs_0_), custom_call_target="tpu_custom_call" | custom-call | flops 934281216 | bytes 6291456 | tf_op jit(solution)/shard_map/logits_half/pallas_call | solution.py:26
  84.9 5.1 %logits_rest.1 = (f32[594,768]{1,0:T(8,128)S(1)}, f32[1,2304]{1,0:T(1,128)S(1)}) custom-call(s32[4]{0:T(128)S(1)} %add_subtract_fusion.block_ref, bf16[4,768,256]{2,1,0:T(8,128)(2,1)} %collective-permute-done.3.first_ref.refs_2_, bf16[4,768,256]{2,1,0:T(8,128)(2,1)} %collective-permute-done.7.second_ref.refs_3_, bf16[594,4096]{1,0:T(8,128)(2,1)S(1)} %bitcast.30, ...), custom_call_target="tpu_custom_call" | custom-call | flops 1868562432 | bytes 8388608 | tf_op jit(solution)/shard_map/logits_rest/pallas_call | solution.py:26
  93.9 2.4 %collective-permute-start.9 = (f32[1,2304]{1,0:T(1,128)S(1)}, f32[1,2304]{1,0:T(1,128)S(1)}, u32[]{:S(2)}, u32[]{:S(2)}) collective-permute-start(f32[1,2304]{1,0:T(1,128)S(1)} %pad_maximum_fusion), channel_id=1, source_target_pairs={{0,6},{1,7},{2,0},{3,1},{4,2},{5,3},{6,4},{7,5},{8,14},{9,15},{10,... | collective-permute-start | bytes 27656 | tf_op jit(solution)/shard_map/ppermute | solution.py:374
  98.3 18.0 %all_to_all.38 = f32[32,1,2304]{2,1,0:T(1,128)S(1)} all-to-all(f32[32,1,2304]{2,1,0:T(1,128)S(1)} %broadcast_in_dim.41), channel_id=1, replica_groups=mesh['seq'=32,'vocab'=8] {'seq'}, dimensions={0} | all-to-all | bytes 589824 | tf_op jit(solution)/shard_map/all_to_all | solution.py:366
  116.3 2.3 %grad_logits.1 = (bf16[594,768]{1,0:T(8,128)(2,1)S(1)}, bf16[768,594]{1,0:T(8,128)(2,1)S(1)}, bf16[4,768,256]{2,1,0:T(8,128)(2,1)S(1)}) custom-call(s32[4]{0:T(128)S(1)} %add_subtract_fusion.block_ref, f32[32,2304]{1,0:T(8,128)S(1)} %bitcast.38, f32[594,768]{1,0:T(8,128)S(1)} %get-tuple-element.28.logits_ref, f32[594,768]{1,0:T(8,128)S(1)} %teacher_columns.1.dense_ref, ...), custom_call_target="tpu_custom_call" | custom-call | flops 934281216 | bytes 12582912 | tf_op jit(solution)/shard_map/grad_logits/pallas_call | solution.py:26
  118.6 1.9 grad_rest.1
  121.2 2.9 %collective-permute-done.13.second_ref = bf16[4,768,256]{2,1,0:T(8,128)(2,1)S(1)} collective-permute-done((bf16[4,768,256]{2,1,0:T(8,128)(2,1)S(1)}, bf16[4,768,256]{2,1,0:T(8,128)(2,1)S(1)}, u32[]{:S(2)}, u32[]{:S(2)}) %collective-permute-start.13) | collective-permute-done | bytes 1572896 | tf_op jit(solution)/shard_map/ppermute | solution.py:465
  124.1 2.2 %collective-permute-done.12.first_ref = bf16[4,768,256]{2,1,0:T(8,128)(2,1)S(1)} collective-permute-done((bf16[4,768,256]{2,1,0:T(8,128)(2,1)S(1)}, bf16[4,768,256]{2,1,0:T(8,128)(2,1)S(1)}, u32[]{:S(2)}, u32[]{:S(2)}) %collective-permute-start.12) | collective-permute-done | bytes 1572896 | tf_op jit(solution)/shard_map/ppermute | solution.py:464
  126.3 4.3 %grad_own.1 = (bf16[4,768,256]{2,1,0:T(8,128)(2,1)S(1)}, bf16[4,192,256]{2,1,0:T(8,128)(2,1)S(1)}, bf16[4,192,256]{2,1,0:T(8,128)(2,1)}, bf16[4,192,256]{2,1,0:T(8,128)(2,1)}, bf16[4,192,256]{2,1,0:T(8,128)(2,1)}) custom-call(s32[4]{0:T(128)S(1)} %fusion.21.block_ref, s32[36]{0:T(128)S(1)} %concatenate.14.at_ref, ...), custom_call_target="tpu_custom_call" | custom-call | flops 1868562432 | bytes 12582912 | tf_op jit(solution)/shard_map/grad_own/pallas_call | solution.py:26
  132.5 5.4 %all-to-all-start.4 = ((bf16[4,768,256]{2,1,0:T(8,128)(2,1)}), bf16[4,768,256]{2,1,0:T(8,128)(2,1)S(1)}, u32[]{:S(2)}, u32[]{:S(2)}) async-start(bf16[4,768,256]{2,1,0:T(8,128)(2,1)} %copy-done.2), calls=%async_computation.4 | async-start | bytes 3145728 | tf_op jit(solution)/shard_map/all_to_all | solution.py:366
  138.2 2.5 %collective-permute-start.16 = (bf16[4,192,256]{2,1,0:T(8,128)(2,1)}, bf16[4,192,256]{2,1,0:T(8,128)(2,1)S(1)}, u32[]{:S(2)}, u32[]{:S(2)}) collective-permute-start(bf16[4,192,256]{2,1,0:T(8,128)(2,1)} %get-tuple-element.33), channel_id=1, source_target_pairs={{0,16},{8,24},{16,0},{24,8},{32,48},{40,56},{48,32},{56,40},{64,80... | collective-permute-start | bytes 1179656 | tf_op jit(solution)/shard_map/ppermute | solution.py:370
  143.9 10.2 %weight_grad.1 = bf16[594,4096]{1,0:T(8,128)(2,1)} custom-call(s32[8]{0:T(128)S(1)} %pad_add_fusion.block_ref, bf16[4,768,256]{2,1,0:T(8,128)(2,1)} %all-to-all-done.1.rows_ref.refs_0_, bf16[4,768,256]{2,1,0:T(8,128)(2,1)} %bitcast.15.rows_ref.refs_1_, bf16[4,768,256]{2,1,0:T(8,128)(2,1)} %collective-permute-done.3.first_ref.refs_2_, ...), custom_call_target="tpu_custom_call" | custom-call | flops 3737124864 | bytes 16777216 | tf_op jit(solution)/shard_map/weight_grad/pallas_call | solution.py:26
  154.1 4.7 %collective-permute-done.14.refs_1_ = bf16[4,192,256]{2,1,0:T(8,128)(2,1)S(1)} collective-permute-done((bf16[4,192,256]{2,1,0:T(8,128)(2,1)}, bf16[4,192,256]{2,1,0:T(8,128)(2,1)S(1)}, u32[]{:S(2)}, u32[]{:S(2)}) %collective-permute-start.14) | collective-permute-done | bytes 393248 | tf_op jit(solution)/shard_map/ppermute | solution.py:370
  161.1 1.8 add_pieces.1
  162.9 4.9 %all-to-all-start.5 = ((bf16[4,192,256]{2,1,0:T(8,128)(2,1)}), bf16[4,192,256]{2,1,0:T(8,128)(2,1)S(1)}, u32[]{:S(2)}, u32[]{:S(2)}) async-start(bf16[4,192,256]{2,1,0:T(8,128)(2,1)} %get-tuple-element.44), calls=%async_computation.5 | async-start | bytes 786432 | tf_op jit(solution)/shard_map/all_to_all | solution.py:366
  168.6 2.5 %collective-permute-start.18 = (bf16[192,256]{1,0:T(8,128)(2,1)S(1)}, bf16[192,256]{1,0:T(8,128)(2,1)S(1)}, u32[]{:S(2)}, u32[]{:S(2)}) collective-permute-start(bf16[192,256]{1,0:T(8,128)(2,1)S(1)} %get-tuple-element.42), channel_id=1, source_target_pairs={{0,24},{8,0},{16,8},{24,16},{32,56},{40,32},{48,40},{56,48},{64,88... | collective-permute-start | bytes 294920 | tf_op jit(solution)/shard_map/ppermute | solution.py:370
  172.0 2.1 %collective-permute-done.17.refs_1_ = bf16[192,256]{1,0:T(8,128)(2,1)S(1)} collective-permute-done((bf16[192,256]{1,0:T(8,128)(2,1)}, bf16[192,256]{1,0:T(8,128)(2,1)S(1)}, u32[]{:S(2)}, u32[]{:S(2)}) %collective-permute-start.17) | collective-permute-done | bytes 98336 | tf_op jit(solution)/shard_map/ppermute | solution.py:370
  174.3 3.0 %collective-permute-done.19.refs_3_ = bf16[192,256]{1,0:T(8,128)(2,1)S(1)} collective-permute-done((bf16[192,256]{1,0:T(8,128)(2,1)S(1)}, bf16[192,256]{1,0:T(8,128)(2,1)S(1)}, u32[]{:S(2)}, u32[]{:S(2)}) %collective-permute-start.19) | collective-permute-done | bytes 98336 | tf_op jit(solution)/shard_map/ppermute | solution.py:370
  177.7 19.9 %all_to_all.39.got_ref = bf16[32,9,512]{2,1,0:T(8,128)(2,1)S(1)} all-to-all(bf16[32,9,512]{2,1,0:T(8,128)(2,1)S(1)} %spread_rows.1), channel_id=1, replica_groups=mesh['seq'=32,'vocab'=8] {'seq'}, dimensions={0} | all-to-all | bytes 589824 | tf_op jit(solution)/shard_map/all_to_all | solution.py:366
  (103 shorter events, 33.6 us)
Async XLA Ops:
  0.6 15.8 %copy-start.17 = (s32[32]{0:T(128)S(1)}, s32[32]{0:T(128)}, u32[]{:S(2)}) copy-start(s32[32]{0:T(128)} %param.7) | copy-start | bytes 388
  3.1 13.4 %copy-start.15 = (s32[768,64]{0,1:T(8,128)S(1)}, s32[768,64]{0,1:T(8,128)}, u32[]{:S(2)}) copy-start(s32[768,64]{0,1:T(8,128)} %param.10) | copy-start | bytes 589828
  5.0 12.0 %copy-start.16 = (f32[768,64]{0,1:T(8,128)S(1)}, f32[768,64]{0,1:T(8,128)}, u32[]{:S(2)}) copy-start(f32[768,64]{0,1:T(8,128)} %param.11) | copy-start | bytes 589828
  5.0 29.2 %all-to-all-start = ((bf16[32,9,512]{2,1,0:T(8,128)(2,1)}), bf16[32,9,512]{2,1,0:T(8,128)(2,1)S(1)}, u32[]{:S(2)}, u32[]{:S(2)}) async-start(bf16[32,9,512]{2,1,0:T(8,128)(2,1)} %sort_rows.1), calls=%async_computation | async-start | bytes 1048576 | tf_op jit(solution)/shard_map/all_to_all | solution.py:366
  35.4 14.9 %all-to-all-start.2 = ((bf16[4,192,256]{2,1,0:T(8,128)(2,1)}), bf16[4,192,256]{2,1,0:T(8,128)(2,1)S(1)}, u32[]{:S(2)}, u32[]{:S(2)}) async-start(bf16[4,192,256]{2,1,0:T(8,128)(2,1)} %broadcast_in_dim.40), calls=%async_computation.2 | async-start | bytes 786432 | tf_op jit(solution)/shard_map/all_to_all | solution.py:366
  40.3 5.8 %collective-permute-start.2 = (bf16[192,256]{1,0:T(8,128)(2,1)S(1)}, bf16[192,256]{1,0:T(8,128)(2,1)S(1)}, u32[]{:S(2)}, u32[]{:S(2)}) collective-permute-start(bf16[192,256]{1,0:T(8,128)(2,1)S(1)} %get-tuple-element.46.refs_0_), channel_id=1, source_target_pairs={{0,8},{8,16},{16,24},{24,0},{32,40},{40,48},{48,56},{56,32},{64,72... | collective-permute-start | bytes 294920 | tf_op jit(solution)/shard_map/ppermute | solution.py:370
  41.2 6.3 %collective-permute-start.1 = (bf16[192,256]{1,0:T(8,128)(2,1)S(1)}, bf16[192,256]{1,0:T(8,128)(2,1)S(1)}, u32[]{:S(2)}, u32[]{:S(2)}) collective-permute-start(bf16[192,256]{1,0:T(8,128)(2,1)S(1)} %get-tuple-element.46.refs_0_), channel_id=1, source_target_pairs={{0,16},{8,24},{16,0},{24,8},{32,48},{40,56},{48,32},{56,40},{64,80... | collective-permute-start | bytes 294920 | tf_op jit(solution)/shard_map/ppermute | solution.py:370
  43.9 4.6 %collective-permute-start = (bf16[192,256]{1,0:T(8,128)(2,1)S(1)}, bf16[192,256]{1,0:T(8,128)(2,1)S(1)}, u32[]{:S(2)}, u32[]{:S(2)}) collective-permute-start(bf16[192,256]{1,0:T(8,128)(2,1)S(1)} %get-tuple-element.46.refs_0_), channel_id=1, source_target_pairs={{0,24},{8,0},{16,8},{24,16},{32,56},{40,32},{48,40},{56,48},{64,88... | collective-permute-start | bytes 294920 | tf_op jit(solution)/shard_map/ppermute | solution.py:370
  50.3 8.9 %copy-start.3 = (bf16[4,192,256]{2,1,0:T(8,128)(2,1)}, bf16[4,192,256]{2,1,0:T(8,128)(2,1)S(1)}, u32[]{:S(2)}) copy-start(bf16[4,192,256]{2,1,0:T(8,128)(2,1)S(1)} %all-to-all-done.2.refs_0_) | copy-start | bytes 1179652
  50.3 25.1 %all-to-all-start.1 = ((bf16[4,768,256]{2,1,0:T(8,128)(2,1)}), bf16[4,768,256]{2,1,0:T(8,128)(2,1)}, u32[]{:S(2)}, u32[]{:S(2)}) async-start(bf16[4,768,256]{2,1,0:T(8,128)(2,1)} %bitcast.34), calls=%async_computation.1 | async-start | bytes 3145728 | tf_op jit(solution)/shard_map/all_to_all | solution.py:366
  55.1 13.2 %collective-permute-start.6 = (bf16[4,192,256]{2,1,0:T(8,128)(2,1)S(1)}, bf16[4,192,256]{2,1,0:T(8,128)(2,1)S(1)}, u32[]{:S(2)}, u32[]{:S(2)}) collective-permute-start(bf16[4,192,256]{2,1,0:T(8,128)(2,1)S(1)} %all-to-all-done.2.refs_0_), channel_id=1, source_target_pairs={{0,8},{8,16},{16,24},{24,0},{32,40},{40,48},{48,56},{56,32},{64,72... | collective-permute-start | bytes 1179656 | tf_op jit(solution)/shard_map/ppermute | solution.py:370
  56.5 16.1 %collective-permute-start.5 = (bf16[4,192,256]{2,1,0:T(8,128)(2,1)S(1)}, bf16[4,192,256]{2,1,0:T(8,128)(2,1)S(1)}, u32[]{:S(2)}, u32[]{:S(2)}) collective-permute-start(bf16[4,192,256]{2,1,0:T(8,128)(2,1)S(1)} %all-to-all-done.2.refs_0_), channel_id=1, source_target_pairs={{0,16},{8,24},{16,0},{24,8},{32,48},{40,56},{48,32},{56,40},{64,80... | collective-permute-start | bytes 1179656 | tf_op jit(solution)/shard_map/ppermute | solution.py:370
  59.2 13.3 %collective-permute-start.4 = (bf16[4,192,256]{2,1,0:T(8,128)(2,1)S(1)}, bf16[4,192,256]{2,1,0:T(8,128)(2,1)S(1)}, u32[]{:S(2)}, u32[]{:S(2)}) collective-permute-start(bf16[4,192,256]{2,1,0:T(8,128)(2,1)S(1)} %all-to-all-done.2.refs_0_), channel_id=1, source_target_pairs={{0,24},{8,0},{16,8},{24,16},{32,56},{40,32},{48,40},{56,48},{64,88... | collective-permute-start | bytes 1179656 | tf_op jit(solution)/shard_map/ppermute | solution.py:370
  75.4 9.5 %collective-permute-start.7 = (bf16[4,768,256]{2,1,0:T(8,128)(2,1)}, bf16[4,768,256]{2,1,0:T(8,128)(2,1)}, u32[]{:S(2)}, u32[]{:S(2)}) collective-permute-start(bf16[4,768,256]{2,1,0:T(8,128)(2,1)} %bitcast.15.rows_ref.refs_1_), channel_id=1, source_target_pairs={{0,1},{1,0},{2,3},{3,2},{4,5},{5,4},{6,7},{7,6},{8,9},{9,8},{10,11... | collective-permute-start | bytes 4718600 | tf_op jit(solution)/shard_map/ppermute | solution.py:453
  75.4 9.5 %collective-permute-start.3 = (bf16[4,768,256]{2,1,0:T(8,128)(2,1)}, bf16[4,768,256]{2,1,0:T(8,128)(2,1)}, u32[]{:S(2)}, u32[]{:S(2)}) collective-permute-start(bf16[4,768,256]{2,1,0:T(8,128)(2,1)} %all-to-all-done.1.rows_ref.refs_0_), channel_id=1, source_target_pairs={{0,1},{1,0},{2,3},{3,2},{4,5},{5,4},{6,7},{7,6},{8,9},{9,8},{10,11... | collective-permute-start | bytes 4718600 | tf_op jit(solution)/shard_map/ppermute | solution.py:455
  90.0 1.3 collective-permute-start.8
  91.3 4.9 %collective-permute-start.11 = (f32[1,2304]{1,0:T(1,128)S(1)}, f32[1,2304]{1,0:T(1,128)S(1)}, u32[]{:S(2)}, u32[]{:S(2)}) collective-permute-start(f32[1,2304]{1,0:T(1,128)S(1)} %pad_maximum_fusion), channel_id=1, source_target_pairs={{0,2},{1,3},{2,4},{3,5},{4,6},{5,7},{6,0},{7,1},{8,10},{9,11},{10,... | collective-permute-start | bytes 27656 | tf_op jit(solution)/shard_map/ppermute | solution.py:374
  92.9 5.2 %collective-permute-start.10 = (f32[1,2304]{1,0:T(1,128)S(1)}, f32[1,2304]{1,0:T(1,128)S(1)}, u32[]{:S(2)}, u32[]{:S(2)}) collective-permute-start(f32[1,2304]{1,0:T(1,128)S(1)} %pad_maximum_fusion), channel_id=1, source_target_pairs={{0,4},{1,5},{2,6},{3,7},{4,0},{5,1},{6,2},{7,3},{8,12},{9,13},{10,... | collective-permute-start | bytes 27656 | tf_op jit(solution)/shard_map/ppermute | solution.py:374
  93.9 4.2 %collective-permute-start.9 = (f32[1,2304]{1,0:T(1,128)S(1)}, f32[1,2304]{1,0:T(1,128)S(1)}, u32[]{:S(2)}, u32[]{:S(2)}) collective-permute-start(f32[1,2304]{1,0:T(1,128)S(1)} %pad_maximum_fusion), channel_id=1, source_target_pairs={{0,6},{1,7},{2,0},{3,1},{4,2},{5,3},{6,4},{7,5},{8,14},{9,15},{10,... | collective-permute-start | bytes 27656 | tf_op jit(solution)/shard_map/ppermute | solution.py:374
  120.6 3.5 %collective-permute-start.13 = (bf16[4,768,256]{2,1,0:T(8,128)(2,1)S(1)}, bf16[4,768,256]{2,1,0:T(8,128)(2,1)S(1)}, u32[]{:S(2)}, u32[]{:S(2)}) collective-permute-start(bf16[4,768,256]{2,1,0:T(8,128)(2,1)S(1)} %grad_rest.1), channel_id=1, source_target_pairs={{0,1},{1,0},{2,3},{3,2},{4,5},{5,4},{6,7},{7,6},{8,9},{9,8},{10,11... | collective-permute-start | bytes 4718600 | tf_op jit(solution)/shard_map/ppermute | solution.py:465
  120.7 5.6 %collective-permute-start.12 = (bf16[4,768,256]{2,1,0:T(8,128)(2,1)S(1)}, bf16[4,768,256]{2,1,0:T(8,128)(2,1)S(1)}, u32[]{:S(2)}, u32[]{:S(2)}) collective-permute-start(bf16[4,768,256]{2,1,0:T(8,128)(2,1)S(1)} %get-tuple-element.30), channel_id=1, source_target_pairs={{0,1},{1,0},{2,3},{3,2},{4,5},{5,4},{6,7},{7,6},{8,9},{9,8},{10,11... | collective-permute-start | bytes 4718600 | tf_op jit(solution)/shard_map/ppermute | solution.py:464
  132.5 27.6 %all-to-all-start.4 = ((bf16[4,768,256]{2,1,0:T(8,128)(2,1)}), bf16[4,768,256]{2,1,0:T(8,128)(2,1)S(1)}, u32[]{:S(2)}, u32[]{:S(2)}) async-start(bf16[4,768,256]{2,1,0:T(8,128)(2,1)} %copy-done.2), calls=%async_computation.4 | async-start | bytes 3145728 | tf_op jit(solution)/shard_map/all_to_all | solution.py:366
  138.1 20.7 %collective-permute-start.14 = (bf16[4,192,256]{2,1,0:T(8,128)(2,1)}, bf16[4,192,256]{2,1,0:T(8,128)(2,1)S(1)}, u32[]{:S(2)}, u32[]{:S(2)}) collective-permute-start(bf16[4,192,256]{2,1,0:T(8,128)(2,1)} %get-tuple-element.32), channel_id=1, source_target_pairs={{0,8},{8,16},{16,24},{24,0},{32,40},{40,48},{48,56},{56,32},{64,72... | collective-permute-start | bytes 1179656 | tf_op jit(solution)/shard_map/ppermute | solution.py:370
  138.2 20.6 %collective-permute-start.16 = (bf16[4,192,256]{2,1,0:T(8,128)(2,1)}, bf16[4,192,256]{2,1,0:T(8,128)(2,1)S(1)}, u32[]{:S(2)}, u32[]{:S(2)}) collective-permute-start(bf16[4,192,256]{2,1,0:T(8,128)(2,1)} %get-tuple-element.33), channel_id=1, source_target_pairs={{0,16},{8,24},{16,0},{24,8},{32,48},{40,56},{48,32},{56,40},{64,80... | collective-permute-start | bytes 1179656 | tf_op jit(solution)/shard_map/ppermute | solution.py:370
  140.7 18.7 %collective-permute-start.15 = (bf16[4,192,256]{2,1,0:T(8,128)(2,1)}, bf16[4,192,256]{2,1,0:T(8,128)(2,1)S(1)}, u32[]{:S(2)}, u32[]{:S(2)}) collective-permute-start(bf16[4,192,256]{2,1,0:T(8,128)(2,1)} %get-tuple-element.34), channel_id=1, source_target_pairs={{0,24},{8,0},{16,8},{24,16},{32,56},{40,32},{48,40},{56,48},{64,88... | collective-permute-start | bytes 1179656 | tf_op jit(solution)/shard_map/ppermute | solution.py:370
  143.9 16.2 %copy-start.8 = (bf16[4,192,256]{2,1,0:T(8,128)(2,1)S(1)}, bf16[4,192,256]{2,1,0:T(8,128)(2,1)}, u32[]{:S(2)}) copy-start(bf16[4,192,256]{2,1,0:T(8,128)(2,1)} %copy-done.7) | copy-start | bytes 1179652
  162.9 34.7 %copy-start.6 = (bf16[36,4096]{1,0:T(8,128)(2,1)S(1)}, bf16[36,4096]{1,0:T(8,128)(2,1)}, u32[]{:S(2)}) copy-start(bf16[36,4096]{1,0:T(8,128)(2,1)} %rows_ref.3) | copy-start | bytes 884740
  162.9 34.7 %copy-start.12 = (f32[4096]{0:T(1024)S(1)}, f32[4096]{0:T(1024)}, u32[]{:S(2)}) copy-start(f32[4096]{0:T(1024)} %param.8) | copy-start | bytes 49156
  162.9 14.3 %all-to-all-start.5 = ((bf16[4,192,256]{2,1,0:T(8,128)(2,1)}), bf16[4,192,256]{2,1,0:T(8,128)(2,1)S(1)}, u32[]{:S(2)}, u32[]{:S(2)}) async-start(bf16[4,192,256]{2,1,0:T(8,128)(2,1)} %get-tuple-element.44), calls=%async_computation.5 | async-start | bytes 786432 | tf_op jit(solution)/shard_map/all_to_all | solution.py:366
  167.9 6.2 %collective-permute-start.17 = (bf16[192,256]{1,0:T(8,128)(2,1)}, bf16[192,256]{1,0:T(8,128)(2,1)S(1)}, u32[]{:S(2)}, u32[]{:S(2)}) collective-permute-start(bf16[192,256]{1,0:T(8,128)(2,1)} %get-tuple-element.41), channel_id=1, source_target_pairs={{0,8},{8,16},{16,24},{24,0},{32,40},{40,48},{48,56},{56,32},{64,72... | collective-permute-start | bytes 294920 | tf_op jit(solution)/shard_map/ppermute | solution.py:370
  168.6 5.7 %collective-permute-start.18 = (bf16[192,256]{1,0:T(8,128)(2,1)S(1)}, bf16[192,256]{1,0:T(8,128)(2,1)S(1)}, u32[]{:S(2)}, u32[]{:S(2)}) collective-permute-start(bf16[192,256]{1,0:T(8,128)(2,1)S(1)} %get-tuple-element.42), channel_id=1, source_target_pairs={{0,24},{8,0},{16,8},{24,16},{32,56},{40,32},{48,40},{56,48},{64,88... | collective-permute-start | bytes 294920 | tf_op jit(solution)/shard_map/ppermute | solution.py:370
  171.1 6.1 %collective-permute-start.19 = (bf16[192,256]{1,0:T(8,128)(2,1)S(1)}, bf16[192,256]{1,0:T(8,128)(2,1)S(1)}, u32[]{:S(2)}, u32[]{:S(2)}) collective-permute-start(bf16[192,256]{1,0:T(8,128)(2,1)S(1)} %get-tuple-element.43), channel_id=1, source_target_pairs={{0,16},{8,24},{16,0},{24,8},{32,48},{40,56},{48,32},{56,40},{64,80... | collective-permute-start | bytes 294920 | tf_op jit(solution)/shard_map/ppermute | solution.py:370
  (13 other events, 24.6 us)

commit v5 on v3

--- a/solution.py
+++ b/solution.py
@@ -284,18 +284,22 @@
     first = sum(r[...].astype(f32) for r in by_x)
     second = sum(by_y_ref[j].astype(f32) for j in range(by_y_ref.shape[0]))
     both = jnp.concatenate([first.astype(bf16), second.astype(bf16)], axis=1)
-    turns = out_ref.shape[1]
-    slots = NX * turns
+    slots, lanes = out_ref.shape[1:]
+    turns = slots // NX
     for z in range(out_ref.shape[0] // NX):
         rows = dot(spread_ref[z * slots : (z + 1) * slots, :].astype(bf16), both).astype(bf16)
         for k in range(NX):
-            out_ref[z * NX + k] = rows[k * turns : (k + 1) * turns]
+            for i in range(both.shape[1] // lanes):
+                out_ref[z * NX + k, i * turns : (i + 1) * turns, :] = rows[
+                    k * turns : (k + 1) * turns, i * lanes : (i + 1) * lanes
+                ]
 
 
 def finish_kernel(at_ref, got_ref, rows_ref, gain_ref, dots_ref, out_ref, sum_ref, grad_ref):
     offset, count = own_slots(at_ref)
-    turns, share = sum_ref.shape[1:]
+    lanes, share = sum_ref.shape[2], grad_ref.shape[1]
     slots, features = rows_ref.shape
+    turns = slots // NX
     tokens = dots_ref.shape[1]
     for k in range(NX):
         total = got_ref[k].astype(f32)
@@ -304,7 +308,11 @@
         sum_ref[k] = total
     for i in range(NX):
         for m in range(turns):
-            grad_ref[NX * m + i : NX * m + i + 1, :] = sum_ref[(offset + i) & (NX - 1), m : m + 1, :]
+            for j in range(share // lanes):
+                row = j * turns + m
+                grad_ref[NX * m + i : NX * m + i + 1, j * lanes : (j + 1) * lanes] = sum_ref[
+                    (offset + i) & (NX - 1), row : row + 1, :
+                ]
     rank = offset + lax.broadcasted_iota(jnp.int32, (slots, tokens), 0)
     row = (rank & (NX - 1)) * (tokens // NX) + ((rank & (GROUPS - 1)) >> 2) * (tokens // GROUPS) + (rank >> 5)
     here = row == lax.broadcasted_iota(jnp.int32, (slots, tokens), 1)
@@ -474,12 +482,12 @@
     by_x = to_ahead(pieces, along_x)
     by_y = exchange(to_y, "vocab", Y_LINES)
     spread_grad = call(
-        spread_kernel, "spread_rows", array((GROUPS, turns, share), bf16), *by_x, by_y, spread, size=2**20
+        spread_kernel, "spread_rows", array((GROUPS, slots, share // NX), bf16), *by_x, by_y, spread, size=2**20
     )
     grad_rollout = call(
         finish_kernel, "finish", array((slots, share), bf16), exchange(spread_grad, "seq"), rollout, final_gain[None, :],
         dots, prefetch=(at,), ins=[inside] * 4, outs=inside,
-        scratch=[pltpu.VMEM((NX, turns, share), f32), pltpu.VMEM((slots, share), f32)], size=2**19,
+        scratch=[pltpu.VMEM((NX, slots, share // NX), f32), pltpu.VMEM((slots, share), f32)], size=2**19,
     )
     return (kl, weight_t.T, grad_rollout)
 

time: 198 us -> 195 us (0.985)
  blocking collectives: 37.9 us -> 34.3 us
    all_to_all x2, blocking collectives: 37.9 us -> 34.3 us  [exchange(): return lax.all_to_all(x, axis, 0, 0, tiled=True, axis_index_groups=lines)]
  transfers between devices with their start and end apart: 25 -> 25, of which waited for: 13 -> 13; matrix products, arithmetic and copies ran while one was open for 1% -> 1% of each run, Pallas kernels for 19% -> 20%
where the time goes in v5:
time: 195 us; the launch traced here: 194 us
  starting transfers between devices  55.4 us (28%)
  Pallas kernels  51.5 us (26%)
  waiting for transfers between devices  37.8 us (19%)
  blocking collectives  34.3 us (18%)
  local copies, waits for them, and re-layouts  12.8 us (7%)
    pallas_call x16, Pallas kernels, call(): pl.pallas_call(body, grid_spec=pltpu.PrefetchScalarGridSpec(num_scalar_pr...  51.5 us
    all_to_all x2, blocking collectives, exchange(): return lax.all_to_all(x, axis, 0, 0, tiled=True, axis_index_groups=lines)  34.3 us
    all_to_all x5, starting transfers between devices, exchange(): return lax.all_to_all(x, axis, 0, 0, tiled=True, axis_index_groups=lines)  31.6 us
    ppermute x12, waiting for transfers between devices, along_x(): lax.ppermute(x, 'seq', [(i, i // NX * NX + (i + k) % NX) for i in range(G...  27.6 us
    ppermute x12, starting transfers between devices, along_x(): lax.ppermute(x, 'seq', [(i, i // NX * NX + (i + k) % NX) for i in range(G...  17.8 us
    unnamed x59, local copies, waits for them, and re-layouts  9.93 us
    all_to_all x5, waiting for transfers between devices, exchange(): return lax.all_to_all(x, axis, 0, 0, tiled=True, axis_index_groups=lines)  7.18 us
    ppermute x3, starting transfers between devices, along_y(): lax.ppermute(x, 'vocab', [(i, (i + 2 * k) % (2 * NY)) for i in range(2 *...  4.88 us
  transfers between devices with their start and end apart: 25, of which 13 were waited for; matrix products, arithmetic and copies ran while one was open for 1% of the time, Pallas kernels for 20%

profile of v5, /device:TPU:8, one launch (start us, length us, event | category | flops | bytes accessed | tf_op | source)
XLA Modules:
  0.0 193.8 jit_solution(16398385652685533269)
XLA Ops:
  3.1 1.8 sort_rows.1
  5.0 11.4 %all-to-all-start = ((bf16[32,9,512]{2,1,0:T(8,128)(2,1)}), bf16[32,9,512]{2,1,0:T(8,128)(2,1)S(1)}, u32[]{:S(2)}, u32[]{:S(2)}) async-start(bf16[32,9,512]{2,1,0:T(8,128)(2,1)} %sort_rows.1), calls=%async_computation | async-start | bytes 1048576 | tf_op jit(solution)/shard_map/all_to_all | solution.py:367
  17.3 9.3 %teacher_columns.1.dense_ref = f32[594,768]{1,0:T(8,128)S(1)} custom-call(s32[1]{0:T(128)} %bitcast.4.first_ref, s32[64,768]{1,0:T(8,128)S(1)} %bitcast.41, f32[64,768]{1,0:T(8,128)S(1)} %bitcast.36), custom_call_target="tpu_custom_call" | custom-call | flops 116785152 | bytes 1824768 | tf_op jit(solution)/shard_map/teacher_columns/pallas_call | solution.py:26
  27.0 7.2 %all-to-all-done = bf16[32,9,512]{2,1,0:T(8,128)(2,1)S(1)} async-done(((bf16[32,9,512]{2,1,0:T(8,128)(2,1)}), bf16[32,9,512]{2,1,0:T(8,128)(2,1)S(1)}, u32[]{:S(2)}, u32[]{:S(2)}) %all-to-all-start) | async-done | bytes 294944 | tf_op jit(solution)/shard_map/all_to_all | solution.py:367
  35.4 4.9 %all-to-all-start.2 = ((bf16[4,192,256]{2,1,0:T(8,128)(2,1)}), bf16[4,192,256]{2,1,0:T(8,128)(2,1)S(1)}, u32[]{:S(2)}, u32[]{:S(2)}) async-start(bf16[4,192,256]{2,1,0:T(8,128)(2,1)} %broadcast_in_dim.40), calls=%async_computation.2 | async-start | bytes 786432 | tf_op jit(solution)/shard_map/all_to_all | solution.py:367
  41.2 2.7 %collective-permute-start.1 = (bf16[192,256]{1,0:T(8,128)(2,1)S(1)}, bf16[192,256]{1,0:T(8,128)(2,1)S(1)}, u32[]{:S(2)}, u32[]{:S(2)}) collective-permute-start(bf16[192,256]{1,0:T(8,128)(2,1)S(1)} %get-tuple-element.46.refs_0_), channel_id=1, source_target_pairs={{0,16},{8,24},{16,0},{24,8},{32,48},{40,56},{48,32},{56,40},{64,80... | collective-permute-start | bytes 294920 | tf_op jit(solution)/shard_map/ppermute | solution.py:371
  50.3 4.8 %all-to-all-start.1 = ((bf16[4,768,256]{2,1,0:T(8,128)(2,1)}), bf16[4,768,256]{2,1,0:T(8,128)(2,1)}, u32[]{:S(2)}, u32[]{:S(2)}) async-start(bf16[4,768,256]{2,1,0:T(8,128)(2,1)} %bitcast.35), calls=%async_computation.1 | async-start | bytes 3145728 | tf_op jit(solution)/shard_map/all_to_all | solution.py:367
  56.5 2.8 %collective-permute-start.5 = (bf16[4,192,256]{2,1,0:T(8,128)(2,1)S(1)}, bf16[4,192,256]{2,1,0:T(8,128)(2,1)S(1)}, u32[]{:S(2)}, u32[]{:S(2)}) collective-permute-start(bf16[4,192,256]{2,1,0:T(8,128)(2,1)S(1)} %all-to-all-done.2.refs_0_), channel_id=1, source_target_pairs={{0,16},{8,24},{16,0},{24,8},{32,48},{40,56},{48,32},{56,40},{64,80... | collective-permute-start | bytes 1179656 | tf_op jit(solution)/shard_map/ppermute | solution.py:371
  59.7 8.6 %collective-permute-done.6.refs_3_ = bf16[4,192,256]{2,1,0:T(8,128)(2,1)S(1)} collective-permute-done((bf16[4,192,256]{2,1,0:T(8,128)(2,1)S(1)}, bf16[4,192,256]{2,1,0:T(8,128)(2,1)S(1)}, u32[]{:S(2)}, u32[]{:S(2)}) %collective-permute-start.6) | collective-permute-done | bytes 393248 | tf_op jit(solution)/shard_map/ppermute | solution.py:371
  68.3 4.3 %collective-permute-done.5.refs_2_ = bf16[4,192,256]{2,1,0:T(8,128)(2,1)S(1)} collective-permute-done((bf16[4,192,256]{2,1,0:T(8,128)(2,1)S(1)}, bf16[4,192,256]{2,1,0:T(8,128)(2,1)S(1)}, u32[]{:S(2)}, u32[]{:S(2)}) %collective-permute-start.5) | collective-permute-done | bytes 393248 | tf_op jit(solution)/shard_map/ppermute | solution.py:371
  72.6 1.8 gather_rows.1
  74.9 2.4 %copy-done = bf16[4096,594]{0,1:T(8,128)(2,1)S(1)} copy-done((bf16[4096,594]{0,1:T(8,128)(2,1)S(1)}, bf16[4096,594]{0,1:T(8,128)(2,1)}, u32[]{:S(2)}) %copy-start) | copy-done | bytes 4866072
  77.3 3.4 %logits_half.2.refs_0_ = f32[594,768]{1,0:T(8,128)S(1)} custom-call(s32[4]{0:T(128)S(1)} %fusion.21.block_ref, bf16[4,768,256]{2,1,0:T(8,128)(2,1)} %bitcast.15.rows_ref.refs_1_, bf16[594,4096]{1,0:T(8,128)(2,1)S(1)} %bitcast.26), custom_call_target="tpu_custom_call" | custom-call | flops 934281216 | bytes 6291456 | tf_op jit(solution)/shard_map/logits_half/pallas_call | solution.py:26
  80.7 3.1 %logits_half.3.own_ref = f32[594,768]{1,0:T(8,128)S(1)} custom-call(s32[4]{0:T(128)S(1)} %fusion.21.block_ref, bf16[4,768,256]{2,1,0:T(8,128)(2,1)} %all-to-all-done.1.rows_ref.refs_0_, bf16[594,4096]{1,0:T(8,128)(2,1)S(1)} %bitcast.29, f32[594,768]{1,0:T(8,128)S(1)} %logits_half.2.refs_0_), custom_call_target="tpu_custom_call" | custom-call | flops 934281216 | bytes 6291456 | tf_op jit(solution)/shard_map/logits_half/pallas_call | solution.py:26
  83.9 5.1 %logits_rest.1 = (f32[594,768]{1,0:T(8,128)S(1)}, f32[1,2304]{1,0:T(1,128)S(1)}) custom-call(s32[4]{0:T(128)S(1)} %add_subtract_fusion.block_ref, bf16[4,768,256]{2,1,0:T(8,128)(2,1)} %collective-permute-done.3.first_ref.refs_2_, bf16[4,768,256]{2,1,0:T(8,128)(2,1)} %collective-permute-done.7.second_ref.refs_3_, bf16[594,4096]{1,0:T(8,128)(2,1)S(1)} %bitcast.30, ...), custom_call_target="tpu_custom_call" | custom-call | flops 1868562432 | bytes 8388608 | tf_op jit(solution)/shard_map/logits_rest/pallas_call | solution.py:26
  92.9 2.3 %collective-permute-start.9 = (f32[1,2304]{1,0:T(1,128)S(1)}, f32[1,2304]{1,0:T(1,128)S(1)}, u32[]{:S(2)}, u32[]{:S(2)}) collective-permute-start(f32[1,2304]{1,0:T(1,128)S(1)} %pad_maximum_fusion), channel_id=1, source_target_pairs={{0,6},{1,7},{2,0},{3,1},{4,2},{5,3},{6,4},{7,5},{8,14},{9,15},{10,... | collective-permute-start | bytes 27656 | tf_op jit(solution)/shard_map/ppermute | solution.py:375
  95.2 1.8 collective-permute-done.10
  97.3 18.0 %all_to_all.38 = f32[32,1,2304]{2,1,0:T(1,128)S(1)} all-to-all(f32[32,1,2304]{2,1,0:T(1,128)S(1)} %broadcast_in_dim.41), channel_id=1, replica_groups=mesh['seq'=32,'vocab'=8] {'seq'}, dimensions={0} | all-to-all | bytes 589824 | tf_op jit(solution)/shard_map/all_to_all | solution.py:367
  115.3 2.3 %grad_logits.1 = (bf16[594,768]{1,0:T(8,128)(2,1)S(1)}, bf16[768,594]{1,0:T(8,128)(2,1)S(1)}, bf16[4,768,256]{2,1,0:T(8,128)(2,1)S(1)}) custom-call(s32[4]{0:T(128)S(1)} %add_subtract_fusion.block_ref, f32[32,2304]{1,0:T(8,128)S(1)} %bitcast.39, f32[594,768]{1,0:T(8,128)S(1)} %get-tuple-element.28.logits_ref, f32[594,768]{1,0:T(8,128)S(1)} %teacher_columns.1.dense_ref, ...), custom_call_target="tpu_custom_call" | custom-call | flops 934281216 | bytes 12582912 | tf_op jit(solution)/shard_map/grad_logits/pallas_call | solution.py:26
  117.7 3.1 %grad_rest.1 = bf16[4,768,256]{2,1,0:T(8,128)(2,1)} custom-call(s32[4]{0:T(128)S(1)} %add_subtract_fusion.block_ref, bf16[768,594]{1,0:T(8,128)(2,1)S(1)} %get-tuple-element.29.turned_ref, bf16[594,4096]{1,0:T(8,128)(2,1)S(1)} %bitcast.32), custom_call_target="tpu_custom_call" | custom-call | flops 934281216 | bytes 6291456 | tf_op jit(solution)/shard_map/grad_rest/pallas_call | solution.py:26
  121.3 3.2 %grad_first.1 = bf16[4,768,256]{2,1,0:T(8,128)(2,1)} custom-call(s32[4]{0:T(128)S(1)} %fusion.21.block_ref, bf16[768,594]{1,0:T(8,128)(2,1)S(1)} %get-tuple-element.29.turned_ref, bf16[594,4096]{1,0:T(8,128)(2,1)S(1)} %bitcast.33, bf16[4,768,256]{2,1,0:T(8,128)(2,1)S(1)} %collective-permute-done.12.other_ref), custom_call_target="tpu_custom_call" | custom-call | flops 934281216 | bytes 6291456 | tf_op jit(solution)/shard_map/grad_first/pallas_call | solution.py:26
  124.5 5.5 %all-to-all-start.4 = ((bf16[4,768,256]{2,1,0:T(8,128)(2,1)}), bf16[4,768,256]{2,1,0:T(8,128)(2,1)S(1)}, u32[]{:S(2)}, u32[]{:S(2)}) async-start(bf16[4,768,256]{2,1,0:T(8,128)(2,1)} %grad_first.1), calls=%async_computation.4 | async-start | bytes 3145728 | tf_op jit(solution)/shard_map/all_to_all | solution.py:367
  130.3 2.4 %copy-done.1 = bf16[4096,594]{0,1:T(8,128)(2,1)S(1)} copy-done((bf16[4096,594]{0,1:T(8,128)(2,1)S(1)}, bf16[4096,594]{0,1:T(8,128)(2,1)}, u32[]{:S(2)}) %copy-start.1) | copy-done | bytes 4866072
  132.7 3.5 %grad_second.1 = (bf16[4,192,256]{2,1,0:T(8,128)(2,1)S(1)}, bf16[4,192,256]{2,1,0:T(8,128)(2,1)S(1)}, bf16[4,192,256]{2,1,0:T(8,128)(2,1)S(1)}, bf16[4,192,256]{2,1,0:T(8,128)(2,1)S(1)}) custom-call(s32[4]{0:T(128)S(1)} %fusion.21.block_ref, s32[36]{0:T(128)S(1)} %concatenate.14.at_ref, bf16[768,594]{1,0:T(8,128)(2,1)S(1)} %get-tuple-element.29.turned_ref, ...), custom_call_target="tpu_custom_call" | custom-call | flops 934281216 | bytes 6291456 | tf_op jit(solution)/shard_map/grad_second/pallas_call | solution.py:26
  136.2 2.5 %collective-permute-start.16 = (bf16[4,192,256]{2,1,0:T(8,128)(2,1)S(1)}, bf16[4,192,256]{2,1,0:T(8,128)(2,1)S(1)}, u32[]{:S(2)}, u32[]{:S(2)}) collective-permute-start(bf16[4,192,256]{2,1,0:T(8,128)(2,1)S(1)} %get-tuple-element.34), channel_id=1, source_target_pairs={{0,16},{8,24},{16,0},{24,8},{32,48},{40,56},{48,32},{56,40},{64,80... | collective-permute-start | bytes 1179656 | tf_op jit(solution)/shard_map/ppermute | solution.py:371
  140.8 10.2 %weight_grad.1 = bf16[594,4096]{1,0:T(8,128)(2,1)} custom-call(s32[8]{0:T(128)S(1)} %pad_add_fusion.block_ref, bf16[4,768,256]{2,1,0:T(8,128)(2,1)} %all-to-all-done.1.rows_ref.refs_0_, bf16[4,768,256]{2,1,0:T(8,128)(2,1)} %bitcast.15.rows_ref.refs_1_, bf16[4,768,256]{2,1,0:T(8,128)(2,1)} %collective-permute-done.3.first_ref.refs_2_, ...), custom_call_target="tpu_custom_call" | custom-call | flops 3737124864 | bytes 16777216 | tf_op jit(solution)/shard_map/weight_grad/pallas_call | solution.py:26
  151.0 5.5 %collective-permute-done.14.refs_1_ = bf16[4,192,256]{2,1,0:T(8,128)(2,1)S(1)} collective-permute-done((bf16[4,192,256]{2,1,0:T(8,128)(2,1)S(1)}, bf16[4,192,256]{2,1,0:T(8,128)(2,1)S(1)}, u32[]{:S(2)}, u32[]{:S(2)}) %collective-permute-start.14) | collective-permute-done | bytes 393248 | tf_op jit(solution)/shard_map/ppermute | solution.py:371
  160.8 4.9 %all-to-all-start.5 = ((bf16[4,192,256]{2,1,0:T(8,128)(2,1)}), bf16[4,192,256]{2,1,0:T(8,128)(2,1)S(1)}, u32[]{:S(2)}, u32[]{:S(2)}) async-start(bf16[4,192,256]{2,1,0:T(8,128)(2,1)} %get-tuple-element.44), calls=%async_computation.5 | async-start | bytes 786432 | tf_op jit(solution)/shard_map/all_to_all | solution.py:367
  166.5 2.5 %collective-permute-start.18 = (bf16[192,256]{1,0:T(8,128)(2,1)}, bf16[192,256]{1,0:T(8,128)(2,1)S(1)}, u32[]{:S(2)}, u32[]{:S(2)}) collective-permute-start(bf16[192,256]{1,0:T(8,128)(2,1)} %copy-done.21), channel_id=1, source_target_pairs={{0,24},{8,0},{16,8},{24,16},{32,56},{40,32},{48,40},{56,48},{64,88... | collective-permute-start | bytes 294920 | tf_op jit(solution)/shard_map/ppermute | solution.py:371
  169.8 1.9 %collective-permute-done.17.refs_1_ = bf16[192,256]{1,0:T(8,128)(2,1)S(1)} collective-permute-done((bf16[192,256]{1,0:T(8,128)(2,1)}, bf16[192,256]{1,0:T(8,128)(2,1)S(1)}, u32[]{:S(2)}, u32[]{:S(2)}) %collective-permute-start.17) | collective-permute-done | bytes 98336 | tf_op jit(solution)/shard_map/ppermute | solution.py:371
  172.4 2.9 %collective-permute-done.19.refs_3_ = bf16[192,256]{1,0:T(8,128)(2,1)S(1)} collective-permute-done((bf16[192,256]{1,0:T(8,128)(2,1)}, bf16[192,256]{1,0:T(8,128)(2,1)S(1)}, u32[]{:S(2)}, u32[]{:S(2)}) %collective-permute-start.19) | collective-permute-done | bytes 98336 | tf_op jit(solution)/shard_map/ppermute | solution.py:371
  175.9 16.3 %all_to_all.39.got_ref = bf16[32,36,128]{2,1,0:T(8,128)(2,1)S(1)} all-to-all(bf16[32,36,128]{2,1,0:T(8,128)(2,1)S(1)} %spread_rows.1), channel_id=1, replica_groups=mesh['seq'=32,'vocab'=8] {'seq'}, dimensions={0} | all-to-all | bytes 589824 | tf_op jit(solution)/shard_map/all_to_all | solution.py:367
  (120 shorter events, 30.1 us)
Async XLA Ops:
  5.0 29.2 %all-to-all-start = ((bf16[32,9,512]{2,1,0:T(8,128)(2,1)}), bf16[32,9,512]{2,1,0:T(8,128)(2,1)S(1)}, u32[]{:S(2)}, u32[]{:S(2)}) async-start(bf16[32,9,512]{2,1,0:T(8,128)(2,1)} %sort_rows.1), calls=%async_computation | async-start | bytes 1048576 | tf_op jit(solution)/shard_map/all_to_all | solution.py:367
  17.3 17.0 %copy-start.3 = (f32[768,64]{0,1:T(8,128)}, f32[768,64]{0,1:T(8,128)S(1)}, u32[]{:S(2)}) copy-start(f32[768,64]{0,1:T(8,128)S(1)} %copy.28) | copy-start | bytes 589828
  35.4 14.9 %all-to-all-start.2 = ((bf16[4,192,256]{2,1,0:T(8,128)(2,1)}), bf16[4,192,256]{2,1,0:T(8,128)(2,1)S(1)}, u32[]{:S(2)}, u32[]{:S(2)}) async-start(bf16[4,192,256]{2,1,0:T(8,128)(2,1)} %broadcast_in_dim.40), calls=%async_computation.2 | async-start | bytes 786432 | tf_op jit(solution)/shard_map/all_to_all | solution.py:367
  40.3 5.8 %collective-permute-start.2 = (bf16[192,256]{1,0:T(8,128)(2,1)S(1)}, bf16[192,256]{1,0:T(8,128)(2,1)S(1)}, u32[]{:S(2)}, u32[]{:S(2)}) collective-permute-start(bf16[192,256]{1,0:T(8,128)(2,1)S(1)} %get-tuple-element.46.refs_0_), channel_id=1, source_target_pairs={{0,8},{8,16},{16,24},{24,0},{32,40},{40,48},{48,56},{56,32},{64,72... | collective-permute-start | bytes 294920 | tf_op jit(solution)/shard_map/ppermute | solution.py:371
  41.2 6.3 %collective-permute-start.1 = (bf16[192,256]{1,0:T(8,128)(2,1)S(1)}, bf16[192,256]{1,0:T(8,128)(2,1)S(1)}, u32[]{:S(2)}, u32[]{:S(2)}) collective-permute-start(bf16[192,256]{1,0:T(8,128)(2,1)S(1)} %get-tuple-element.46.refs_0_), channel_id=1, source_target_pairs={{0,16},{8,24},{16,0},{24,8},{32,48},{40,56},{48,32},{56,40},{64,80... | collective-permute-start | bytes 294920 | tf_op jit(solution)/shard_map/ppermute | solution.py:371
  43.9 4.6 %collective-permute-start = (bf16[192,256]{1,0:T(8,128)(2,1)S(1)}, bf16[192,256]{1,0:T(8,128)(2,1)S(1)}, u32[]{:S(2)}, u32[]{:S(2)}) collective-permute-start(bf16[192,256]{1,0:T(8,128)(2,1)S(1)} %get-tuple-element.46.refs_0_), channel_id=1, source_target_pairs={{0,24},{8,0},{16,8},{24,16},{32,56},{40,32},{48,40},{56,48},{64,88... | collective-permute-start | bytes 294920 | tf_op jit(solution)/shard_map/ppermute | solution.py:371
  50.3 24.1 %all-to-all-start.1 = ((bf16[4,768,256]{2,1,0:T(8,128)(2,1)}), bf16[4,768,256]{2,1,0:T(8,128)(2,1)}, u32[]{:S(2)}, u32[]{:S(2)}) async-start(bf16[4,768,256]{2,1,0:T(8,128)(2,1)} %bitcast.35), calls=%async_computation.1 | async-start | bytes 3145728 | tf_op jit(solution)/shard_map/all_to_all | solution.py:367
  55.1 13.2 %collective-permute-start.6 = (bf16[4,192,256]{2,1,0:T(8,128)(2,1)S(1)}, bf16[4,192,256]{2,1,0:T(8,128)(2,1)S(1)}, u32[]{:S(2)}, u32[]{:S(2)}) collective-permute-start(bf16[4,192,256]{2,1,0:T(8,128)(2,1)S(1)} %all-to-all-done.2.refs_0_), channel_id=1, source_target_pairs={{0,8},{8,16},{16,24},{24,0},{32,40},{40,48},{48,56},{56,32},{64,72... | collective-permute-start | bytes 1179656 | tf_op jit(solution)/shard_map/ppermute | solution.py:371
  56.5 16.1 %collective-permute-start.5 = (bf16[4,192,256]{2,1,0:T(8,128)(2,1)S(1)}, bf16[4,192,256]{2,1,0:T(8,128)(2,1)S(1)}, u32[]{:S(2)}, u32[]{:S(2)}) collective-permute-start(bf16[4,192,256]{2,1,0:T(8,128)(2,1)S(1)} %all-to-all-done.2.refs_0_), channel_id=1, source_target_pairs={{0,16},{8,24},{16,0},{24,8},{32,48},{40,56},{48,32},{56,40},{64,80... | collective-permute-start | bytes 1179656 | tf_op jit(solution)/shard_map/ppermute | solution.py:371
  59.2 13.3 %collective-permute-start.4 = (bf16[4,192,256]{2,1,0:T(8,128)(2,1)S(1)}, bf16[4,192,256]{2,1,0:T(8,128)(2,1)S(1)}, u32[]{:S(2)}, u32[]{:S(2)}) collective-permute-start(bf16[4,192,256]{2,1,0:T(8,128)(2,1)S(1)} %all-to-all-done.2.refs_0_), channel_id=1, source_target_pairs={{0,24},{8,0},{16,8},{24,16},{32,56},{40,32},{48,40},{56,48},{64,88... | collective-permute-start | bytes 1179656 | tf_op jit(solution)/shard_map/ppermute | solution.py:371
  74.4 9.5 %collective-permute-start.7 = (bf16[4,768,256]{2,1,0:T(8,128)(2,1)}, bf16[4,768,256]{2,1,0:T(8,128)(2,1)}, u32[]{:S(2)}, u32[]{:S(2)}) collective-permute-start(bf16[4,768,256]{2,1,0:T(8,128)(2,1)} %bitcast.15.rows_ref.refs_1_), channel_id=1, source_target_pairs={{0,1},{1,0},{2,3},{3,2},{4,5},{5,4},{6,7},{7,6},{8,9},{9,8},{10,11... | collective-permute-start | bytes 4718600 | tf_op jit(solution)/shard_map/ppermute | solution.py:454
  74.4 9.5 %collective-permute-start.3 = (bf16[4,768,256]{2,1,0:T(8,128)(2,1)}, bf16[4,768,256]{2,1,0:T(8,128)(2,1)}, u32[]{:S(2)}, u32[]{:S(2)}) collective-permute-start(bf16[4,768,256]{2,1,0:T(8,128)(2,1)} %all-to-all-done.1.rows_ref.refs_0_), channel_id=1, source_target_pairs={{0,1},{1,0},{2,3},{3,2},{4,5},{5,4},{6,7},{7,6},{8,9},{9,8},{10,11... | collective-permute-start | bytes 4718600 | tf_op jit(solution)/shard_map/ppermute | solution.py:456
  74.9 42.8 %copy-start.14 = (s32[4]{0:T(128)}, s32[4]{0:T(128)S(1)}, u32[]{:S(2)}) copy-start(s32[4]{0:T(128)S(1)} %add_subtract_fusion.block_ref) | copy-start | bytes 52
  89.0 26.3 %copy-start.4 = (f32[768,64]{0,1:T(8,128)S(1)}, f32[768,64]{0,1:T(8,128)}, u32[]{:S(2)}) copy-start(f32[768,64]{0,1:T(8,128)} %copy-done.3) | copy-start | bytes 589828
  89.0 1.3 collective-permute-start.8
  90.3 4.9 %collective-permute-start.11 = (f32[1,2304]{1,0:T(1,128)S(1)}, f32[1,2304]{1,0:T(1,128)S(1)}, u32[]{:S(2)}, u32[]{:S(2)}) collective-permute-start(f32[1,2304]{1,0:T(1,128)S(1)} %pad_maximum_fusion), channel_id=1, source_target_pairs={{0,2},{1,3},{2,4},{3,5},{4,6},{5,7},{6,0},{7,1},{8,10},{9,11},{10,... | collective-permute-start | bytes 27656 | tf_op jit(solution)/shard_map/ppermute | solution.py:375
  91.9 5.2 %collective-permute-start.10 = (f32[1,2304]{1,0:T(1,128)S(1)}, f32[1,2304]{1,0:T(1,128)S(1)}, u32[]{:S(2)}, u32[]{:S(2)}) collective-permute-start(f32[1,2304]{1,0:T(1,128)S(1)} %pad_maximum_fusion), channel_id=1, source_target_pairs={{0,4},{1,5},{2,6},{3,7},{4,0},{5,1},{6,2},{7,3},{8,12},{9,13},{10,... | collective-permute-start | bytes 27656 | tf_op jit(solution)/shard_map/ppermute | solution.py:375
  92.9 4.2 %collective-permute-start.9 = (f32[1,2304]{1,0:T(1,128)S(1)}, f32[1,2304]{1,0:T(1,128)S(1)}, u32[]{:S(2)}, u32[]{:S(2)}) collective-permute-start(f32[1,2304]{1,0:T(1,128)S(1)} %pad_maximum_fusion), channel_id=1, source_target_pairs={{0,6},{1,7},{2,0},{3,1},{4,2},{5,3},{6,4},{7,5},{8,14},{9,15},{10,... | collective-permute-start | bytes 27656 | tf_op jit(solution)/shard_map/ppermute | solution.py:375
  117.6 3.7 %collective-permute-start.12 = (bf16[4,768,256]{2,1,0:T(8,128)(2,1)S(1)}, bf16[4,768,256]{2,1,0:T(8,128)(2,1)S(1)}, u32[]{:S(2)}, u32[]{:S(2)}) collective-permute-start(bf16[4,768,256]{2,1,0:T(8,128)(2,1)S(1)} %get-tuple-element.30), channel_id=1, source_target_pairs={{0,1},{1,0},{2,3},{3,2},{4,5},{5,4},{6,7},{7,6},{8,9},{9,8},{10,11... | collective-permute-start | bytes 4718600 | tf_op jit(solution)/shard_map/ppermute | solution.py:465
  120.8 9.4 %collective-permute-start.13 = (bf16[4,768,256]{2,1,0:T(8,128)(2,1)}, bf16[4,768,256]{2,1,0:T(8,128)(2,1)}, u32[]{:S(2)}, u32[]{:S(2)}) collective-permute-start(bf16[4,768,256]{2,1,0:T(8,128)(2,1)} %grad_rest.1), channel_id=1, source_target_pairs={{0,1},{1,0},{2,3},{3,2},{4,5},{5,4},{6,7},{7,6},{8,9},{9,8},{10,11... | collective-permute-start | bytes 4718600 | tf_op jit(solution)/shard_map/ppermute | solution.py:466
  124.5 32.6 %all-to-all-start.4 = ((bf16[4,768,256]{2,1,0:T(8,128)(2,1)}), bf16[4,768,256]{2,1,0:T(8,128)(2,1)S(1)}, u32[]{:S(2)}, u32[]{:S(2)}) async-start(bf16[4,768,256]{2,1,0:T(8,128)(2,1)} %grad_first.1), calls=%async_computation.4 | async-start | bytes 3145728 | tf_op jit(solution)/shard_map/all_to_all | solution.py:367
  136.1 20.4 %collective-permute-start.14 = (bf16[4,192,256]{2,1,0:T(8,128)(2,1)S(1)}, bf16[4,192,256]{2,1,0:T(8,128)(2,1)S(1)}, u32[]{:S(2)}, u32[]{:S(2)}) collective-permute-start(bf16[4,192,256]{2,1,0:T(8,128)(2,1)S(1)} %get-tuple-element.33), channel_id=1, source_target_pairs={{0,8},{8,16},{16,24},{24,0},{32,40},{40,48},{48,56},{56,32},{64,72... | collective-permute-start | bytes 1179656 | tf_op jit(solution)/shard_map/ppermute | solution.py:371
  136.2 20.3 %collective-permute-start.16 = (bf16[4,192,256]{2,1,0:T(8,128)(2,1)S(1)}, bf16[4,192,256]{2,1,0:T(8,128)(2,1)S(1)}, u32[]{:S(2)}, u32[]{:S(2)}) collective-permute-start(bf16[4,192,256]{2,1,0:T(8,128)(2,1)S(1)} %get-tuple-element.34), channel_id=1, source_target_pairs={{0,16},{8,24},{16,0},{24,8},{32,48},{40,56},{48,32},{56,40},{64,80... | collective-permute-start | bytes 1179656 | tf_op jit(solution)/shard_map/ppermute | solution.py:371
  138.8 18.4 %collective-permute-start.15 = (bf16[4,192,256]{2,1,0:T(8,128)(2,1)S(1)}, bf16[4,192,256]{2,1,0:T(8,128)(2,1)S(1)}, u32[]{:S(2)}, u32[]{:S(2)}) collective-permute-start(bf16[4,192,256]{2,1,0:T(8,128)(2,1)S(1)} %get-tuple-element.35), channel_id=1, source_target_pairs={{0,24},{8,0},{16,8},{24,16},{32,56},{40,32},{48,40},{56,48},{64,88... | collective-permute-start | bytes 1179656 | tf_op jit(solution)/shard_map/ppermute | solution.py:371
  151.0 24.3 %copy-start.9 = (f32[288,192]{1,0:T(8,128)S(1)}, f32[288,192]{1,0:T(8,128)}, u32[]{:S(2)}) copy-start(f32[288,192]{1,0:T(8,128)} %copy-done.8) | copy-start | bytes 663556
  160.8 31.4 %copy-start.11 = (bf16[36,4096]{1,0:T(8,128)(2,1)S(1)}, bf16[36,4096]{1,0:T(8,128)(2,1)}, u32[]{:S(2)}) copy-start(bf16[36,4096]{1,0:T(8,128)(2,1)} %rows_ref.3) | copy-start | bytes 884740
  160.8 31.4 %copy-start.13 = (f32[4096]{0:T(1024)S(1)}, f32[4096]{0:T(1024)}, u32[]{:S(2)}) copy-start(f32[4096]{0:T(1024)} %param.8) | copy-start | bytes 49156
  160.8 31.4 %copy-start.17 = (f32[1,768]{1,0:T(1,128)S(1)}, f32[1,768]{1,0:T(1,128)}, u32[]{:S(2)}) copy-start(f32[1,768]{1,0:T(1,128)} %copy-done.16) | copy-start | bytes 9220
  160.8 14.5 %all-to-all-start.5 = ((bf16[4,192,256]{2,1,0:T(8,128)(2,1)}), bf16[4,192,256]{2,1,0:T(8,128)(2,1)S(1)}, u32[]{:S(2)}, u32[]{:S(2)}) async-start(bf16[4,192,256]{2,1,0:T(8,128)(2,1)} %get-tuple-element.44), calls=%async_computation.5 | async-start | bytes 786432 | tf_op jit(solution)/shard_map/all_to_all | solution.py:367
  165.8 6.0 %collective-permute-start.17 = (bf16[192,256]{1,0:T(8,128)(2,1)}, bf16[192,256]{1,0:T(8,128)(2,1)S(1)}, u32[]{:S(2)}, u32[]{:S(2)}) collective-permute-start(bf16[192,256]{1,0:T(8,128)(2,1)} %copy-done.22), channel_id=1, source_target_pairs={{0,8},{8,16},{16,24},{24,0},{32,40},{40,48},{48,56},{56,32},{64,72... | collective-permute-start | bytes 294920 | tf_op jit(solution)/shard_map/ppermute | solution.py:371
  166.5 6.0 %collective-permute-start.18 = (bf16[192,256]{1,0:T(8,128)(2,1)}, bf16[192,256]{1,0:T(8,128)(2,1)S(1)}, u32[]{:S(2)}, u32[]{:S(2)}) collective-permute-start(bf16[192,256]{1,0:T(8,128)(2,1)} %copy-done.21), channel_id=1, source_target_pairs={{0,24},{8,0},{16,8},{24,16},{32,56},{40,32},{48,40},{56,48},{64,88... | collective-permute-start | bytes 294920 | tf_op jit(solution)/shard_map/ppermute | solution.py:371
  169.0 6.3 %collective-permute-start.19 = (bf16[192,256]{1,0:T(8,128)(2,1)}, bf16[192,256]{1,0:T(8,128)(2,1)S(1)}, u32[]{:S(2)}, u32[]{:S(2)}) collective-permute-start(bf16[192,256]{1,0:T(8,128)(2,1)} %copy-done.20), channel_id=1, source_target_pairs={{0,16},{8,24},{16,0},{24,8},{32,48},{40,56},{48,32},{56,40},{64,80... | collective-permute-start | bytes 294920 | tf_op jit(solution)/shard_map/ppermute | solution.py:371
  (21 other events, 107.0 us)

commit v6 on v5

--- a/solution.py
+++ b/solution.py
@@ -61,7 +61,7 @@
 def sort_kernel(at_ref, rows_ref, gain_ref, out_ref):
     vocab = at_ref[3]
     slots, features = rows_ref.shape
-    turns, share = out_ref.shape[1:]
+    turns, lanes, share = slots // NX, out_ref.shape[2], NX * out_ref.shape[2]
     offset, count = own_slots(at_ref)
     inv_rms = inverse_rms(rows_ref, share)
     part = pl.ds(pl.multiple_of(vocab * share, share), share)
@@ -74,7 +74,24 @@
     by_class = dot(pick, normed).astype(bf16)
     for g in range(out_ref.shape[0]):
         k = g % NX
-        out_ref[g] = by_class[k * turns : (k + 1) * turns]
+        for i in range(NX):
+            out_ref[g, i * turns : (i + 1) * turns, :] = by_class[
+                k * turns : (k + 1) * turns, i * lanes : (i + 1) * lanes
+            ]
+
+
+def compact_kernel(got_ref, spread_ref, first_ref, second_ref, rows_ref):
+    count, slots, lanes = got_ref.shape
+    turns = slots // NX
+    for g in range(count):
+        for i in range(NX):
+            piece = got_ref[g, i * turns : (i + 1) * turns, :].astype(f32)
+            rows_ref[g * turns : (g + 1) * turns, i * lanes : (i + 1) * lanes] = piece
+    rows = dot(spread_ref[...].astype(bf16), rows_ref[...].astype(bf16), 0, 0).astype(bf16)
+    half = first_ref.shape[1]
+    first_ref[...] = rows[:, :half]
+    for y in range(second_ref.shape[0]):
+        second_ref[y] = rows[:, half:]
 
 
 def teacher_kernel(first_ref, index_ref, logprob_ref, dense_ref):
@@ -415,7 +432,7 @@
     at = jnp.concatenate([jnp.stack([own_x, own_y, seq, vocab]).astype(jnp.int32), group_count])
 
     of_class = call(
-        sort_kernel, "sort_rows", array((GROUPS, turns, share), bf16), rollout, final_gain[None, :], prefetch=(at,), size=2**19
+        sort_kernel, "sort_rows", array((GROUPS, slots, share // NX), bf16), rollout, final_gain[None, :], prefetch=(at,), size=2**19
     )
     of_class = exchange(of_class, "seq")
 
@@ -437,10 +454,15 @@
     place_ids = jnp.arange(class_rows, dtype=jnp.int32)
     place = after(place, dense)
     spread = lax.optimization_barrier((place.reshape(-1, 1) == place_ids[None, :]).astype(f32))
-    dense_rows = dot(spread.astype(bf16), of_class.reshape(-1, share), 0, 0).astype(bf16)
-
-    by_x = from_ahead(dense_rows[:, :half], along_x)
-    all_y = exchange(jnp.broadcast_to(dense_rows[:, half:], (NY, class_rows, half)), "vocab", Y_LINES)
+    inside = pl.BlockSpec(memory_space=pltpu.VMEM)
+    own_first, own_second = call(
+        compact_kernel, "compact", [array((class_rows, half), bf16), array((NY, class_rows, half), bf16)],
+        of_class, spread, ins=[inside] * 2, outs=[inside] * 2,
+        scratch=[pltpu.VMEM((GROUPS * turns, share), f32)], size=2**20,
+    )
+
+    by_x = from_ahead(own_first, along_x)
+    all_y = exchange(own_second, "vocab", Y_LINES)
     all_x = call(place_kernel, "place", array((NY, NX, class_rows, half), bf16), *by_x, prefetch=(at,), size=2**21)
     by_x = from_ahead(all_y, along_x)
     own_first = exchange(all_x.reshape(NY, tokens, half), "vocab", Y_LINES)

time: 195 us -> 195 us (level)
  waiting for transfers between devices: 37.8 us -> 33.1 us
  blocking collectives: 34.3 us -> 38.3 us
    all_to_all x5, waiting for transfers between devices: 7.18 us -> 1.88 us  [exchange(): return lax.all_to_all(x, axis, 0, 0, tiled=True, axis_index_groups=lines)]
    all_to_all x2, blocking collectives: 34.3 us -> 38.3 us  [exchange(): return lax.all_to_all(x, axis, 0, 0, tiled=True, axis_index_groups=lines)]
    pallas_call x16 -> x17, Pallas kernels: 51.5 us -> 52.6 us  [call(): pl.pallas_call(body, grid_spec=pltpu.PrefetchScalarGridSpec(num_scalar_pr...]
    unnamed x59 -> x57, local copies, waits for them, and re-layouts: 9.93 us -> 10.9 us
  transfers between devices with their start and end apart: 25 -> 25, of which waited for: 13 -> 12; matrix products, arithmetic and copies ran while one was open for 1% -> 2% of each run, Pallas kernels for 20% -> 20%
where the time goes in v6:
time: 195 us; the launch traced here: 194 us
  starting transfers between devices  54.7 us (28%)
  Pallas kernels  52.6 us (27%)
  blocking collectives  38.3 us (20%)
  waiting for transfers between devices  33.1 us (17%)
  local copies, waits for them, and re-layouts  12.8 us (7%)
    pallas_call x17, Pallas kernels, call(): pl.pallas_call(body, grid_spec=pltpu.PrefetchScalarGridSpec(num_scalar_pr...  52.6 us
    all_to_all x2, blocking collectives, exchange(): return lax.all_to_all(x, axis, 0, 0, tiled=True, axis_index_groups=lines)  38.3 us
    all_to_all x5, starting transfers between devices, exchange(): return lax.all_to_all(x, axis, 0, 0, tiled=True, axis_index_groups=lines)  31.5 us
    ppermute x12, waiting for transfers between devices, along_x(): lax.ppermute(x, 'seq', [(i, i // NX * NX + (i + k) % NX) for i in range(G...  28.1 us
    ppermute x12, starting transfers between devices, along_x(): lax.ppermute(x, 'seq', [(i, i // NX * NX + (i + k) % NX) for i in range(G...  17.3 us
    unnamed x57, local copies, waits for them, and re-layouts  10.9 us
    ppermute x3, starting transfers between devices, along_y(): lax.ppermute(x, 'vocab', [(i, (i + 2 * k) % (2 * NY)) for i in range(2 *...  4.78 us
  transfers between devices with their start and end apart: 25, of which 12 were waited for; matrix products, arithmetic and copies ran while one was open for 2% of the time, Pallas kernels for 20%

profile of v6, /device:TPU:8, one launch (start us, length us, event | category | flops | bytes accessed | tf_op | source)
XLA Modules:
  0.0 193.7 jit_solution(4141679021738514871)
XLA Ops:
  3.1 1.8 sort_rows.1
  4.9 11.3 %all-to-all-start = ((bf16[32,36,128]{2,1,0:T(8,128)(2,1)}), bf16[32,36,128]{2,1,0:T(8,128)(2,1)S(1)}, u32[]{:S(2)}, u32[]{:S(2)}) async-start(bf16[32,36,128]{2,1,0:T(8,128)(2,1)} %sort_rows.1), calls=%async_computation | async-start | bytes 655360 | tf_op jit(solution)/shard_map/all_to_all | solution.py:384
  18.7 9.3 %teacher_columns.1.dense_ref = f32[594,768]{1,0:T(8,128)S(1)} custom-call(s32[1]{0:T(128)} %bitcast.5.first_ref, s32[64,768]{1,0:T(8,128)S(1)} %bitcast.40, f32[64,768]{1,0:T(8,128)S(1)} %bitcast.35), custom_call_target="tpu_custom_call" | custom-call | flops 116785152 | bytes 1824768 | tf_op jit(solution)/shard_map/teacher_columns/pallas_call | solution.py:26
  28.3 1.9 all-to-all-done.got_ref
  31.4 4.9 %all-to-all-start.2 = ((bf16[4,192,256]{2,1,0:T(8,128)(2,1)}), bf16[4,192,256]{2,1,0:T(8,128)(2,1)S(1)}, u32[]{:S(2)}, u32[]{:S(2)}) async-start(bf16[4,192,256]{2,1,0:T(8,128)(2,1)} %get-tuple-element.28), calls=%async_computation.2 | async-start | bytes 786432 | tf_op jit(solution)/shard_map/all_to_all | solution.py:384
  36.7 2.7 %collective-permute-start.1 = (bf16[192,256]{1,0:T(8,128)(2,1)S(1)}, bf16[192,256]{1,0:T(8,128)(2,1)S(1)}, u32[]{:S(2)}, u32[]{:S(2)}) collective-permute-start(bf16[192,256]{1,0:T(8,128)(2,1)S(1)} %get-tuple-element.27.refs_0_), channel_id=1, source_target_pairs={{0,16},{8,24},{16,0},{24,8},{32,48},{40,56},{48,32},{56,40},{64,80... | collective-permute-start | bytes 294920 | tf_op jit(solution)/shard_map/ppermute | solution.py:388
  40.8 2.3 %collective-permute-done.2.refs_3_ = bf16[192,256]{1,0:T(8,128)(2,1)S(1)} collective-permute-done((bf16[192,256]{1,0:T(8,128)(2,1)S(1)}, bf16[192,256]{1,0:T(8,128)(2,1)S(1)}, u32[]{:S(2)}, u32[]{:S(2)}) %collective-permute-start.2) | collective-permute-done | bytes 98336 | tf_op jit(solution)/shard_map/ppermute | solution.py:388
  45.8 4.8 %all-to-all-start.1 = ((bf16[4,768,256]{2,1,0:T(8,128)(2,1)}), bf16[4,768,256]{2,1,0:T(8,128)(2,1)}, u32[]{:S(2)}, u32[]{:S(2)}) async-start(bf16[4,768,256]{2,1,0:T(8,128)(2,1)} %bitcast.34), calls=%async_computation.1 | async-start | bytes 3145728 | tf_op jit(solution)/shard_map/all_to_all | solution.py:384
  51.9 2.8 %collective-permute-start.5 = (bf16[4,192,256]{2,1,0:T(8,128)(2,1)S(1)}, bf16[4,192,256]{2,1,0:T(8,128)(2,1)S(1)}, u32[]{:S(2)}, u32[]{:S(2)}) collective-permute-start(bf16[4,192,256]{2,1,0:T(8,128)(2,1)S(1)} %all-to-all-done.2.refs_0_), channel_id=1, source_target_pairs={{0,16},{8,24},{16,0},{24,8},{32,48},{40,56},{48,32},{56,40},{64,80... | collective-permute-start | bytes 1179656 | tf_op jit(solution)/shard_map/ppermute | solution.py:388
  55.2 8.7 %collective-permute-done.6.refs_3_ = bf16[4,192,256]{2,1,0:T(8,128)(2,1)S(1)} collective-permute-done((bf16[4,192,256]{2,1,0:T(8,128)(2,1)S(1)}, bf16[4,192,256]{2,1,0:T(8,128)(2,1)S(1)}, u32[]{:S(2)}, u32[]{:S(2)}) %collective-permute-start.6) | collective-permute-done | bytes 393248 | tf_op jit(solution)/shard_map/ppermute | solution.py:388
  63.8 4.6 %collective-permute-done.5.refs_2_ = bf16[4,192,256]{2,1,0:T(8,128)(2,1)S(1)} collective-permute-done((bf16[4,192,256]{2,1,0:T(8,128)(2,1)S(1)}, bf16[4,192,256]{2,1,0:T(8,128)(2,1)S(1)}, u32[]{:S(2)}, u32[]{:S(2)}) %collective-permute-start.5) | collective-permute-done | bytes 393248 | tf_op jit(solution)/shard_map/ppermute | solution.py:388
  70.8 2.4 %copy-done = bf16[4096,594]{0,1:T(8,128)(2,1)S(1)} copy-done((bf16[4096,594]{0,1:T(8,128)(2,1)S(1)}, bf16[4096,594]{0,1:T(8,128)(2,1)}, u32[]{:S(2)}) %copy-start) | copy-done | bytes 4866072
  73.2 3.4 %logits_half.2.refs_0_ = f32[594,768]{1,0:T(8,128)S(1)} custom-call(s32[4]{0:T(128)S(1)} %fusion.20.block_ref, bf16[4,768,256]{2,1,0:T(8,128)(2,1)} %bitcast.15.rows_ref.refs_1_, bf16[594,4096]{1,0:T(8,128)(2,1)S(1)} %bitcast.25), custom_call_target="tpu_custom_call" | custom-call | flops 934281216 | bytes 6291456 | tf_op jit(solution)/shard_map/logits_half/pallas_call | solution.py:26
  76.6 3.1 %logits_half.3.own_ref = f32[594,768]{1,0:T(8,128)S(1)} custom-call(s32[4]{0:T(128)S(1)} %fusion.20.block_ref, bf16[4,768,256]{2,1,0:T(8,128)(2,1)} %all-to-all-done.1.rows_ref.refs_0_, bf16[594,4096]{1,0:T(8,128)(2,1)S(1)} %bitcast.28, f32[594,768]{1,0:T(8,128)S(1)} %logits_half.2.refs_0_), custom_call_target="tpu_custom_call" | custom-call | flops 934281216 | bytes 6291456 | tf_op jit(solution)/shard_map/logits_half/pallas_call | solution.py:26
  79.8 5.1 %logits_rest.1 = (f32[594,768]{1,0:T(8,128)S(1)}, f32[1,2304]{1,0:T(1,128)S(1)}) custom-call(s32[4]{0:T(128)S(1)} %add_subtract_fusion.block_ref, bf16[4,768,256]{2,1,0:T(8,128)(2,1)} %collective-permute-done.3.first_ref.refs_2_, bf16[4,768,256]{2,1,0:T(8,128)(2,1)} %collective-permute-done.7.second_ref.refs_3_, bf16[594,4096]{1,0:T(8,128)(2,1)S(1)} %bitcast.29, ...), custom_call_target="tpu_custom_call" | custom-call | flops 1868562432 | bytes 8388608 | tf_op jit(solution)/shard_map/logits_rest/pallas_call | solution.py:26
  88.8 2.2 %collective-permute-start.9 = (f32[1,2304]{1,0:T(1,128)S(1)}, f32[1,2304]{1,0:T(1,128)S(1)}, u32[]{:S(2)}, u32[]{:S(2)}) collective-permute-start(f32[1,2304]{1,0:T(1,128)S(1)} %pad_maximum_fusion), channel_id=1, source_target_pairs={{0,6},{1,7},{2,0},{3,1},{4,2},{5,3},{6,4},{7,5},{8,14},{9,15},{10,... | collective-permute-start | bytes 27656 | tf_op jit(solution)/shard_map/ppermute | solution.py:392
  91.0 1.9 collective-permute-done.10
  93.2 22.0 %all_to_all.38 = f32[32,1,2304]{2,1,0:T(1,128)S(1)} all-to-all(f32[32,1,2304]{2,1,0:T(1,128)S(1)} %broadcast_in_dim.37), channel_id=1, replica_groups=mesh['seq'=32,'vocab'=8] {'seq'}, dimensions={0} | all-to-all | bytes 589824 | tf_op jit(solution)/shard_map/all_to_all | solution.py:384
  115.3 2.3 %grad_logits.1 = (bf16[594,768]{1,0:T(8,128)(2,1)S(1)}, bf16[768,594]{1,0:T(8,128)(2,1)S(1)}, bf16[4,768,256]{2,1,0:T(8,128)(2,1)S(1)}) custom-call(s32[4]{0:T(128)S(1)} %add_subtract_fusion.block_ref, f32[32,2304]{1,0:T(8,128)S(1)} %bitcast.38, f32[594,768]{1,0:T(8,128)S(1)} %get-tuple-element.32.logits_ref, f32[594,768]{1,0:T(8,128)S(1)} %teacher_columns.1.dense_ref, ...), custom_call_target="tpu_custom_call" | custom-call | flops 934281216 | bytes 12582912 | tf_op jit(solution)/shard_map/grad_logits/pallas_call | solution.py:26
  117.7 3.1 %grad_rest.1 = bf16[4,768,256]{2,1,0:T(8,128)(2,1)} custom-call(s32[4]{0:T(128)S(1)} %add_subtract_fusion.block_ref, bf16[768,594]{1,0:T(8,128)(2,1)S(1)} %get-tuple-element.33.turned_ref, bf16[594,4096]{1,0:T(8,128)(2,1)S(1)} %bitcast.31), custom_call_target="tpu_custom_call" | custom-call | flops 934281216 | bytes 6291456 | tf_op jit(solution)/shard_map/grad_rest/pallas_call | solution.py:26
  121.3 3.2 %grad_first.1 = bf16[4,768,256]{2,1,0:T(8,128)(2,1)} custom-call(s32[4]{0:T(128)S(1)} %fusion.20.block_ref, bf16[768,594]{1,0:T(8,128)(2,1)S(1)} %get-tuple-element.33.turned_ref, bf16[594,4096]{1,0:T(8,128)(2,1)S(1)} %bitcast.32, bf16[4,768,256]{2,1,0:T(8,128)(2,1)S(1)} %collective-permute-done.12.other_ref), custom_call_target="tpu_custom_call" | custom-call | flops 934281216 | bytes 6291456 | tf_op jit(solution)/shard_map/grad_first/pallas_call | solution.py:26
  124.5 5.5 %all-to-all-start.4 = ((bf16[4,768,256]{2,1,0:T(8,128)(2,1)}), bf16[4,768,256]{2,1,0:T(8,128)(2,1)S(1)}, u32[]{:S(2)}, u32[]{:S(2)}) async-start(bf16[4,768,256]{2,1,0:T(8,128)(2,1)} %grad_first.1), calls=%async_computation.4 | async-start | bytes 3145728 | tf_op jit(solution)/shard_map/all_to_all | solution.py:384
  130.2 2.4 %copy-done.1 = bf16[4096,594]{0,1:T(8,128)(2,1)S(1)} copy-done((bf16[4096,594]{0,1:T(8,128)(2,1)S(1)}, bf16[4096,594]{0,1:T(8,128)(2,1)}, u32[]{:S(2)}) %copy-start.1) | copy-done | bytes 4866072
  132.6 3.5 %grad_second.1 = (bf16[4,192,256]{2,1,0:T(8,128)(2,1)S(1)}, bf16[4,192,256]{2,1,0:T(8,128)(2,1)S(1)}, bf16[4,192,256]{2,1,0:T(8,128)(2,1)S(1)}, bf16[4,192,256]{2,1,0:T(8,128)(2,1)S(1)}) custom-call(s32[4]{0:T(128)S(1)} %fusion.20.block_ref, s32[36]{0:T(128)S(1)} %concatenate.14.at_ref, bf16[768,594]{1,0:T(8,128)(2,1)S(1)} %get-tuple-element.33.turned_ref, ...), custom_call_target="tpu_custom_call" | custom-call | flops 934281216 | bytes 6291456 | tf_op jit(solution)/shard_map/grad_second/pallas_call | solution.py:26
  136.2 2.5 %collective-permute-start.16 = (bf16[4,192,256]{2,1,0:T(8,128)(2,1)S(1)}, bf16[4,192,256]{2,1,0:T(8,128)(2,1)S(1)}, u32[]{:S(2)}, u32[]{:S(2)}) collective-permute-start(bf16[4,192,256]{2,1,0:T(8,128)(2,1)S(1)} %get-tuple-element.38), channel_id=1, source_target_pairs={{0,16},{8,24},{16,0},{24,8},{32,48},{40,56},{48,32},{56,40},{64,80... | collective-permute-start | bytes 1179656 | tf_op jit(solution)/shard_map/ppermute | solution.py:388
  140.7 10.2 %weight_grad.1 = bf16[594,4096]{1,0:T(8,128)(2,1)} custom-call(s32[8]{0:T(128)S(1)} %pad_add_fusion.block_ref, bf16[4,768,256]{2,1,0:T(8,128)(2,1)} %all-to-all-done.1.rows_ref.refs_0_, bf16[4,768,256]{2,1,0:T(8,128)(2,1)} %bitcast.15.rows_ref.refs_1_, bf16[4,768,256]{2,1,0:T(8,128)(2,1)} %collective-permute-done.3.first_ref.refs_2_, ...), custom_call_target="tpu_custom_call" | custom-call | flops 3737124864 | bytes 16777216 | tf_op jit(solution)/shard_map/weight_grad/pallas_call | solution.py:26
  150.9 5.5 %collective-permute-done.14.refs_1_ = bf16[4,192,256]{2,1,0:T(8,128)(2,1)S(1)} collective-permute-done((bf16[4,192,256]{2,1,0:T(8,128)(2,1)S(1)}, bf16[4,192,256]{2,1,0:T(8,128)(2,1)S(1)}, u32[]{:S(2)}, u32[]{:S(2)}) %collective-permute-start.14) | collective-permute-done | bytes 393248 | tf_op jit(solution)/shard_map/ppermute | solution.py:388
  160.8 4.9 %all-to-all-start.5 = ((bf16[4,192,256]{2,1,0:T(8,128)(2,1)}), bf16[4,192,256]{2,1,0:T(8,128)(2,1)S(1)}, u32[]{:S(2)}, u32[]{:S(2)}) async-start(bf16[4,192,256]{2,1,0:T(8,128)(2,1)} %get-tuple-element.48), calls=%async_computation.5 | async-start | bytes 786432 | tf_op jit(solution)/shard_map/all_to_all | solution.py:384
  166.4 2.5 %collective-permute-start.18 = (bf16[192,256]{1,0:T(8,128)(2,1)}, bf16[192,256]{1,0:T(8,128)(2,1)S(1)}, u32[]{:S(2)}, u32[]{:S(2)}) collective-permute-start(bf16[192,256]{1,0:T(8,128)(2,1)} %copy-done.21), channel_id=1, source_target_pairs={{0,24},{8,0},{16,8},{24,16},{32,56},{40,32},{48,40},{56,48},{64,88... | collective-permute-start | bytes 294920 | tf_op jit(solution)/shard_map/ppermute | solution.py:388
  169.8 1.9 %collective-permute-done.17.refs_1_ = bf16[192,256]{1,0:T(8,128)(2,1)S(1)} collective-permute-done((bf16[192,256]{1,0:T(8,128)(2,1)}, bf16[192,256]{1,0:T(8,128)(2,1)S(1)}, u32[]{:S(2)}, u32[]{:S(2)}) %collective-permute-start.17) | collective-permute-done | bytes 98336 | tf_op jit(solution)/shard_map/ppermute | solution.py:388
  172.4 2.9 %collective-permute-done.19.refs_3_ = bf16[192,256]{1,0:T(8,128)(2,1)S(1)} collective-permute-done((bf16[192,256]{1,0:T(8,128)(2,1)}, bf16[192,256]{1,0:T(8,128)(2,1)S(1)}, u32[]{:S(2)}, u32[]{:S(2)}) %collective-permute-start.19) | collective-permute-done | bytes 98336 | tf_op jit(solution)/shard_map/ppermute | solution.py:388
  175.8 16.3 %all_to_all.39.got_ref = bf16[32,36,128]{2,1,0:T(8,128)(2,1)S(1)} all-to-all(bf16[32,36,128]{2,1,0:T(8,128)(2,1)S(1)} %spread_rows.1), channel_id=1, replica_groups=mesh['seq'=32,'vocab'=8] {'seq'}, dimensions={0} | all-to-all | bytes 589824 | tf_op jit(solution)/shard_map/all_to_all | solution.py:384
  (115 shorter events, 30.5 us)
Async XLA Ops:
  4.9 25.3 %all-to-all-start = ((bf16[32,36,128]{2,1,0:T(8,128)(2,1)}), bf16[32,36,128]{2,1,0:T(8,128)(2,1)S(1)}, u32[]{:S(2)}, u32[]{:S(2)}) async-start(bf16[32,36,128]{2,1,0:T(8,128)(2,1)} %sort_rows.1), calls=%async_computation | async-start | bytes 655360 | tf_op jit(solution)/shard_map/all_to_all | solution.py:384
  28.3 16.3 %copy-start.8 = (f32[288,192]{1,0:T(8,128)}, f32[288,192]{1,0:T(8,128)S(1)}, u32[]{:S(2)}) copy-start(f32[288,192]{1,0:T(8,128)S(1)} %fusion.spread_ref.refs_5_) | copy-start | bytes 663556
  31.4 14.5 %all-to-all-start.2 = ((bf16[4,192,256]{2,1,0:T(8,128)(2,1)}), bf16[4,192,256]{2,1,0:T(8,128)(2,1)S(1)}, u32[]{:S(2)}, u32[]{:S(2)}) async-start(bf16[4,192,256]{2,1,0:T(8,128)(2,1)} %get-tuple-element.28), calls=%async_computation.2 | async-start | bytes 786432 | tf_op jit(solution)/shard_map/all_to_all | solution.py:384
  36.3 6.9 %collective-permute-start.2 = (bf16[192,256]{1,0:T(8,128)(2,1)S(1)}, bf16[192,256]{1,0:T(8,128)(2,1)S(1)}, u32[]{:S(2)}, u32[]{:S(2)}) collective-permute-start(bf16[192,256]{1,0:T(8,128)(2,1)S(1)} %get-tuple-element.27.refs_0_), channel_id=1, source_target_pairs={{0,8},{8,16},{16,24},{24,0},{32,40},{40,48},{48,56},{56,32},{64,72... | collective-permute-start | bytes 294920 | tf_op jit(solution)/shard_map/ppermute | solution.py:388
  36.7 6.5 %collective-permute-start.1 = (bf16[192,256]{1,0:T(8,128)(2,1)S(1)}, bf16[192,256]{1,0:T(8,128)(2,1)S(1)}, u32[]{:S(2)}, u32[]{:S(2)}) collective-permute-start(bf16[192,256]{1,0:T(8,128)(2,1)S(1)} %get-tuple-element.27.refs_0_), channel_id=1, source_target_pairs={{0,16},{8,24},{16,0},{24,8},{32,48},{40,56},{48,32},{56,40},{64,80... | collective-permute-start | bytes 294920 | tf_op jit(solution)/shard_map/ppermute | solution.py:388
  39.3 4.7 %collective-permute-start = (bf16[192,256]{1,0:T(8,128)(2,1)S(1)}, bf16[192,256]{1,0:T(8,128)(2,1)S(1)}, u32[]{:S(2)}, u32[]{:S(2)}) collective-permute-start(bf16[192,256]{1,0:T(8,128)(2,1)S(1)} %get-tuple-element.27.refs_0_), channel_id=1, source_target_pairs={{0,24},{8,0},{16,8},{24,16},{32,56},{40,32},{48,40},{56,48},{64,88... | collective-permute-start | bytes 294920 | tf_op jit(solution)/shard_map/ppermute | solution.py:388
  45.8 24.5 %all-to-all-start.1 = ((bf16[4,768,256]{2,1,0:T(8,128)(2,1)}), bf16[4,768,256]{2,1,0:T(8,128)(2,1)}, u32[]{:S(2)}, u32[]{:S(2)}) async-start(bf16[4,768,256]{2,1,0:T(8,128)(2,1)} %bitcast.34), calls=%async_computation.1 | async-start | bytes 3145728 | tf_op jit(solution)/shard_map/all_to_all | solution.py:384
  50.6 13.2 %collective-permute-start.6 = (bf16[4,192,256]{2,1,0:T(8,128)(2,1)S(1)}, bf16[4,192,256]{2,1,0:T(8,128)(2,1)S(1)}, u32[]{:S(2)}, u32[]{:S(2)}) collective-permute-start(bf16[4,192,256]{2,1,0:T(8,128)(2,1)S(1)} %all-to-all-done.2.refs_0_), channel_id=1, source_target_pairs={{0,8},{8,16},{16,24},{24,0},{32,40},{40,48},{48,56},{56,32},{64,72... | collective-permute-start | bytes 1179656 | tf_op jit(solution)/shard_map/ppermute | solution.py:388
  51.9 16.5 %collective-permute-start.5 = (bf16[4,192,256]{2,1,0:T(8,128)(2,1)S(1)}, bf16[4,192,256]{2,1,0:T(8,128)(2,1)S(1)}, u32[]{:S(2)}, u32[]{:S(2)}) collective-permute-start(bf16[4,192,256]{2,1,0:T(8,128)(2,1)S(1)} %all-to-all-done.2.refs_0_), channel_id=1, source_target_pairs={{0,16},{8,24},{16,0},{24,8},{32,48},{40,56},{48,32},{56,40},{64,80... | collective-permute-start | bytes 1179656 | tf_op jit(solution)/shard_map/ppermute | solution.py:388
  54.8 13.7 %collective-permute-start.4 = (bf16[4,192,256]{2,1,0:T(8,128)(2,1)S(1)}, bf16[4,192,256]{2,1,0:T(8,128)(2,1)S(1)}, u32[]{:S(2)}, u32[]{:S(2)}) collective-permute-start(bf16[4,192,256]{2,1,0:T(8,128)(2,1)S(1)} %all-to-all-done.2.refs_0_), channel_id=1, source_target_pairs={{0,24},{8,0},{16,8},{24,16},{32,56},{40,32},{48,40},{56,48},{64,88... | collective-permute-start | bytes 1179656 | tf_op jit(solution)/shard_map/ppermute | solution.py:388
  70.3 9.5 %collective-permute-start.7 = (bf16[4,768,256]{2,1,0:T(8,128)(2,1)}, bf16[4,768,256]{2,1,0:T(8,128)(2,1)}, u32[]{:S(2)}, u32[]{:S(2)}) collective-permute-start(bf16[4,768,256]{2,1,0:T(8,128)(2,1)} %bitcast.15.rows_ref.refs_1_), channel_id=1, source_target_pairs={{0,1},{1,0},{2,3},{3,2},{4,5},{5,4},{6,7},{7,6},{8,9},{9,8},{10,11... | collective-permute-start | bytes 4718600 | tf_op jit(solution)/shard_map/ppermute | solution.py:476
  70.3 9.5 %collective-permute-start.3 = (bf16[4,768,256]{2,1,0:T(8,128)(2,1)}, bf16[4,768,256]{2,1,0:T(8,128)(2,1)}, u32[]{:S(2)}, u32[]{:S(2)}) collective-permute-start(bf16[4,768,256]{2,1,0:T(8,128)(2,1)} %all-to-all-done.1.rows_ref.refs_0_), channel_id=1, source_target_pairs={{0,1},{1,0},{2,3},{3,2},{4,5},{5,4},{6,7},{7,6},{8,9},{9,8},{10,11... | collective-permute-start | bytes 4718600 | tf_op jit(solution)/shard_map/ppermute | solution.py:478
  70.8 46.9 %copy-start.14 = (s32[4]{0:T(128)}, s32[4]{0:T(128)S(1)}, u32[]{:S(2)}) copy-start(s32[4]{0:T(128)S(1)} %add_subtract_fusion.block_ref) | copy-start | bytes 52
  84.9 30.4 %copy-start.4 = (f32[768,64]{0,1:T(8,128)S(1)}, f32[768,64]{0,1:T(8,128)}, u32[]{:S(2)}) copy-start(f32[768,64]{0,1:T(8,128)} %copy-done.3) | copy-start | bytes 589828
  84.9 1.3 collective-permute-start.8
  86.2 4.8 %collective-permute-start.11 = (f32[1,2304]{1,0:T(1,128)S(1)}, f32[1,2304]{1,0:T(1,128)S(1)}, u32[]{:S(2)}, u32[]{:S(2)}) collective-permute-start(f32[1,2304]{1,0:T(1,128)S(1)} %pad_maximum_fusion), channel_id=1, source_target_pairs={{0,2},{1,3},{2,4},{3,5},{4,6},{5,7},{6,0},{7,1},{8,10},{9,11},{10,... | collective-permute-start | bytes 27656 | tf_op jit(solution)/shard_map/ppermute | solution.py:392
  87.8 5.2 %collective-permute-start.10 = (f32[1,2304]{1,0:T(1,128)S(1)}, f32[1,2304]{1,0:T(1,128)S(1)}, u32[]{:S(2)}, u32[]{:S(2)}) collective-permute-start(f32[1,2304]{1,0:T(1,128)S(1)} %pad_maximum_fusion), channel_id=1, source_target_pairs={{0,4},{1,5},{2,6},{3,7},{4,0},{5,1},{6,2},{7,3},{8,12},{9,13},{10,... | collective-permute-start | bytes 27656 | tf_op jit(solution)/shard_map/ppermute | solution.py:392
  88.8 4.2 %collective-permute-start.9 = (f32[1,2304]{1,0:T(1,128)S(1)}, f32[1,2304]{1,0:T(1,128)S(1)}, u32[]{:S(2)}, u32[]{:S(2)}) collective-permute-start(f32[1,2304]{1,0:T(1,128)S(1)} %pad_maximum_fusion), channel_id=1, source_target_pairs={{0,6},{1,7},{2,0},{3,1},{4,2},{5,3},{6,4},{7,5},{8,14},{9,15},{10,... | collective-permute-start | bytes 27656 | tf_op jit(solution)/shard_map/ppermute | solution.py:392
  117.6 3.7 %collective-permute-start.12 = (bf16[4,768,256]{2,1,0:T(8,128)(2,1)S(1)}, bf16[4,768,256]{2,1,0:T(8,128)(2,1)S(1)}, u32[]{:S(2)}, u32[]{:S(2)}) collective-permute-start(bf16[4,768,256]{2,1,0:T(8,128)(2,1)S(1)} %get-tuple-element.34), channel_id=1, source_target_pairs={{0,1},{1,0},{2,3},{3,2},{4,5},{5,4},{6,7},{7,6},{8,9},{9,8},{10,11... | collective-permute-start | bytes 4718600 | tf_op jit(solution)/shard_map/ppermute | solution.py:487
  120.8 9.4 %collective-permute-start.13 = (bf16[4,768,256]{2,1,0:T(8,128)(2,1)}, bf16[4,768,256]{2,1,0:T(8,128)(2,1)}, u32[]{:S(2)}, u32[]{:S(2)}) collective-permute-start(bf16[4,768,256]{2,1,0:T(8,128)(2,1)} %grad_rest.1), channel_id=1, source_target_pairs={{0,1},{1,0},{2,3},{3,2},{4,5},{5,4},{6,7},{7,6},{8,9},{9,8},{10,11... | collective-permute-start | bytes 4718600 | tf_op jit(solution)/shard_map/ppermute | solution.py:488
  124.5 32.6 %all-to-all-start.4 = ((bf16[4,768,256]{2,1,0:T(8,128)(2,1)}), bf16[4,768,256]{2,1,0:T(8,128)(2,1)S(1)}, u32[]{:S(2)}, u32[]{:S(2)}) async-start(bf16[4,768,256]{2,1,0:T(8,128)(2,1)} %grad_first.1), calls=%async_computation.4 | async-start | bytes 3145728 | tf_op jit(solution)/shard_map/all_to_all | solution.py:384
  136.1 20.4 %collective-permute-start.14 = (bf16[4,192,256]{2,1,0:T(8,128)(2,1)S(1)}, bf16[4,192,256]{2,1,0:T(8,128)(2,1)S(1)}, u32[]{:S(2)}, u32[]{:S(2)}) collective-permute-start(bf16[4,192,256]{2,1,0:T(8,128)(2,1)S(1)} %get-tuple-element.37), channel_id=1, source_target_pairs={{0,8},{8,16},{16,24},{24,0},{32,40},{40,48},{48,56},{56,32},{64,72... | collective-permute-start | bytes 1179656 | tf_op jit(solution)/shard_map/ppermute | solution.py:388
  136.2 20.3 %collective-permute-start.16 = (bf16[4,192,256]{2,1,0:T(8,128)(2,1)S(1)}, bf16[4,192,256]{2,1,0:T(8,128)(2,1)S(1)}, u32[]{:S(2)}, u32[]{:S(2)}) collective-permute-start(bf16[4,192,256]{2,1,0:T(8,128)(2,1)S(1)} %get-tuple-element.38), channel_id=1, source_target_pairs={{0,16},{8,24},{16,0},{24,8},{32,48},{40,56},{48,32},{56,40},{64,80... | collective-permute-start | bytes 1179656 | tf_op jit(solution)/shard_map/ppermute | solution.py:388
  138.7 18.4 %collective-permute-start.15 = (bf16[4,192,256]{2,1,0:T(8,128)(2,1)S(1)}, bf16[4,192,256]{2,1,0:T(8,128)(2,1)S(1)}, u32[]{:S(2)}, u32[]{:S(2)}) collective-permute-start(bf16[4,192,256]{2,1,0:T(8,128)(2,1)S(1)} %get-tuple-element.39), channel_id=1, source_target_pairs={{0,24},{8,0},{16,8},{24,16},{32,56},{40,32},{48,40},{56,48},{64,88... | collective-permute-start | bytes 1179656 | tf_op jit(solution)/shard_map/ppermute | solution.py:388
  150.9 24.3 %copy-start.9 = (f32[288,192]{1,0:T(8,128)S(1)}, f32[288,192]{1,0:T(8,128)}, u32[]{:S(2)}) copy-start(f32[288,192]{1,0:T(8,128)} %copy-done.8) | copy-start | bytes 663556
  160.8 31.4 %copy-start.11 = (bf16[36,4096]{1,0:T(8,128)(2,1)S(1)}, bf16[36,4096]{1,0:T(8,128)(2,1)}, u32[]{:S(2)}) copy-start(bf16[36,4096]{1,0:T(8,128)(2,1)} %rows_ref.3) | copy-start | bytes 884740
  160.8 31.4 %copy-start.13 = (f32[4096]{0:T(1024)S(1)}, f32[4096]{0:T(1024)}, u32[]{:S(2)}) copy-start(f32[4096]{0:T(1024)} %param.8) | copy-start | bytes 49156
  160.8 31.4 %copy-start.17 = (f32[1,768]{1,0:T(1,128)S(1)}, f32[1,768]{1,0:T(1,128)}, u32[]{:S(2)}) copy-start(f32[1,768]{1,0:T(1,128)} %copy-done.16) | copy-start | bytes 9220
  160.8 14.5 %all-to-all-start.5 = ((bf16[4,192,256]{2,1,0:T(8,128)(2,1)}), bf16[4,192,256]{2,1,0:T(8,128)(2,1)S(1)}, u32[]{:S(2)}, u32[]{:S(2)}) async-start(bf16[4,192,256]{2,1,0:T(8,128)(2,1)} %get-tuple-element.48), calls=%async_computation.5 | async-start | bytes 786432 | tf_op jit(solution)/shard_map/all_to_all | solution.py:384
  165.7 6.0 %collective-permute-start.17 = (bf16[192,256]{1,0:T(8,128)(2,1)}, bf16[192,256]{1,0:T(8,128)(2,1)S(1)}, u32[]{:S(2)}, u32[]{:S(2)}) collective-permute-start(bf16[192,256]{1,0:T(8,128)(2,1)} %copy-done.22), channel_id=1, source_target_pairs={{0,8},{8,16},{16,24},{24,0},{32,40},{40,48},{48,56},{56,32},{64,72... | collective-permute-start | bytes 294920 | tf_op jit(solution)/shard_map/ppermute | solution.py:388
  166.4 6.0 %collective-permute-start.18 = (bf16[192,256]{1,0:T(8,128)(2,1)}, bf16[192,256]{1,0:T(8,128)(2,1)S(1)}, u32[]{:S(2)}, u32[]{:S(2)}) collective-permute-start(bf16[192,256]{1,0:T(8,128)(2,1)} %copy-done.21), channel_id=1, source_target_pairs={{0,24},{8,0},{16,8},{24,16},{32,56},{40,32},{48,40},{56,48},{64,88... | collective-permute-start | bytes 294920 | tf_op jit(solution)/shard_map/ppermute | solution.py:388
  168.9 6.3 %collective-permute-start.19 = (bf16[192,256]{1,0:T(8,128)(2,1)}, bf16[192,256]{1,0:T(8,128)(2,1)S(1)}, u32[]{:S(2)}, u32[]{:S(2)}) collective-permute-start(bf16[192,256]{1,0:T(8,128)(2,1)} %copy-done.20), channel_id=1, source_target_pairs={{0,16},{8,24},{16,0},{24,8},{32,48},{40,56},{48,32},{56,40},{64,80... | collective-permute-start | bytes 294920 | tf_op jit(solution)/shard_map/ppermute | solution.py:388
  (20 other events, 94.7 us)
